TPU v7x, 32 devices: a whole 2x2x4 slice. The times are simulated.
32 devices in a mesh: dp: 8 (over z, y), mp: 4 (over x, core).
Axes of the slice: x: 2, y: 2, z: 4, core: 2. Of those that a mesh axis runs over, the one named last changes fastest.
Arguments:
- hidden_act: bfloat16 [2048, 14336], P('dp', 'mp'), may hold values from -6 to 6
- readout: bfloat16 [2048, 2560], P('dp'), may hold values from -6 to 6
- log_gap: float32 [256, 8], P('dp'), may hold values from -0.6 to 0.6
- advantage: float32 [256], P('dp'), may hold values from -6 to 6
- version: int32 [256], P('dp'), may hold values from 0 to 3
- lengths: int32 [8, 32], P('dp'), may hold values from 1 to 8, 224 in all within a row
- routes: int32 [256, 1], P('dp'), may hold values from 0 to 7; in each aligned block of 32 rows (0 to 31, 32 to 63, ...) at most 8 rows name the same one
- weight: bfloat16 [14336, 2560], P(('mp', 'dp')), may hold values from -0.046875 to 0.046875
Outputs:
- log_ratio: float32 [512, 8], P('dp')
- weight_grad: float32 [14336, 2560], P(('mp', 'dp'))
Inputs may be any that keep to these rules, and one draw needn't show every extreme that they name: `routes`: among the 32 responses of one generator device at most 8 name the same learner shard, and some shard receives exactly 8; every learner shard receives at least one response. The lengths of one generator device's responses sum to 224, and one of them is 8.
All inputs are finite; a program needn't handle non-finite values.
Results may differ from a plain program's by a relative error of at most 0.0029.
Values may be sent and summed in bfloat16 or wider, within the bound.
No kernel may reach another device: no remote copies, remote signals or barrier semaphores. Data moves between devices by JAX's collectives and lax.ppermute only.
A program may use at most 128 MiB of HBM per device.

v0:
```python
import math

import jax
import jax.numpy as jnp
from jax import lax
from jax.sharding import PartitionSpec as P

NVER = 4


def token_shift(rows_act, rows_read, weight):
    width = rows_read.shape[1]
    layer_out = jnp.dot(
        rows_act,
        lax.all_gather(weight, "dp", axis=0, tiled=True),
        preferred_element_type=jnp.float32,
    )
    partial_dot = jnp.sum(layer_out * rows_read.astype(jnp.float32), axis=1)
    return lax.psum(partial_dot, "mp") * (0.15 / math.sqrt(width))


def surrogate_coef(logit_all, live, stale, adv, count_each):
    ratio = jnp.exp(logit_all)
    squash = jnp.tanh((ratio - 1.0) / 0.2)
    clipped = 1.0 + 0.2 * squash
    adv_col = adv[:, None]
    plain = ratio * adv_col <= clipped * adv_col
    slope = jnp.where(plain, 1.0, 1.0 - squash * squash)
    return jnp.where(
        live, -512.0 * stale[:, None] * adv_col * ratio * slope / count_each[:, None], 0.0
    )


def weight_terms(rows_act, out_grad):
    full_term = lax.dot_general(
        rows_act, out_grad, (((0,), (0,)), ((), ())), preferred_element_type=jnp.float32
    )
    return lax.psum_scatter(full_term, "dp", scatter_dimension=0, tiled=True)


def body(hidden_act, readout, log_gap, advantage, version, lengths, routes, weight):
    shards = lax.axis_size("dp")
    respond, seglen = log_gap.shape
    width = readout.shape[1]
    slots = 2 * respond // shards
    total_slots = shards * slots
    dest = routes[:, 0]
    onehot = (dest[:, None] == jnp.arange(shards, dtype=jnp.int32)[None, :]).astype(jnp.int32)
    rank = jnp.sum((jnp.cumsum(onehot, axis=0) - onehot) * onehot, axis=1)
    slot_of = dest * slots + rank
    select = (jnp.arange(total_slots, dtype=jnp.int32)[:, None] == slot_of[None, :]).astype(
        jnp.float32
    )
    lens = lengths[0]
    lens_float = lens.astype(jnp.float32)
    stale = jnp.power(jnp.float32(0.7), (NVER - 1 - version).astype(jnp.float32))
    positions = jnp.arange(seglen, dtype=jnp.int32)
    scale_out = 0.15 / math.sqrt(width)
    shift = token_shift(hidden_act, readout, weight)
    logit_all = log_gap + shift.reshape(respond, seglen)
    live = positions[None, :] < lens[:, None]
    onehot_float = onehot.astype(jnp.float32)
    histogram = jnp.sum(onehot_float * lens_float[:, None], axis=0)
    shard_count = lax.psum(histogram, "dp")
    count_each = jnp.sum(onehot_float * shard_count[None, :], axis=1)
    local_ratio = jnp.where(live, logit_all, 0.0)
    send_ratio = jnp.dot(select, local_ratio, precision=lax.Precision.HIGHEST)
    log_ratio = lax.all_to_all(send_ratio, "dp", split_axis=0, concat_axis=0, tiled=True)
    coef = surrogate_coef(logit_all, live, stale, advantage, count_each)
    out_grad = (coef.reshape(-1)[:, None] * scale_out * readout.astype(jnp.float32)).astype(
        jnp.bfloat16
    )
    weight_grad = weight_terms(hidden_act, out_grad)
    return (log_ratio, weight_grad)


def solution(mesh):
    placed = (
        P("dp", "mp"),
        P("dp", None),
        P("dp", None),
        P("dp"),
        P("dp"),
        P("dp", None),
        P("dp", None),
        P(("mp", "dp"), None),
    )
    return jax.shard_map(
        body,
        mesh=mesh,
        in_specs=placed,
        out_specs=(P("dp", None), P(("mp", "dp"), None)),
        check_vma=False,
    )
```

profile of v0, /device:TPU:0, one launch (start us, length us, event | category | flops | bytes accessed | tf_op | source)
XLA Modules:
  0.0 1029.6 jit_solution(15450315464226959039)
XLA Ops:
  7.2 0.0 copy-start
  7.2 0.0 all-gather.2.cloned.1.call-start
  7.2 0.7 all-gather.2.cloned.1.call-update
  7.9 0.0 reduce-scatter.4.cloned.1.call-start
  8.0 0.7 bitcast_convert_fusion
  8.6 0.7 multiply_reduce_fusion.1
  9.4 43.8 %psum.15 = f32[8]{0:T(128)S(1)} all-reduce(f32[8]{0:T(128)S(1)} %multiply_reduce_fusion.1), channel_id=1, replica_groups=mesh['dp'=8,'mp'=4] {'dp'}, use_global_device_ids=true, to_apply=%region_5.6 | all-reduce | flops 8 | bytes 64 | tf_op jit(solution)/shard_map/psum | solution.py:64
  53.2 0.8 copy.16
  54.0 0.8 multiply_reduce_fusion
  54.8 0.7 multiply_multiply_fusion
  55.5 0.0 copy-start.4
  55.5 0.0 copy-start.5
  55.5 0.0 copy-start.2
  55.5 309.8 %all-gather.2.cloned.1.call-done = bf16[3584,2560]{1,0:T(8,128)(2,1)} async-done(((bf16[448,2560]{1,0:T(8,128)(2,1)}), bf16[3584,2560]{1,0:T(8,128)(2,1)}) %all-gather.2.cloned.1.call-update) | async-done | bytes 18350096 | tf_op jit(solution)/shard_map/all_gather | solution.py:15
  365.3 0.0 copy-done
  365.3 9.5 fusion.1
  374.8 6.9 psum.14
  381.7 0.1 reshape.38
  381.8 0.0 copy-done.4
  381.8 0.0 copy-done.5
  381.8 0.1 select_multiply_fusion
  381.9 0.1 mul.125
  382.0 0.0 copy-done.2
  382.0 14.4 %convolution_bitcast_fusion = f32[3584,2560]{0,1:T(8,128)} fusion(bf16[256,3584]{1,0:T(8,128)(2,1)S(1)} %copy-done, bf16[256,2560]{1,0:T(8,128)(2,1)S(1)} %copy-done.2, f32[256]{0:T(256)S(1)} %mul.125), kind=kOutput, calls=%fused_computation | convolution fusion | flops 4699586560 | bytes 39846912 | tf_op jit(solution)/shard_map/dot_general | solution.py:35
  396.5 37.0 %copy.20 = f32[3584,2560]{1,0:T(8,128)} copy(f32[3584,2560]{0,1:T(8,128)} %convolution_bitcast_fusion) | data formatting | bytes 73400320
  433.4 0.0 copy-start.3
  433.4 0.0 reduce-scatter.4.cloned.1.call-update
  433.4 0.6 copy-done.3
  434.1 0.0 copy-start.1
  434.1 0.1 fusion.9
  434.2 0.1 reduce_window_sum.11
  434.2 0.2 fusion.6
  434.4 0.2 fusion.4
  434.6 0.1 all_to_all.8
  434.7 0.1 copy.17
  434.8 11.3 %all_to_all.12 = f32[8,8,8]{1,2,0:T(8,128)S(1)} all-to-all(f32[8,8,8]{1,2,0:T(8,128)S(1)} %copy.17), channel_id=1, replica_groups=mesh['dp'=8,'mp'=4] {'dp'}, dimensions={0} | all-to-all | bytes 4096 | tf_op jit(solution)/shard_map/all_to_all | solution.py:68
  446.1 0.7 all_to_all.10
  446.8 576.0 %reduce-scatter.4.cloned.1.call-done = f32[448,2560]{1,0:T(8,128)} async-done(((f32[3584,2560]{1,0:T(8,128)}), f32[448,2560]{1,0:T(8,128)}) %reduce-scatter.4.cloned.1.call-update) | async-done | bytes 4587536
  1022.8 0.0 copy-done.1
  (3 shorter events, 0.0 us)
Async XLA Ops:
  7.2 358.1 %copy-start = (bf16[256,3584]{1,0:T(8,128)(2,1)S(1)}, bf16[256,3584]{1,0:T(8,128)(2,1)}, u32[]{:S(2)}) copy-start(bf16[256,3584]{1,0:T(8,128)(2,1)} %param.8) | copy-start | bytes 5505028
  7.2 358.1 %all-gather.2.cloned.1.call-start = ((), (), s32[]{:S(2)}) async-start(), calls=%async_computation.2 | async-start | bytes 20643840 | tf_op jit(solution)/shard_map/all_gather | solution.py:15
  7.9 1014.9 %reduce-scatter.4.cloned.1.call-start = ((), (), s32[]{:S(2)}) async-start(), calls=%async_computation.3 | async-start | bytes 41287680
  55.5 326.3 %copy-start.4 = (f32[32]{0:T(128)S(1)}, f32[32]{0:T(128)}, u32[]{:S(2)}) copy-start(f32[32]{0:T(128)} %param.11) | copy-start | bytes 388
  55.5 326.3 %copy-start.5 = (s32[1,32]{1,0:T(1,128)S(1)}, s32[1,32]{1,0:T(1,128)}, u32[]{:S(2)}) copy-start(s32[1,32]{1,0:T(1,128)} %param.13) | copy-start | bytes 388
  55.5 326.5 %copy-start.2 = (bf16[256,2560]{1,0:T(8,128)(2,1)S(1)}, bf16[256,2560]{1,0:T(8,128)(2,1)}, u32[]{:S(2)}) copy-start(bf16[256,2560]{1,0:T(8,128)(2,1)} %param.9) | copy-start | bytes 3932164
  433.4 0.7 copy-start.3
  434.1 588.7 %copy-start.1 = (bf16[256,3584]{1,0:T(8,128)(2,1)S(1)}, bf16[256,3584]{1,0:T(8,128)(2,1)}, u32[]{:S(2)}) copy-start(bf16[256,3584]{1,0:T(8,128)(2,1)} %param.8) | copy-start | bytes 5505028
Sparse Core Ops, SparseCore 0:
  9.5 355.7 all-gather.1
  433.6 589.1 reduce-scatter.3
where the time goes:
time: 1030 us
  waiting for transfers between devices  886 us (86%)
  blocking collectives  62.1 us (6%)
  local copies, waits for them, and re-layouts  39.4 us (4%)
  matrix products  24.2 us (2%)
  between operations  14.1 us (1%)
    unnamed x3, waiting for transfers between devices  577 us
    all_gather x1, waiting for transfers between devices, token_shift(): lax.all_gather(weight, 'dp', axis=0, tiled=True)  310 us
    psum x1, blocking collectives, body(): shard_count = lax.psum(histogram, 'dp')  43.8 us
    unnamed x14, local copies, waits for them, and re-layouts  38.4 us
  transfers between devices with their start and end apart: 2, of which 2 were waited for; matrix products, arithmetic and copies ran while one was open for 0% of the time, Pallas kernels for 0%

commit v1 on v0

v1 whole, which is shorter than its diff:
```python
import functools
import math

import jax
import jax.numpy as jnp
import numpy as np
from jax import lax
from jax.experimental import pallas as pl
from jax.experimental.pallas import tpu as pltpu
from jax.sharding import PartitionSpec as P

NVER = 4
SCALE = 0.15
EXACT = lax.Precision.HIGHEST
VMEM = pl.BlockSpec(memory_space=pltpu.VMEM)
SMEM = pl.BlockSpec(memory_space=pltpu.SMEM)
ANY = pl.BlockSpec(memory_space=pl.ANY)
GAP, ADV, STALE, DEST, RANK, POS = range(6)


def iota(shape, axis):
    return lax.broadcasted_iota(jnp.int32, shape, axis)


def rows_of(*rows):
    n = rows[0].shape[1]
    row = iota((8, n), 0)
    table = jnp.zeros((8, n), jnp.float32)
    for i, values in enumerate(rows):
        table = jnp.where(row == i, values, table)
    return table


def pack_readout(live_rows, seglen, place, lens, routes, gap, adv, version, read, table, sel, own, first, both):
    respond, tokens = gap.shape[0], gap.shape[0] * seglen
    mp = place[1]
    expand = (iota((respond, tokens), 0) == lax.div(iota((respond, tokens), 1), seglen)).astype(jnp.float32)
    spread = (iota((seglen, tokens), 0) == lax.rem(iota((seglen, tokens), 1), seglen)).astype(jnp.float32)
    eye = iota((respond, respond), 0) == iota((respond, respond), 1)
    dest_col = routes[...].astype(jnp.float32)
    dest_row = jnp.sum(jnp.where(eye, dest_col, 0.0), axis=0, keepdims=True)
    earlier = (dest_col == dest_row) & (iota((respond, respond), 0) < iota((respond, respond), 1))
    rank_row = jnp.sum(jnp.where(earlier, 1.0, 0.0), axis=0, keepdims=True)
    age = NVER - 1 - version[...]
    stale = jnp.ones(age.shape, jnp.float32)
    for years in range(1, NVER):
        stale = jnp.where(age == years, jnp.float32(np.float32(0.7) ** years), stale)
    by_token = jnp.dot(
        rows_of(adv[...], stale, dest_row, rank_row, lens[...].astype(jnp.float32)),
        expand, precision=EXACT, preferred_element_type=jnp.float32,
    )
    gap_wide = jnp.dot(gap[...], spread, precision=EXACT, preferred_element_type=jnp.float32)
    gap_row = jnp.sum(gap_wide * expand, axis=0, keepdims=True)
    pos_row = lax.rem(iota((1, tokens), 1), seglen).astype(jnp.float32)
    live = pos_row < by_token[4:5, :]
    before = (iota((tokens, tokens), 0) < iota((tokens, tokens), 1)).astype(jnp.bfloat16)
    live_wide = jnp.broadcast_to(live.astype(jnp.float32), (16, tokens)).astype(jnp.bfloat16)
    order = jnp.dot(live_wide, before, preferred_element_type=jnp.float32)[0:1, :]
    chosen = live & (order == iota((live_rows, tokens), 0).astype(jnp.float32))
    chosen_f32 = chosen.astype(jnp.float32)
    select = chosen_f32.astype(jnp.bfloat16)
    sel[...] = select
    table[...] = lax.dot_general(
        rows_of(gap_row, by_token[0:1, :], by_token[1:2, :], by_token[2:3, :], by_token[3:4, :], pos_row),
        chosen_f32, (((1,), (1,)), ((), ())), precision=EXACT, preferred_element_type=jnp.float32,
    )
    wide = read.shape[1] // 4
    for quarter in range(4):
        part = jnp.dot(
            select, read[:, quarter * wide:(quarter + 1) * wide], preferred_element_type=jnp.float32
        ).astype(jnp.bfloat16)
        own[mp ^ quarter] = part

        @pl.when(mp == quarter)
        def _():
            first[...] = part
            both[:live_rows] = part

        @pl.when((mp ^ 2) == quarter)
        def _():
            both[live_rows:] = part


def packed_rows(units, live_rows):
    return units * live_rows // 128


def pack_hidden(place, hidden, sel, *rest):
    outs, held = rest[:-1], rest[-1]
    dp = place[0]
    live_rows = sel.shape[0]
    units = hidden.shape[1] // len(outs)
    tail = live_rows - 128
    fold = 128 // math.gcd(tail, 128)
    short = units // fold
    pieces = tail * fold // 128
    rows = packed_rows(units, live_rows)
    for block in range(0, len(outs), 2):
        turned = lax.dot_general(
            hidden[:, block * units:(block + 2) * units], sel[...], (((0,), (1,)), ((), ())),
            preferred_element_type=jnp.float32,
        )
        for i in range(2):
            part = turned[i * units:(i + 1) * units]
            at = (block + i) * rows
            held[at:at + units] = part[:, :128].astype(jnp.bfloat16)
            wide = jnp.concatenate([part[j * short:(j + 1) * short, 128:] for j in range(fold)], axis=1)
            for j in range(pieces):
                start = at + units + j * short
                held[start:start + short] = wide[:, j * 128:(j + 1) * 128].astype(jnp.bfloat16)
    for k, out in enumerate(outs):
        out[...] = held[pl.ds(pl.multiple_of((dp ^ k) * rows, 16), rows)]


def unpack_hidden(packed, units, live_rows):
    tail = live_rows - 128
    fold = 128 // math.gcd(tail, 128)
    short = units // fold
    pieces = tail * fold // 128
    wide = jnp.concatenate(
        [packed[units + j * short:units + (j + 1) * short].astype(jnp.float32) for j in range(pieces)], axis=1
    )
    folded = jnp.concatenate([wide[:, j * tail:(j + 1) * tail] for j in range(fold)], axis=0)
    return packed[:units].astype(jnp.float32), folded


def fetch(pieces, refs, held, sems):
    copies = {}
    live_rows = held.shape[2]
    for (k, e), (ref, at) in pieces.items():
        source = refs[ref].at[at] if ref == 0 else refs[ref].at[pl.ds(at * live_rows, live_rows)]
        copy = pltpu.make_async_copy(source, held.at[e, k], sems.at[k, e])
        copy.start()
        copies[k, e] = copy
    return copies


def shift_kernel(pieces, n_refs, slots, place, weight, *rest):
    n = len(slots)
    hidden, refs, out = rest[:n], rest[n:n + n_refs], rest[n + n_refs]
    held, sems = rest[n + n_refs + 1:]
    mp = place[1]
    wide, live_rows = held.shape[3], held.shape[2]
    units = weight.shape[0]
    copies = fetch(pieces, refs, held, sems)
    row = iota((8, live_rows), 0)
    total = jnp.zeros((8, live_rows), jnp.float32)
    for i in range(n):
        product = jnp.zeros((units, live_rows), jnp.float32)
        for e in range(4):
            copies[i, e].wait()
            product += lax.dot_general(
                weight[:, pl.ds(pl.multiple_of((mp ^ e) * wide, 128), wide)], held[e, i],
                (((1,), (1,)), ((), ())), preferred_element_type=jnp.float32,
            )
        head, tail = unpack_hidden(hidden[i], units, live_rows)
        sums = jnp.concatenate(
            [jnp.sum(product[:, :128] * head, axis=0, keepdims=True),
             jnp.sum(product[:, 128:] * tail, axis=0, keepdims=True)], axis=1,
        )
        total = jnp.where(row == i, sums, total)
    out[...] = total


def by_slot(table, which, slots):
    live_rows = table.shape[1]
    row = iota((slots, live_rows), 0)
    out = jnp.zeros((slots, live_rows), jnp.float32)
    for k in range(slots):
        out = jnp.where(row == k, table[k * 8 + which:k * 8 + which + 1, :], out)
    return out


def swap_rows(values, m):
    n = values.shape[0]
    row = iota(values.shape, 0)
    out = jnp.zeros_like(values)
    for k in range(n):
        out = jnp.where(row == k, values[k ^ m:(k ^ m) + 1, :], out)
    return out


def grad_kernel(pieces, n_refs, shards, offsets, slots_each, seglen, place, *rest):
    hidden, rest = rest[:shards], rest[shards:]
    refs, rest = rest[:n_refs], rest[n_refs:]
    sums, rest = rest[:len(offsets)], rest[len(offsets):]
    table, ratio_out, grad_out, held, turned, scaled, result, sems, out_sems = rest
    dp, mp = place[0], place[1]
    wide, live_rows = held.shape[3], held.shape[2]
    units = turned.shape[0]
    copies = fetch(pieces, refs, held, sems)
    scale = SCALE / math.sqrt(4 * wide)
    for k in range(shards):
        head, tail = unpack_hidden(hidden[k], units, live_rows)
        turned[:, k * live_rows:(k + 1) * live_rows] = jnp.concatenate([head, tail], axis=1).astype(jnp.bfloat16)

    total = jnp.zeros((shards, live_rows), jnp.float32)
    for ref, m in zip(sums, offsets):
        total = total + swap_rows(ref[...], m)
    logit = by_slot(table, GAP, shards) + total * scale
    adv, dest = by_slot(table, ADV, shards), by_slot(table, DEST, shards)
    counts = jnp.zeros((shards, live_rows), jnp.float32)
    for shard in range(shards):
        here = dest == float(shard)
        tally = jnp.sum(jnp.sum(jnp.where(here, 1.0, 0.0), axis=1, keepdims=True), axis=0, keepdims=True)
        counts = jnp.where(here, tally, counts)
    ratio = jnp.exp(logit)
    squash = jnp.tanh((ratio - 1.0) / 0.2)
    clipped = 1.0 + 0.2 * squash
    slope = jnp.where(ratio * adv <= clipped * adv, 1.0, 1.0 - squash * squash)
    coef = -512.0 * by_slot(table, STALE, shards) * adv * ratio * slope / counts * scale

    mine = jnp.where(dest == dp.astype(jnp.float32), logit, 0.0)
    rank, pos = by_slot(table, RANK, shards), by_slot(table, POS, shards)
    lane = iota((seglen, live_rows), 0).astype(jnp.float32)
    slot = iota((slots_each, live_rows), 0).astype(jnp.float32)
    to_me = dest == dp.astype(jnp.float32)
    for k in range(shards):
        left = jnp.where((slot == rank[k:k + 1]) & to_me[k:k + 1], mine[k:k + 1], 0.0)
        right = jnp.where(lane == pos[k:k + 1], 1.0, 0.0)
        ratio_out[pl.ds(pl.multiple_of((dp ^ k) * slots_each, 8), slots_each)] = lax.dot_general(
            left, right, (((1,), (1,)), ((), ())), precision=EXACT, preferred_element_type=jnp.float32
        )

    eye = iota((live_rows, live_rows), 0) == iota((live_rows, live_rows), 1)
    columns = [jnp.sum(jnp.where(eye, coef[k:k + 1], 0.0), axis=1, keepdims=True) for k in range(shards)]
    writes = []
    for e in range(4):
        for k in range(shards):
            copies[k, e].wait()
            scaled[k * live_rows:(k + 1) * live_rows] = (columns[k] * held[e, k].astype(jnp.float32)).astype(jnp.bfloat16)
        result[e] = jnp.dot(turned[...], scaled[...], preferred_element_type=jnp.float32)
        write = pltpu.make_async_copy(
            result.at[e], grad_out.at[:, pl.ds(pl.multiple_of((mp ^ e) * wide, 128), wide)], out_sems.at[e]
        )
        write.start()
        writes.append(write)
    for write in writes:
        write.wait()


def cube_body(hidden_act, readout, log_gap, advantage, version, lengths, routes, weight):
    shards, quarters = lax.axis_size("dp"), lax.axis_size("mp")
    respond, seglen = log_gap.shape
    live_rows = 7 * respond * seglen // 8
    width = readout.shape[1]
    wide = width // quarters
    units = weight.shape[0]
    rows = packed_rows(units, live_rows)
    slots_each = 2 * respond // shards
    place = jnp.stack([lax.axis_index("dp"), lax.axis_index("mp")]).astype(jnp.int32)
    bf16, f32 = jnp.bfloat16, jnp.float32
    big = pltpu.CompilerParams(vmem_limit_bytes=56 * 1024 * 1024)

    table, sel, own, first, both = pl.pallas_call(
        functools.partial(pack_readout, live_rows, seglen),
        out_shape=(
            jax.ShapeDtypeStruct((8, live_rows), f32),
            jax.ShapeDtypeStruct((live_rows, respond * seglen), bf16),
            jax.ShapeDtypeStruct((quarters, live_rows, wide), bf16),
            jax.ShapeDtypeStruct((live_rows, wide), bf16),
            jax.ShapeDtypeStruct((2 * live_rows, wide), bf16),
        ),
        in_specs=[SMEM] + [VMEM] * 6,
        out_specs=(VMEM,) * 5,
        compiler_params=big,
        name="pack_readout",
    )(place, lengths, routes, log_gap, advantage.reshape(1, respond), version.reshape(1, respond), readout)
    hidden = pl.pallas_call(
        pack_hidden,
        out_shape=(jax.ShapeDtypeStruct((rows, 128), bf16),) * shards,
        in_specs=[SMEM, VMEM, VMEM],
        out_specs=(VMEM,) * shards,
        scratch_shapes=[pltpu.VMEM((shards * rows, 128), bf16)],
        compiler_params=big,
        name="pack_hidden",
    )(place, hidden_act, sel)

    def over_dp(x, m):
        return lax.ppermute(x, "dp", [(s, s ^ m) for s in range(shards)])

    def over_mp(x, m):
        return lax.ppermute(x, "mp", [(s, s ^ m) for s in range(quarters)])

    def over_both(x, m, h):
        pairs = [(s * quarters + t, (s ^ m) * quarters + (t ^ h)) for s in range(shards) for t in range(quarters)]
        return lax.ppermute(x, ("dp", "mp"), pairs)

    def after(x, *others):
        return lax.optimization_barrier((x, *others))[0]

    near = over_dp(first, 2)
    far = over_dp(first, 6)
    beside = over_dp(both, 1)
    arrived = {0: hidden[0]}
    arrived[4] = over_dp(after(hidden[4], near), 4)
    near_far = jnp.concatenate([near, far], axis=0)
    next_far = over_dp(far, 2)
    x_near_far = over_mp(near_far, 2)
    y_near_far = over_dp(near_far, 1)
    arrived[5] = over_dp(after(hidden[5], x_near_far), 5)
    y_next = over_dp(next_far, 1)
    x_next = over_mp(next_far, 2)
    arrived[1] = over_dp(after(hidden[1], next_far), 1)
    arrived[6] = over_dp(after(hidden[6], y_near_far), 6)
    arrived[3] = over_dp(after(hidden[3], y_near_far), 3)
    arrived[7] = over_dp(after(hidden[7], x_near_far), 7)
    xy_near_far = over_mp(y_near_far, 2)
    xy_next = over_mp(y_next, 2)
    arrived[2] = over_dp(after(hidden[2], x_near_far), 2)
    got = [
        (beside, (1, 1), (0, 2)),
        (near_far, (2, 6), (0, 0)),
        (next_far, (4,), (0,)),
        (y_near_far, (3, 7), (0, 0)),
        (y_next, (5,), (0,)),
        (x_near_far, (2, 6), (2, 2)),
        (x_next, (4,), (2,)),
        (xy_near_far, (3, 7), (2, 2)),
        (xy_next, (5,), (2,)),
    ]
    refs = [own]
    pieces = {(0, e): (0, e) for e in range(quarters)}
    for array, ks, es in got:
        for core in (0, 1):
            refs.append(over_mp(array, 1) if core else array)
            for block, (k, e) in enumerate(zip(ks, es)):
                pieces[k, e ^ core] = (len(refs) - 1, block)

    tables = table
    for m in (1, 2, 4):
        tables = jnp.concatenate([tables, over_dp(tables, m)], axis=0)

    hidden_list = [arrived[k] for k in range(shards)]
    sums = pl.pallas_call(
        functools.partial(shift_kernel, pieces, len(refs), tuple(range(shards))),
        out_shape=jax.ShapeDtypeStruct((8, live_rows), f32),
        in_specs=[SMEM, VMEM] + [VMEM] * shards + [ANY] * len(refs),
        out_specs=VMEM,
        scratch_shapes=[
            pltpu.VMEM((quarters, shards, live_rows, wide), bf16),
            pltpu.SemaphoreType.DMA((shards, quarters)),
        ],
        compiler_params=big,
        name="shift_sums",
    )(place, weight, *hidden_list, *refs)

    sums = sums + over_mp(sums, 1)
    sums = sums + over_mp(sums, 2)
    offsets = tuple(range(shards))
    parts = [sums] + [over_dp(sums, m) for m in offsets[1:]]

    log_ratio, weight_grad = pl.pallas_call(
        functools.partial(grad_kernel, pieces, len(refs), shards, offsets, slots_each, seglen),
        out_shape=(
            jax.ShapeDtypeStruct((shards * slots_each, seglen), f32),
            jax.ShapeDtypeStruct((units, width), f32),
        ),
        in_specs=[SMEM] + [VMEM] * shards + [ANY] * len(refs) + [VMEM] * (len(offsets) + 1),
        out_specs=(VMEM, ANY),
        scratch_shapes=[
            pltpu.VMEM((quarters, shards, live_rows, wide), bf16),
            pltpu.VMEM((units, shards * live_rows), bf16),
            pltpu.VMEM((shards * live_rows, wide), bf16),
            pltpu.VMEM((quarters, units, wide), f32),
            pltpu.SemaphoreType.DMA((shards, quarters)),
            pltpu.SemaphoreType.DMA((quarters,)),
        ],
        compiler_params=big,
        name="weight_grad",
    )(place, *hidden_list, *refs, *parts, tables)
    return (log_ratio, weight_grad)


def general_body(hidden_act, readout, log_gap, advantage, version, lengths, routes, weight):
    shards = lax.axis_size("dp")
    respond, seglen = log_gap.shape
    tokens = respond * seglen
    live_rows = 7 * tokens // 8
    width = readout.shape[1]
    units = weight.shape[0]
    slots = 2 * respond // shards
    scale = SCALE / math.sqrt(width)
    f32 = jnp.float32
    dest = routes[:, 0]
    onehot = (dest[:, None] == jnp.arange(shards, dtype=jnp.int32)[None, :]).astype(jnp.int32)
    rank = jnp.sum((jnp.cumsum(onehot, axis=0) - onehot) * onehot, axis=1)
    lens = lengths[0]
    live = (jnp.arange(seglen, dtype=jnp.int32)[None, :] < lens[:, None]).reshape(-1)
    order = jnp.cumsum(live.astype(jnp.int32)) - 1
    select = live[None, :] & (order[None, :] == jnp.arange(live_rows, dtype=jnp.int32)[:, None])
    hidden = jnp.dot(select.astype(jnp.bfloat16), hidden_act)
    hidden = lax.all_to_all(
        hidden.reshape(live_rows, shards, units).swapaxes(0, 1), "dp", split_axis=0, concat_axis=0
    )
    read = lax.all_gather(jnp.dot(select.astype(jnp.bfloat16), readout), "dp", axis=0)

    def one_sum(k, sums):
        product = lax.dot_general(read[k], weight, (((1,), (1,)), ((), ())), preferred_element_type=f32)
        return sums.at[k].set(jnp.sum(product * hidden[k].astype(f32), axis=1))

    sums = lax.fori_loop(0, shards, one_sum, jnp.zeros((shards, live_rows), f32))
    sums = lax.psum(lax.psum_scatter(sums, "dp", scatter_dimension=0, tiled=True)[0], "mp")
    shift = jnp.dot(sums[None, :], select.astype(f32), precision=EXACT).reshape(respond, seglen) * scale
    logit = log_gap + shift
    live = live.reshape(respond, seglen)
    onehot_float = onehot.astype(f32)
    shard_count = lax.psum(jnp.sum(onehot_float * lens.astype(f32)[:, None], axis=0), "dp")
    count_each = jnp.sum(onehot_float * shard_count[None, :], axis=1)
    stale = jnp.power(jnp.float32(0.7), (NVER - 1 - version).astype(f32))
    send = jnp.arange(shards * slots, dtype=jnp.int32)[:, None] == (dest * slots + rank)[None, :]
    log_ratio = lax.all_to_all(
        jnp.dot(send.astype(f32), jnp.where(live, logit, 0.0), precision=EXACT),
        "dp", split_axis=0, concat_axis=0, tiled=True,
    )
    ratio = jnp.exp(logit)
    squash = jnp.tanh((ratio - 1.0) / 0.2)
    clipped = 1.0 + 0.2 * squash
    adv = advantage[:, None]
    slope = jnp.where(ratio * adv <= clipped * adv, 1.0, 1.0 - squash * squash)
    coef = jnp.where(live, -512.0 * stale[:, None] * adv * ratio * slope / count_each[:, None], 0.0)
    coef = jnp.dot(select.astype(f32), coef.reshape(-1, 1), precision=EXACT)[:, 0]
    coefs = lax.all_gather(coef, "dp", axis=0)

    def one_term(k, grad):
        out_grad = (coefs[k][:, None] * scale * read[k].astype(f32)).astype(jnp.bfloat16)
        return grad + lax.dot_general(
            hidden[k], out_grad, (((0,), (0,)), ((), ())), preferred_element_type=f32
        )

    return (log_ratio, lax.fori_loop(0, shards, one_term, jnp.zeros((units, width), f32)))


def body(*args):
    if lax.axis_size("dp") == 8 and lax.axis_size("mp") == 4:
        return cube_body(*args)
    return general_body(*args)


def solution(mesh):
    placed = (
        P("dp", "mp"),
        P("dp", None),
        P("dp", None),
        P("dp"),
        P("dp"),
        P("dp", None),
        P("dp", None),
        P(("mp", "dp"), None),
    )
    return jax.shard_map(
        body,
        mesh=mesh,
        in_specs=placed,
        out_specs=(P("dp", None), P(("mp", "dp"), None)),
        check_vma=False,
    )
```

time: 1030 us -> 156 us (0.15)
  waiting for transfers between devices: 886 us -> 54.8 us
  blocking collectives: 62.1 us -> 0 us
  starting transfers between devices: 0.08 us -> 49.3 us
  Pallas kernels: 0 us -> 41.6 us
  local copies, waits for them, and re-layouts: 39.4 us -> 6.28 us
  matrix products: 24.2 us -> 0 us
  between operations: 14.1 us -> 1.04 us
    unnamed x3 -> x0, waiting for transfers between devices: 577 us -> none
    all_gather x1 -> x0, waiting for transfers between devices: 310 us -> none  [token_shift(): lax.all_gather(weight, 'dp', axis=0, tiled=True)]
    ppermute x0 -> x38, waiting for transfers between devices: none -> 54.8 us  [the longest x23 43.4 us: over_dp(): return lax.ppermute(x, 'dp', [(s, s ^ m) for s in range(shards)])]
    psum x2 -> x0, blocking collectives: 50.7 us -> none  [the longest x1 43.8 us: body(): shard_count = lax.psum(histogram, 'dp')]
    ppermute x0 -> x38, starting transfers between devices: none -> 49.3 us  [the longest x23 41.5 us: over_dp(): return lax.ppermute(x, 'dp', [(s, s ^ m) for s in range(shards)])]
    pallas_call x0 -> x4, Pallas kernels: none -> 41.6 us  [the longest x1 18.4 us: cube_body(): pl.pallas_call(functools.partial(shift_kernel, pieces, len(refs), tuple(r...]
    unnamed x14 -> x65, local copies, waits for them, and re-layouts: 38.4 us -> 4.82 us
    dot_general x3 -> x0, matrix products: 24.2 us -> none  [the longest x1 14.4 us: weight_terms(): lax.dot_general(rows_act, out_grad, (((0,), (0,)), ((), ())), preferred_e...]
  transfers between devices with their start and end apart: 2 -> 38, of which waited for: 2 -> 17; matrix products, arithmetic and copies ran while one was open for 0% -> 1% of each run, Pallas kernels for 0% -> 14%
where the time goes in v1:
time: 156 us
  waiting for transfers between devices  54.8 us (35%)
  starting transfers between devices  49.3 us (32%)
  Pallas kernels  41.6 us (27%)
  local copies, waits for them, and re-layouts  6.28 us (4%)
  other arithmetic  2.67 us (2%)
    ppermute x23, waiting for transfers between devices, over_dp(): return lax.ppermute(x, 'dp', [(s, s ^ m) for s in range(shards)])  43.4 us
    ppermute x23, starting transfers between devices, over_dp(): return lax.ppermute(x, 'dp', [(s, s ^ m) for s in range(shards)])  41.5 us
    pallas_call x1, Pallas kernels, cube_body(): pl.pallas_call(functools.partial(shift_kernel, pieces, len(refs), tuple(r...  18.4 us
    pallas_call x1, Pallas kernels, cube_body(): pl.pallas_call(functools.partial(grad_kernel, pieces, len(refs), shards,...  15.3 us
    ppermute x15, waiting for transfers between devices, over_mp(): return lax.ppermute(x, 'mp', [(s, s ^ m) for s in range(quarters)])  11.4 us
    ppermute x15, starting transfers between devices, over_mp(): return lax.ppermute(x, 'mp', [(s, s ^ m) for s in range(quarters)])  7.85 us
    unnamed x65, local copies, waits for them, and re-layouts  4.82 us
    pallas_call x1, Pallas kernels, cube_body(): pl.pallas_call(functools.partial(pack_readout, live_rows, seglen), out_sh...  4.47 us
  transfers between devices with their start and end apart: 38, of which 17 were waited for; matrix products, arithmetic and copies ran while one was open for 1% of the time, Pallas kernels for 14%

profile of v1, /device:TPU:0, one launch (start us, length us, event | category | flops | bytes accessed | tf_op | source)
XLA Modules:
  0.0 155.8 jit_solution(7491461028125690343)
XLA Ops:
  0.6 1.4 copy.11.gap
  2.0 1.3 copy.10.routes
  3.3 0.6 pad_add_fusion.place
  3.9 4.5 %pack_readout.1 = (f32[8,224]{1,0:T(8,128)}, bf16[224,256]{1,0:T(8,128)(2,1)}, bf16[4,224,640]{2,1,0:T(8,128)(2,1)}, bf16[224,640]{1,0:T(8,128)(2,1)}, bf16[448,640]{1,0:T(8,128)(2,1)}) custom-call(s32[2]{0:T(128)} %pad_add_fusion.place, s32[1,32]{1,0:T(1,128)} %lens.1, s32[32,1]{1,0:T(8,128)} %copy.10.routes, f32[32,8]{1,0:T(8,128)} %copy.11.gap, ...), custom_call_target="tpu_custom_call" | custom-call | tf_op jit(solution)/shard_map/pack_readout/pallas_call | solution.py:255
  8.4 3.0 %collective-permute-start.3 = (bf16[224,640]{1,0:T(8,128)(2,1)}, bf16[224,640]{1,0:T(8,128)(2,1)S(1)}, u32[]{:S(2)}, u32[]{:S(2)}) collective-permute-start(bf16[224,640]{1,0:T(8,128)(2,1)} %get-tuple-element.25), channel_id=1, source_target_pairs={{0,8},{4,12},{8,0},{12,4},{16,24},{20,28},{24,16},{28,20},{1,9},{5... | collective-permute-start | bytes 860168 | tf_op jit(solution)/shard_map/ppermute | solution.py:280
  11.4 2.5 %collective-permute-start = (bf16[224,640]{1,0:T(8,128)(2,1)}, bf16[224,640]{1,0:T(8,128)(2,1)S(1)}, u32[]{:S(2)}, u32[]{:S(2)}) collective-permute-start(bf16[224,640]{1,0:T(8,128)(2,1)} %get-tuple-element.25), channel_id=1, source_target_pairs={{0,24},{4,28},{8,16},{12,20},{16,8},{20,12},{24,0},{28,4},{1,25},{... | collective-permute-start | bytes 860168 | tf_op jit(solution)/shard_map/ppermute | solution.py:280
  13.9 1.5 collective-permute-start.12
  15.4 3.6 %collective-permute-done.3 = bf16[224,640]{1,0:T(8,128)(2,1)S(1)} collective-permute-done((bf16[224,640]{1,0:T(8,128)(2,1)}, bf16[224,640]{1,0:T(8,128)(2,1)S(1)}, u32[]{:S(2)}, u32[]{:S(2)}) %collective-permute-start.3) | collective-permute-done | bytes 286752 | tf_op jit(solution)/shard_map/ppermute | solution.py:280
  19.0 7.9 %collective-permute-done = bf16[224,640]{1,0:T(8,128)(2,1)S(1)} collective-permute-done((bf16[224,640]{1,0:T(8,128)(2,1)}, bf16[224,640]{1,0:T(8,128)(2,1)S(1)}, u32[]{:S(2)}, u32[]{:S(2)}) %collective-permute-start) | collective-permute-done | bytes 286752 | tf_op jit(solution)/shard_map/ppermute | solution.py:280
  26.9 1.6 %collective-permute-start.6 = (bf16[448,640]{1,0:T(8,128)(2,1)S(1)}, bf16[448,640]{1,0:T(8,128)(2,1)S(1)}, u32[]{:S(2)}, u32[]{:S(2)}) collective-permute-start(bf16[448,640]{1,0:T(8,128)(2,1)S(1)} %constant_dynamic-update-slice_fusion.rest_11_), channel_id=1, source_target_pairs={{0,4},{4,0},{8,12},{12,8},{16,20},{20,16},{24,28},{28,24},{1,5},{5... | collective-permute-start | bytes 1720328 | tf_op jit(solution)/shard_map/ppermute | solution.py:280
  28.5 0.6 collective-permute-start.1
  29.1 1.5 collective-permute-start.4
  30.6 0.5 collective-permute-start.35
  31.1 3.5 %pack_hidden.1 = (bf16[784,128]{1,0:T(8,128)(2,1)}, bf16[784,128]{1,0:T(8,128)(2,1)}, bf16[784,128]{1,0:T(8,128)(2,1)}, bf16[784,128]{1,0:T(8,128)(2,1)}, bf16[7...) custom-call(s32[2]{0:T(128)} %pad_add_fusion.place, ...), custom_call_target="tpu_custom_call" | custom-call | tf_op jit(solution)/shard_map/pack_hidden/pallas_call | solution.py:269
  34.7 6.3 %collective-permute-done.35 = f32[8,224]{1,0:T(8,128)S(1)} collective-permute-done((f32[8,224]{1,0:T(8,128)}, f32[8,224]{1,0:T(8,128)S(1)}, u32[]{:S(2)}, u32[]{:S(2)}) %collective-permute-start.35) | collective-permute-done | bytes 7200 | tf_op jit(solution)/shard_map/ppermute | solution.py:280
  41.0 0.1 collective-permute-start.8
  41.1 0.0 collective-permute-done.1.rest_13_
  41.1 1.8 %collective-permute-start.36 = (f32[16,224]{1,0:T(8,128)S(1)}, f32[16,224]{1,0:T(8,128)S(1)}, u32[]{:S(2)}, u32[]{:S(2)}) collective-permute-start(f32[16,224]{1,0:T(8,128)S(1)} %pad_maximum_fusion.2), channel_id=1, source_target_pairs={{0,8},{4,12},{8,0},{12,4},{16,24},{20,28},{24,16},{28,20},{1,9},{5... | collective-permute-start | bytes 43016 | tf_op jit(solution)/shard_map/ppermute | solution.py:280
  43.0 2.8 %collective-permute-done.36 = f32[16,224]{1,0:T(8,128)S(1)} collective-permute-done((f32[16,224]{1,0:T(8,128)S(1)}, f32[16,224]{1,0:T(8,128)S(1)}, u32[]{:S(2)}, u32[]{:S(2)}) %collective-permute-start.36) | collective-permute-done | bytes 14368 | tf_op jit(solution)/shard_map/ppermute | solution.py:280
  45.8 1.5 collective-permute-start.2
  47.3 3.6 %collective-permute-done.8.rest_4_ = bf16[784,128]{1,0:T(8,128)(2,1)S(1)} collective-permute-done((bf16[784,128]{1,0:T(8,128)(2,1)}, bf16[784,128]{1,0:T(8,128)(2,1)S(1)}, u32[]{:S(2)}, u32[]{:S(2)}) %collective-permute-start.8) | collective-permute-done | bytes 200736 | tf_op jit(solution)/shard_map/ppermute | solution.py:280
  50.9 0.0 collective-permute-start.14
  51.0 1.6 %collective-permute-start.20 = (bf16[224,640]{1,0:T(8,128)(2,1)S(1)}, bf16[224,640]{1,0:T(8,128)(2,1)S(1)}, u32[]{:S(2)}, u32[]{:S(2)}) collective-permute-start(bf16[224,640]{1,0:T(8,128)(2,1)S(1)} %collective-permute-done.1.rest_13_), channel_id=1, source_target_pairs={{0,2},{1,3},{2,0},{3,1},{4,6},{5,7},{6,4},{7,5},{8,10},{9,11},{10,... | collective-permute-start | bytes 860168 | tf_op jit(solution)/shard_map/ppermute | solution.py:283
  52.5 1.5 collective-permute-start.17
  54.0 0.0 collective-permute-done.6.rest_15_
  54.1 0.8 collective-permute-start.22
  54.9 5.7 %collective-permute-done.20.rest_21_ = bf16[224,640]{1,0:T(8,128)(2,1)S(1)} collective-permute-done((bf16[224,640]{1,0:T(8,128)(2,1)S(1)}, bf16[224,640]{1,0:T(8,128)(2,1)S(1)}, u32[]{:S(2)}, u32[]{:S(2)}) %collective-permute-start.20) | collective-permute-done | bytes 286752 | tf_op jit(solution)/shard_map/ppermute | solution.py:283
  60.7 2.5 %collective-permute-start.11 = (bf16[784,128]{1,0:T(8,128)(2,1)}, bf16[784,128]{1,0:T(8,128)(2,1)}, u32[]{:S(2)}, u32[]{:S(2)}) collective-permute-start(bf16[784,128]{1,0:T(8,128)(2,1)} %get-tuple-element.38), channel_id=1, source_target_pairs={{0,28},{4,24},{8,20},{12,16},{16,12},{20,8},{24,4},{28,0},{1,29},{... | collective-permute-start | bytes 602120 | tf_op jit(solution)/shard_map/ppermute | solution.py:280
  63.1 2.3 %collective-permute-start.10 = (bf16[784,128]{1,0:T(8,128)(2,1)}, bf16[784,128]{1,0:T(8,128)(2,1)S(1)}, u32[]{:S(2)}, u32[]{:S(2)}) collective-permute-start(bf16[784,128]{1,0:T(8,128)(2,1)} %get-tuple-element.36), channel_id=1, source_target_pairs={{0,24},{4,28},{8,16},{12,20},{16,8},{20,12},{24,0},{28,4},{1,25},{... | collective-permute-start | bytes 602120 | tf_op jit(solution)/shard_map/ppermute | solution.py:280
  65.5 0.1 collective-permute-start.21
  65.6 6.1 %collective-permute-done.11.rest_7_ = bf16[784,128]{1,0:T(8,128)(2,1)} collective-permute-done((bf16[784,128]{1,0:T(8,128)(2,1)}, bf16[784,128]{1,0:T(8,128)(2,1)}, u32[]{:S(2)}, u32[]{:S(2)}) %collective-permute-start.11) | collective-permute-done | bytes 200736 | tf_op jit(solution)/shard_map/ppermute | solution.py:280
  71.7 1.5 collective-permute-start.24
  73.2 2.8 %collective-permute-done.10.rest_6_ = bf16[784,128]{1,0:T(8,128)(2,1)S(1)} collective-permute-done((bf16[784,128]{1,0:T(8,128)(2,1)}, bf16[784,128]{1,0:T(8,128)(2,1)S(1)}, u32[]{:S(2)}, u32[]{:S(2)}) %collective-permute-start.10) | collective-permute-done | bytes 200736 | tf_op jit(solution)/shard_map/ppermute | solution.py:280
  75.9 9.8 %collective-permute-start.7 = (bf16[784,128]{1,0:T(8,128)(2,1)}, bf16[784,128]{1,0:T(8,128)(2,1)}, u32[]{:S(2)}, u32[]{:S(2)}) collective-permute-start(bf16[784,128]{1,0:T(8,128)(2,1)} %get-tuple-element.30), channel_id=1, source_target_pairs={{0,12},{4,8},{8,4},{12,0},{16,28},{20,24},{24,20},{28,16},{1,13},{... | collective-permute-start | bytes 602120 | tf_op jit(solution)/shard_map/ppermute | solution.py:280
  85.7 2.0 %collective-permute-done.9.rest_5_ = bf16[784,128]{1,0:T(8,128)(2,1)S(1)} collective-permute-done((bf16[784,128]{1,0:T(8,128)(2,1)}, bf16[784,128]{1,0:T(8,128)(2,1)S(1)}, u32[]{:S(2)}, u32[]{:S(2)}) %collective-permute-start.9) | collective-permute-done | bytes 200736 | tf_op jit(solution)/shard_map/ppermute | solution.py:280
  87.7 4.5 %collective-permute-done.7.rest_3_ = bf16[784,128]{1,0:T(8,128)(2,1)} collective-permute-done((bf16[784,128]{1,0:T(8,128)(2,1)}, bf16[784,128]{1,0:T(8,128)(2,1)}, u32[]{:S(2)}, u32[]{:S(2)}) %collective-permute-start.7) | collective-permute-done | bytes 200736 | tf_op jit(solution)/shard_map/ppermute | solution.py:280
  92.2 3.1 %collective-permute-done.5.rest_2_ = bf16[784,128]{1,0:T(8,128)(2,1)S(1)} collective-permute-done((bf16[784,128]{1,0:T(8,128)(2,1)}, bf16[784,128]{1,0:T(8,128)(2,1)S(1)}, u32[]{:S(2)}, u32[]{:S(2)}) %collective-permute-start.5) | collective-permute-done | bytes 200736 | tf_op jit(solution)/shard_map/ppermute | solution.py:280
  95.3 0.7 copy-done.21
  96.0 0.5 collective-permute-start.19
  96.5 0.1 collective-permute-start.23
  96.6 0.3 collective-permute-done.18.rest_18_
  96.8 0.2 collective-permute-start.25
  97.0 1.0 collective-permute-start.37
  98.1 0.7 collective-permute-done.19.rest_20_
  98.8 1.2 collective-permute-done.25.rest_26_
  100.2 0.5 copy-done.17
  100.7 0.2 copy-done.9
  100.9 18.4 %shift_sums.1 = f32[8,224]{1,0:T(8,128)} custom-call(s32[2]{0:T(128)} %pad_add_fusion.place, bf16[448,2560]{1,0:T(8,128)(2,1)} %weight.1, bf16[784,128]{1,0:T(8,128)(2,1)} %get-tuple-element.23.rest_0_, bf16[784,128]{1,0:T(8,128)(2,1)} %collective-permute-done.2.rest_1_, bf16[784,128]{1,0:T(8,128)(2,1)} %copy-done.21, ...), custom_call_target="tpu_custom_call" | custom-call | tf_op jit(solution)/shard_map/shift_sums/pallas_call | solution.py:335
  119.3 0.2 collective-permute-start.26
  119.5 1.2 collective-permute-done.26
  120.7 0.7 add.6
  121.4 1.4 collective-permute-start.27
  122.8 2.2 %collective-permute-done.27 = f32[8,224]{1,0:T(8,128)S(1)} collective-permute-done((f32[8,224]{1,0:T(8,128)S(1)}, f32[8,224]{1,0:T(8,128)S(1)}, u32[]{:S(2)}, u32[]{:S(2)}) %collective-permute-start.27) | collective-permute-done | bytes 7200 | tf_op jit(solution)/shard_map/ppermute | solution.py:283
  125.1 2.3 %collective-permute-start.34 = (f32[8,224]{1,0:T(8,128)S(1)}, f32[8,224]{1,0:T(8,128)S(1)}, u32[]{:S(2)}, u32[]{:S(2)}) collective-permute-start(f32[8,224]{1,0:T(8,128)S(1)} %add.7.rest_27_), channel_id=1, source_target_pairs={{0,28},{4,24},{8,20},{12,16},{16,12},{20,8},{24,4},{28,0},{1,29},{... | collective-permute-start | bytes 21512 | tf_op jit(solution)/shard_map/ppermute | solution.py:280
  127.4 1.5 collective-permute-start.33
  128.9 0.1 collective-permute-start.32
  129.0 3.7 %collective-permute-start.31 = (f32[8,224]{1,0:T(8,128)S(1)}, f32[8,224]{1,0:T(8,128)S(1)}, u32[]{:S(2)}, u32[]{:S(2)}) collective-permute-start(f32[8,224]{1,0:T(8,128)S(1)} %add.7.rest_27_), channel_id=1, source_target_pairs={{0,16},{4,20},{8,24},{12,28},{16,0},{20,4},{24,8},{28,12},{1,17},{... | collective-permute-start | bytes 21512 | tf_op jit(solution)/shard_map/ppermute | solution.py:280
  132.7 2.0 %collective-permute-start.29 = (f32[8,224]{1,0:T(8,128)S(1)}, f32[8,224]{1,0:T(8,128)S(1)}, u32[]{:S(2)}, u32[]{:S(2)}) collective-permute-start(f32[8,224]{1,0:T(8,128)S(1)} %add.7.rest_27_), channel_id=1, source_target_pairs={{0,8},{4,12},{8,0},{12,4},{16,24},{20,28},{24,16},{28,20},{1,9},{5... | collective-permute-start | bytes 21512 | tf_op jit(solution)/shard_map/ppermute | solution.py:280
  134.8 1.5 collective-permute-start.28
  136.2 1.4 pad_maximum_fusion.rest_35_
  137.7 0.7 collective-permute-done.28.rest_28_
  138.5 0.6 copy-done.30
  139.1 15.3 %weight_grad.1 = (f32[64,8]{1,0:T(8,128)}, f32[448,2560]{1,0:T(8,128)}) custom-call(s32[2]{0:T(128)} %pad_add_fusion.place, bf16[784,128]{1,0:T(8,128)(2,1)} %get-tuple-element.23.rest_0_, bf16[784,128]{1,0:T(8,128)(2,1)} %collective-permute-done.2.rest_1_, bf16[784,128]{1,0:T(8,128)(2,1)} %copy-done.21, bf16[784,128]{1,0:T(8,128)(2,1)} %collective-permute-done.7.rest_3_, ...), custom_call_target="tpu_custom_call" | custom-call | tf_op jit(solution)/shard_map/weight_grad/pallas_call | solution.py:353
  154.4 1.4 copy.12
  (89 shorter events, 0.3 us)
Async XLA Ops:
  8.4 32.7 %copy-start.22 = (f32[8,224]{1,0:T(8,128)S(1)}, f32[8,224]{1,0:T(8,128)}, u32[]{:S(2)}) copy-start(f32[8,224]{1,0:T(8,128)} %get-tuple-element.41) | copy-start | bytes 21508
  8.4 10.6 %collective-permute-start.3 = (bf16[224,640]{1,0:T(8,128)(2,1)}, bf16[224,640]{1,0:T(8,128)(2,1)S(1)}, u32[]{:S(2)}, u32[]{:S(2)}) collective-permute-start(bf16[224,640]{1,0:T(8,128)(2,1)} %get-tuple-element.25), channel_id=1, source_target_pairs={{0,8},{4,12},{8,0},{12,4},{16,24},{20,28},{24,16},{28,20},{1,9},{5... | collective-permute-start | bytes 860168 | tf_op jit(solution)/shard_map/ppermute | solution.py:280
  11.4 15.5 %collective-permute-start = (bf16[224,640]{1,0:T(8,128)(2,1)}, bf16[224,640]{1,0:T(8,128)(2,1)S(1)}, u32[]{:S(2)}, u32[]{:S(2)}) collective-permute-start(bf16[224,640]{1,0:T(8,128)(2,1)} %get-tuple-element.25), channel_id=1, source_target_pairs={{0,24},{4,28},{8,16},{12,20},{16,8},{20,12},{24,0},{28,4},{1,25},{... | collective-permute-start | bytes 860168 | tf_op jit(solution)/shard_map/ppermute | solution.py:280
  13.9 37.1 %collective-permute-start.12 = (bf16[448,640]{1,0:T(8,128)(2,1)}, bf16[448,640]{1,0:T(8,128)(2,1)S(1)}, u32[]{:S(2)}, u32[]{:S(2)}) collective-permute-start(bf16[448,640]{1,0:T(8,128)(2,1)} %get-tuple-element.40), channel_id=1, source_target_pairs={{0,4},{4,0},{8,12},{12,8},{16,20},{20,16},{24,28},{28,24},{1,5},{5... | collective-permute-start | bytes 1720328 | tf_op jit(solution)/shard_map/ppermute | solution.py:280
  26.9 73.1 %copy-start = (bf16[448,640]{1,0:T(8,128)(2,1)}, bf16[448,640]{1,0:T(8,128)(2,1)S(1)}, u32[]{:S(2)}) copy-start(bf16[448,640]{1,0:T(8,128)(2,1)S(1)} %constant_dynamic-update-slice_fusion.rest_11_) | copy-start | bytes 1720324
  26.9 27.1 %collective-permute-start.6 = (bf16[448,640]{1,0:T(8,128)(2,1)S(1)}, bf16[448,640]{1,0:T(8,128)(2,1)S(1)}, u32[]{:S(2)}, u32[]{:S(2)}) collective-permute-start(bf16[448,640]{1,0:T(8,128)(2,1)S(1)} %constant_dynamic-update-slice_fusion.rest_11_), channel_id=1, source_target_pairs={{0,4},{4,0},{8,12},{12,8},{16,20},{20,16},{24,28},{28,24},{1,5},{5... | collective-permute-start | bytes 1720328 | tf_op jit(solution)/shard_map/ppermute | solution.py:280
  28.5 12.6 %collective-permute-start.1 = (bf16[224,640]{1,0:T(8,128)(2,1)S(1)}, bf16[224,640]{1,0:T(8,128)(2,1)S(1)}, u32[]{:S(2)}, u32[]{:S(2)}) collective-permute-start(bf16[224,640]{1,0:T(8,128)(2,1)S(1)} %collective-permute-done), channel_id=1, source_target_pairs={{0,8},{4,12},{8,0},{12,4},{16,24},{20,28},{24,16},{28,20},{1,9},{5... | collective-permute-start | bytes 860168 | tf_op jit(solution)/shard_map/ppermute | solution.py:280
  29.1 24.9 %collective-permute-start.4 = (bf16[448,640]{1,0:T(8,128)(2,1)S(1)}, bf16[448,640]{1,0:T(8,128)(2,1)S(1)}, u32[]{:S(2)}, u32[]{:S(2)}) collective-permute-start(bf16[448,640]{1,0:T(8,128)(2,1)S(1)} %constant_dynamic-update-slice_fusion.rest_11_), channel_id=1, source_target_pairs={{0,2},{1,3},{2,0},{3,1},{4,6},{5,7},{6,4},{7,5},{8,10},{9,11},{10,... | collective-permute-start | bytes 1720328 | tf_op jit(solution)/shard_map/ppermute | solution.py:283
  30.6 10.3 %collective-permute-start.35 = (f32[8,224]{1,0:T(8,128)}, f32[8,224]{1,0:T(8,128)S(1)}, u32[]{:S(2)}, u32[]{:S(2)}) collective-permute-start(f32[8,224]{1,0:T(8,128)} %get-tuple-element.41), channel_id=1, source_target_pairs={{0,4},{4,0},{8,12},{12,8},{16,20},{20,16},{24,28},{28,24},{1,5},{5... | collective-permute-start | bytes 21512 | tf_op jit(solution)/shard_map/ppermute | solution.py:280
  41.0 10.0 %collective-permute-start.8 = (bf16[784,128]{1,0:T(8,128)(2,1)}, bf16[784,128]{1,0:T(8,128)(2,1)S(1)}, u32[]{:S(2)}, u32[]{:S(2)}) collective-permute-start(bf16[784,128]{1,0:T(8,128)(2,1)} %get-tuple-element.32), channel_id=1, source_target_pairs={{0,16},{4,20},{8,24},{12,28},{16,0},{20,4},{24,8},{28,12},{1,17},{... | collective-permute-start | bytes 602120 | tf_op jit(solution)/shard_map/ppermute | solution.py:280
  41.1 58.9 %copy-start.10 = (bf16[224,640]{1,0:T(8,128)(2,1)}, bf16[224,640]{1,0:T(8,128)(2,1)S(1)}, u32[]{:S(2)}) copy-start(bf16[224,640]{1,0:T(8,128)(2,1)S(1)} %collective-permute-done.1.rest_13_) | copy-start | bytes 860164
  41.1 4.6 %collective-permute-start.36 = (f32[16,224]{1,0:T(8,128)S(1)}, f32[16,224]{1,0:T(8,128)S(1)}, u32[]{:S(2)}, u32[]{:S(2)}) collective-permute-start(f32[16,224]{1,0:T(8,128)S(1)} %pad_maximum_fusion.2), channel_id=1, source_target_pairs={{0,8},{4,12},{8,0},{12,4},{16,24},{20,28},{24,16},{28,20},{1,9},{5... | collective-permute-start | bytes 43016 | tf_op jit(solution)/shard_map/ppermute | solution.py:280
  45.8 6.7 %collective-permute-start.2 = (bf16[784,128]{1,0:T(8,128)(2,1)}, bf16[784,128]{1,0:T(8,128)(2,1)}, u32[]{:S(2)}, u32[]{:S(2)}) collective-permute-start(bf16[784,128]{1,0:T(8,128)(2,1)} %get-tuple-element.26), channel_id=1, source_target_pairs={{0,4},{4,0},{8,12},{12,8},{16,20},{20,16},{24,28},{28,24},{1,5},{5... | collective-permute-start | bytes 602120 | tf_op jit(solution)/shard_map/ppermute | solution.py:280
  50.9 49.1 %copy-start.18 = (bf16[784,128]{1,0:T(8,128)(2,1)}, bf16[784,128]{1,0:T(8,128)(2,1)S(1)}, u32[]{:S(2)}) copy-start(bf16[784,128]{1,0:T(8,128)(2,1)S(1)} %collective-permute-done.8.rest_4_) | copy-start | bytes 602116
  50.9 14.5 %collective-permute-start.14 = (bf16[448,640]{1,0:T(8,128)(2,1)S(1)}, bf16[448,640]{1,0:T(8,128)(2,1)S(1)}, u32[]{:S(2)}, u32[]{:S(2)}) collective-permute-start(bf16[448,640]{1,0:T(8,128)(2,1)S(1)} %constant_dynamic-update-slice_fusion.rest_11_), channel_id=1, source_target_pairs={{0,1},{1,0},{2,3},{3,2},{4,5},{5,4},{6,7},{7,6},{8,9},{9,8},{10,11... | collective-permute-start | bytes 1720328 | tf_op jit(solution)/shard_map/ppermute | solution.py:283
  51.0 49.1 %copy-start.1 = (bf16[448,640]{1,0:T(8,128)(2,1)}, bf16[448,640]{1,0:T(8,128)(2,1)S(1)}, u32[]{:S(2)}) copy-start(bf16[448,640]{1,0:T(8,128)(2,1)S(1)} %collective-permute-done.12.rest_9_) | copy-start | bytes 1720324
  51.0 9.7 %collective-permute-start.20 = (bf16[224,640]{1,0:T(8,128)(2,1)S(1)}, bf16[224,640]{1,0:T(8,128)(2,1)S(1)}, u32[]{:S(2)}, u32[]{:S(2)}) collective-permute-start(bf16[224,640]{1,0:T(8,128)(2,1)S(1)} %collective-permute-done.1.rest_13_), channel_id=1, source_target_pairs={{0,2},{1,3},{2,0},{3,1},{4,6},{5,7},{6,4},{7,5},{8,10},{9,11},{10,... | collective-permute-start | bytes 860168 | tf_op jit(solution)/shard_map/ppermute | solution.py:283
  52.5 10.6 %collective-permute-start.17 = (bf16[224,640]{1,0:T(8,128)(2,1)S(1)}, bf16[224,640]{1,0:T(8,128)(2,1)S(1)}, u32[]{:S(2)}, u32[]{:S(2)}) collective-permute-start(bf16[224,640]{1,0:T(8,128)(2,1)S(1)} %collective-permute-done.1.rest_13_), channel_id=1, source_target_pairs={{0,4},{4,0},{8,12},{12,8},{16,20},{20,16},{24,28},{28,24},{1,5},{5... | collective-permute-start | bytes 860168 | tf_op jit(solution)/shard_map/ppermute | solution.py:280
  54.0 46.0 %copy-start.2 = (bf16[448,640]{1,0:T(8,128)(2,1)}, bf16[448,640]{1,0:T(8,128)(2,1)S(1)}, u32[]{:S(2)}) copy-start(bf16[448,640]{1,0:T(8,128)(2,1)S(1)} %collective-permute-done.6.rest_15_) | copy-start | bytes 1720324
  54.1 11.4 %collective-permute-start.15 = (bf16[224,640]{1,0:T(8,128)(2,1)S(1)}, bf16[224,640]{1,0:T(8,128)(2,1)S(1)}, u32[]{:S(2)}, u32[]{:S(2)}) collective-permute-start(bf16[224,640]{1,0:T(8,128)(2,1)S(1)} %collective-permute-done.1.rest_13_), channel_id=1, source_target_pairs={{0,1},{1,0},{2,3},{3,2},{4,5},{5,4},{6,7},{7,6},{8,9},{9,8},{10,11... | collective-permute-start | bytes 860168 | tf_op jit(solution)/shard_map/ppermute | solution.py:283
  54.1 46.0 %copy-start.3 = (bf16[448,640]{1,0:T(8,128)(2,1)}, bf16[448,640]{1,0:T(8,128)(2,1)S(1)}, u32[]{:S(2)}) copy-start(bf16[448,640]{1,0:T(8,128)(2,1)S(1)} %collective-permute-done.4.rest_19_) | copy-start | bytes 1720324
  54.1 42.4 %collective-permute-start.22 = (bf16[448,640]{1,0:T(8,128)(2,1)S(1)}, bf16[448,640]{1,0:T(8,128)(2,1)S(1)}, u32[]{:S(2)}, u32[]{:S(2)}) collective-permute-start(bf16[448,640]{1,0:T(8,128)(2,1)S(1)} %collective-permute-done.6.rest_15_), channel_id=1, source_target_pairs={{0,2},{1,3},{2,0},{3,1},{4,6},{5,7},{6,4},{7,5},{8,10},{9,11},{10,... | collective-permute-start | bytes 1720328 | tf_op jit(solution)/shard_map/ppermute | solution.py:283
  60.7 39.4 %copy-start.11 = (bf16[224,640]{1,0:T(8,128)(2,1)}, bf16[224,640]{1,0:T(8,128)(2,1)S(1)}, u32[]{:S(2)}) copy-start(bf16[224,640]{1,0:T(8,128)(2,1)S(1)} %collective-permute-done.20.rest_21_) | copy-start | bytes 860164
  60.7 11.0 %collective-permute-start.11 = (bf16[784,128]{1,0:T(8,128)(2,1)}, bf16[784,128]{1,0:T(8,128)(2,1)}, u32[]{:S(2)}, u32[]{:S(2)}) collective-permute-start(bf16[784,128]{1,0:T(8,128)(2,1)} %get-tuple-element.38), channel_id=1, source_target_pairs={{0,28},{4,24},{8,20},{12,16},{16,12},{20,8},{24,4},{28,0},{1,29},{... | collective-permute-start | bytes 602120 | tf_op jit(solution)/shard_map/ppermute | solution.py:280
  63.1 36.9 %copy-start.12 = (bf16[224,640]{1,0:T(8,128)(2,1)}, bf16[224,640]{1,0:T(8,128)(2,1)S(1)}, u32[]{:S(2)}) copy-start(bf16[224,640]{1,0:T(8,128)(2,1)S(1)} %collective-permute-done.17.rest_17_) | copy-start | bytes 860164
  63.1 12.8 %collective-permute-start.10 = (bf16[784,128]{1,0:T(8,128)(2,1)}, bf16[784,128]{1,0:T(8,128)(2,1)S(1)}, u32[]{:S(2)}, u32[]{:S(2)}) collective-permute-start(bf16[784,128]{1,0:T(8,128)(2,1)} %get-tuple-element.36), channel_id=1, source_target_pairs={{0,24},{4,28},{8,16},{12,20},{16,8},{20,12},{24,0},{28,4},{1,25},{... | collective-permute-start | bytes 602120 | tf_op jit(solution)/shard_map/ppermute | solution.py:280
  65.5 34.6 %copy-start.13 = (bf16[224,640]{1,0:T(8,128)(2,1)}, bf16[224,640]{1,0:T(8,128)(2,1)S(1)}, u32[]{:S(2)}) copy-start(bf16[224,640]{1,0:T(8,128)(2,1)S(1)} %collective-permute-done.15.rest_14_) | copy-start | bytes 860164
  65.5 22.2 %collective-permute-start.9 = (bf16[784,128]{1,0:T(8,128)(2,1)}, bf16[784,128]{1,0:T(8,128)(2,1)S(1)}, u32[]{:S(2)}, u32[]{:S(2)}) collective-permute-start(bf16[784,128]{1,0:T(8,128)(2,1)} %get-tuple-element.34), channel_id=1, source_target_pairs={{0,20},{4,16},{8,28},{12,24},{16,4},{20,0},{24,12},{28,8},{1,21},{... | collective-permute-start | bytes 602120 | tf_op jit(solution)/shard_map/ppermute | solution.py:280
  65.5 34.6 %copy-start.4 = (bf16[448,640]{1,0:T(8,128)(2,1)}, bf16[448,640]{1,0:T(8,128)(2,1)S(1)}, u32[]{:S(2)}) copy-start(bf16[448,640]{1,0:T(8,128)(2,1)S(1)} %collective-permute-done.14.rest_12_) | copy-start | bytes 1720324
  65.5 30.5 %collective-permute-start.21 = (bf16[224,640]{1,0:T(8,128)(2,1)S(1)}, bf16[224,640]{1,0:T(8,128)(2,1)S(1)}, u32[]{:S(2)}, u32[]{:S(2)}) collective-permute-start(bf16[224,640]{1,0:T(8,128)(2,1)S(1)} %collective-permute-done.20.rest_21_), channel_id=1, source_target_pairs={{0,1},{1,0},{2,3},{3,2},{4,5},{5,4},{6,7},{7,6},{8,9},{9,8},{10,11... | collective-permute-start | bytes 860168 | tf_op jit(solution)/shard_map/ppermute | solution.py:283
  71.7 24.3 %collective-permute-start.24 = (bf16[224,640]{1,0:T(8,128)(2,1)S(1)}, bf16[224,640]{1,0:T(8,128)(2,1)S(1)}, u32[]{:S(2)}, u32[]{:S(2)}) collective-permute-start(bf16[224,640]{1,0:T(8,128)(2,1)S(1)} %collective-permute-done.17.rest_17_), channel_id=1, source_target_pairs={{0,2},{1,3},{2,0},{3,1},{4,6},{5,7},{6,4},{7,5},{8,10},{9,11},{10,... | collective-permute-start | bytes 860168 | tf_op jit(solution)/shard_map/ppermute | solution.py:283
  75.9 16.3 %copy-start.19 = (bf16[784,128]{1,0:T(8,128)(2,1)}, bf16[784,128]{1,0:T(8,128)(2,1)S(1)}, u32[]{:S(2)}) copy-start(bf16[784,128]{1,0:T(8,128)(2,1)S(1)} %collective-permute-done.10.rest_6_) | copy-start | bytes 602116
  75.9 16.2 %collective-permute-start.7 = (bf16[784,128]{1,0:T(8,128)(2,1)}, bf16[784,128]{1,0:T(8,128)(2,1)}, u32[]{:S(2)}, u32[]{:S(2)}) collective-permute-start(bf16[784,128]{1,0:T(8,128)(2,1)} %get-tuple-element.30), channel_id=1, source_target_pairs={{0,12},{4,8},{8,4},{12,0},{16,28},{20,24},{24,20},{28,16},{1,13},{... | collective-permute-start | bytes 602120 | tf_op jit(solution)/shard_map/ppermute | solution.py:280
  87.7 4.5 %copy-start.20 = (bf16[784,128]{1,0:T(8,128)(2,1)}, bf16[784,128]{1,0:T(8,128)(2,1)S(1)}, u32[]{:S(2)}) copy-start(bf16[784,128]{1,0:T(8,128)(2,1)S(1)} %collective-permute-done.9.rest_5_) | copy-start | bytes 602116
  87.7 7.6 %collective-permute-start.5 = (bf16[784,128]{1,0:T(8,128)(2,1)}, bf16[784,128]{1,0:T(8,128)(2,1)S(1)}, u32[]{:S(2)}, u32[]{:S(2)}) collective-permute-start(bf16[784,128]{1,0:T(8,128)(2,1)} %get-tuple-element.28), channel_id=1, source_target_pairs={{0,8},{4,12},{8,0},{12,4},{16,24},{20,28},{24,16},{28,20},{1,9},{5... | collective-permute-start | bytes 602120 | tf_op jit(solution)/shard_map/ppermute | solution.py:280
  92.2 4.9 %collective-permute-start.13 = (bf16[448,640]{1,0:T(8,128)(2,1)S(1)}, bf16[448,640]{1,0:T(8,128)(2,1)S(1)}, u32[]{:S(2)}, u32[]{:S(2)}) collective-permute-start(bf16[448,640]{1,0:T(8,128)(2,1)S(1)} %collective-permute-done.12.rest_9_), channel_id=1, source_target_pairs={{0,1},{1,0},{2,3},{3,2},{4,5},{5,4},{6,7},{7,6},{8,9},{9,8},{10,11... | collective-permute-start | bytes 1720328 | tf_op jit(solution)/shard_map/ppermute | solution.py:283
  95.3 1.6 %collective-permute-start.18 = (bf16[224,640]{1,0:T(8,128)(2,1)S(1)}, bf16[224,640]{1,0:T(8,128)(2,1)S(1)}, u32[]{:S(2)}, u32[]{:S(2)}) collective-permute-start(bf16[224,640]{1,0:T(8,128)(2,1)S(1)} %collective-permute-done.17.rest_17_), channel_id=1, source_target_pairs={{0,1},{1,0},{2,3},{3,2},{4,5},{5,4},{6,7},{7,6},{8,9},{9,8},{10,11... | collective-permute-start | bytes 860168 | tf_op jit(solution)/shard_map/ppermute | solution.py:283
  96.0 4.1 %copy-start.14 = (bf16[224,640]{1,0:T(8,128)(2,1)}, bf16[224,640]{1,0:T(8,128)(2,1)S(1)}, u32[]{:S(2)}) copy-start(bf16[224,640]{1,0:T(8,128)(2,1)S(1)} %collective-permute-done.21.rest_22_) | copy-start | bytes 860164
  96.0 2.1 %collective-permute-start.16 = (bf16[448,640]{1,0:T(8,128)(2,1)S(1)}, bf16[448,640]{1,0:T(8,128)(2,1)S(1)}, u32[]{:S(2)}, u32[]{:S(2)}) collective-permute-start(bf16[448,640]{1,0:T(8,128)(2,1)S(1)} %collective-permute-done.6.rest_15_), channel_id=1, source_target_pairs={{0,1},{1,0},{2,3},{3,2},{4,5},{5,4},{6,7},{7,6},{8,9},{9,8},{10,11... | collective-permute-start | bytes 1720328 | tf_op jit(solution)/shard_map/ppermute | solution.py:283
  96.0 4.1 %copy-start.15 = (bf16[224,640]{1,0:T(8,128)(2,1)}, bf16[224,640]{1,0:T(8,128)(2,1)S(1)}, u32[]{:S(2)}) copy-start(bf16[224,640]{1,0:T(8,128)(2,1)S(1)} %collective-permute-done.24.rest_25_) | copy-start | bytes 860164
  96.0 2.8 %collective-permute-start.19 = (bf16[448,640]{1,0:T(8,128)(2,1)S(1)}, bf16[448,640]{1,0:T(8,128)(2,1)S(1)}, u32[]{:S(2)}, u32[]{:S(2)}) collective-permute-start(bf16[448,640]{1,0:T(8,128)(2,1)S(1)} %collective-permute-done.4.rest_19_), channel_id=1, source_target_pairs={{0,1},{1,0},{2,3},{3,2},{4,5},{5,4},{6,7},{7,6},{8,9},{9,8},{10,11... | collective-permute-start | bytes 1720328 | tf_op jit(solution)/shard_map/ppermute | solution.py:283
  96.5 3.6 %copy-start.5 = (bf16[448,640]{1,0:T(8,128)(2,1)}, bf16[448,640]{1,0:T(8,128)(2,1)S(1)}, u32[]{:S(2)}) copy-start(bf16[448,640]{1,0:T(8,128)(2,1)S(1)} %collective-permute-done.22.rest_23_) | copy-start | bytes 1720324
  96.5 3.5 %collective-permute-start.23 = (bf16[448,640]{1,0:T(8,128)(2,1)S(1)}, bf16[448,640]{1,0:T(8,128)(2,1)S(1)}, u32[]{:S(2)}, u32[]{:S(2)}) collective-permute-start(bf16[448,640]{1,0:T(8,128)(2,1)S(1)} %collective-permute-done.22.rest_23_), channel_id=1, source_target_pairs={{0,1},{1,0},{2,3},{3,2},{4,5},{5,4},{6,7},{7,6},{8,9},{9,8},{10,11... | collective-permute-start | bytes 1720328 | tf_op jit(solution)/shard_map/ppermute | solution.py:283
  96.8 3.3 %copy-start.16 = (bf16[224,640]{1,0:T(8,128)(2,1)}, bf16[224,640]{1,0:T(8,128)(2,1)S(1)}, u32[]{:S(2)}) copy-start(bf16[224,640]{1,0:T(8,128)(2,1)S(1)} %collective-permute-done.18.rest_18_) | copy-start | bytes 860164
  96.8 3.2 %collective-permute-start.25 = (bf16[224,640]{1,0:T(8,128)(2,1)S(1)}, bf16[224,640]{1,0:T(8,128)(2,1)S(1)}, u32[]{:S(2)}, u32[]{:S(2)}) collective-permute-start(bf16[224,640]{1,0:T(8,128)(2,1)S(1)} %collective-permute-done.24.rest_25_), channel_id=1, source_target_pairs={{0,1},{1,0},{2,3},{3,2},{4,5},{5,4},{6,7},{7,6},{8,9},{9,8},{10,11... | collective-permute-start | bytes 860168 | tf_op jit(solution)/shard_map/ppermute | solution.py:283
  97.0 3.1 %copy-start.6 = (bf16[448,640]{1,0:T(8,128)(2,1)}, bf16[448,640]{1,0:T(8,128)(2,1)S(1)}, u32[]{:S(2)}) copy-start(bf16[448,640]{1,0:T(8,128)(2,1)S(1)} %collective-permute-done.13.rest_10_) | copy-start | bytes 1720324
  97.0 35.7 %collective-permute-start.37 = (f32[32,224]{1,0:T(8,128)S(1)}, f32[32,224]{1,0:T(8,128)}, u32[]{:S(2)}, u32[]{:S(2)}) collective-permute-start(f32[32,224]{1,0:T(8,128)S(1)} %pad_maximum_fusion.1), channel_id=1, source_target_pairs={{0,16},{4,20},{8,24},{12,28},{16,0},{20,4},{24,8},{28,12},{1,17},{... | collective-permute-start | bytes 86024 | tf_op jit(solution)/shard_map/ppermute | solution.py:280
  98.1 2.1 %copy-start.7 = (bf16[448,640]{1,0:T(8,128)(2,1)}, bf16[448,640]{1,0:T(8,128)(2,1)S(1)}, u32[]{:S(2)}) copy-start(bf16[448,640]{1,0:T(8,128)(2,1)S(1)} %collective-permute-done.16.rest_16_) | copy-start | bytes 1720324
  98.8 1.4 copy-start.8
  100.0 0.9 copy-start.9
  119.3 1.4 collective-permute-start.26
  121.4 3.7 %collective-permute-start.27 = (f32[8,224]{1,0:T(8,128)S(1)}, f32[8,224]{1,0:T(8,128)S(1)}, u32[]{:S(2)}, u32[]{:S(2)}) collective-permute-start(f32[8,224]{1,0:T(8,128)S(1)} %add.6), channel_id=1, source_target_pairs={{0,2},{1,3},{2,0},{3,1},{4,6},{5,7},{6,4},{7,5},{8,10},{9,11},{10,... | collective-permute-start | bytes 21512 | tf_op jit(solution)/shard_map/ppermute | solution.py:283
  125.1 13.3 %copy-start.23 = (f32[8,224]{1,0:T(8,128)}, f32[8,224]{1,0:T(8,128)S(1)}, u32[]{:S(2)}) copy-start(f32[8,224]{1,0:T(8,128)S(1)} %add.7.rest_27_) | copy-start | bytes 21508
  125.1 7.7 %collective-permute-start.34 = (f32[8,224]{1,0:T(8,128)S(1)}, f32[8,224]{1,0:T(8,128)S(1)}, u32[]{:S(2)}, u32[]{:S(2)}) collective-permute-start(f32[8,224]{1,0:T(8,128)S(1)} %add.7.rest_27_), channel_id=1, source_target_pairs={{0,28},{4,24},{8,20},{12,16},{16,12},{20,8},{24,4},{28,0},{1,29},{... | collective-permute-start | bytes 21512 | tf_op jit(solution)/shard_map/ppermute | solution.py:280
  127.4 7.4 %collective-permute-start.33 = (f32[8,224]{1,0:T(8,128)S(1)}, f32[8,224]{1,0:T(8,128)S(1)}, u32[]{:S(2)}, u32[]{:S(2)}) collective-permute-start(f32[8,224]{1,0:T(8,128)S(1)} %add.7.rest_27_), channel_id=1, source_target_pairs={{0,24},{4,28},{8,16},{12,20},{16,8},{20,12},{24,0},{28,4},{1,25},{... | collective-permute-start | bytes 21512 | tf_op jit(solution)/shard_map/ppermute | solution.py:280
  128.9 8.7 %collective-permute-start.32 = (f32[8,224]{1,0:T(8,128)S(1)}, f32[8,224]{1,0:T(8,128)S(1)}, u32[]{:S(2)}, u32[]{:S(2)}) collective-permute-start(f32[8,224]{1,0:T(8,128)S(1)} %add.7.rest_27_), channel_id=1, source_target_pairs={{0,20},{4,16},{8,28},{12,24},{16,4},{20,0},{24,12},{28,8},{1,21},{... | collective-permute-start | bytes 21512 | tf_op jit(solution)/shard_map/ppermute | solution.py:280
  129.0 8.6 %collective-permute-start.31 = (f32[8,224]{1,0:T(8,128)S(1)}, f32[8,224]{1,0:T(8,128)S(1)}, u32[]{:S(2)}, u32[]{:S(2)}) collective-permute-start(f32[8,224]{1,0:T(8,128)S(1)} %add.7.rest_27_), channel_id=1, source_target_pairs={{0,16},{4,20},{8,24},{12,28},{16,0},{20,4},{24,8},{28,12},{1,17},{... | collective-permute-start | bytes 21512 | tf_op jit(solution)/shard_map/ppermute | solution.py:280
  132.7 4.9 %collective-permute-start.30 = (f32[8,224]{1,0:T(8,128)S(1)}, f32[8,224]{1,0:T(8,128)S(1)}, u32[]{:S(2)}, u32[]{:S(2)}) collective-permute-start(f32[8,224]{1,0:T(8,128)S(1)} %add.7.rest_27_), channel_id=1, source_target_pairs={{0,12},{4,8},{8,4},{12,0},{16,28},{20,24},{24,20},{28,16},{1,13},{... | collective-permute-start | bytes 21512 | tf_op jit(solution)/shard_map/ppermute | solution.py:280
  132.7 5.7 %copy-start.24 = (f32[8,224]{1,0:T(8,128)}, f32[8,224]{1,0:T(8,128)S(1)}, u32[]{:S(2)}) copy-start(f32[8,224]{1,0:T(8,128)S(1)} %collective-permute-done.34.rest_34_) | copy-start | bytes 21508
  132.7 4.9 %collective-permute-start.29 = (f32[8,224]{1,0:T(8,128)S(1)}, f32[8,224]{1,0:T(8,128)S(1)}, u32[]{:S(2)}, u32[]{:S(2)}) collective-permute-start(f32[8,224]{1,0:T(8,128)S(1)} %add.7.rest_27_), channel_id=1, source_target_pairs={{0,8},{4,12},{8,0},{12,4},{16,24},{20,28},{24,16},{28,20},{1,9},{5... | collective-permute-start | bytes 21512 | tf_op jit(solution)/shard_map/ppermute | solution.py:280
  134.8 3.7 %copy-start.25 = (f32[8,224]{1,0:T(8,128)}, f32[8,224]{1,0:T(8,128)S(1)}, u32[]{:S(2)}) copy-start(f32[8,224]{1,0:T(8,128)S(1)} %collective-permute-done.33.rest_33_) | copy-start | bytes 21508
  134.8 3.7 %collective-permute-start.28 = (f32[8,224]{1,0:T(8,128)S(1)}, f32[8,224]{1,0:T(8,128)S(1)}, u32[]{:S(2)}, u32[]{:S(2)}) collective-permute-start(f32[8,224]{1,0:T(8,128)S(1)} %add.7.rest_27_), channel_id=1, source_target_pairs={{0,4},{4,0},{8,12},{12,8},{16,20},{20,16},{24,28},{28,24},{1,5},{5... | collective-permute-start | bytes 21512 | tf_op jit(solution)/shard_map/ppermute | solution.py:280
  137.6 0.8 copy-start.26
  137.6 0.8 copy-start.27
  (5 other events, 3.6 us)

commit v2 on v0

v2 whole, which is shorter than its diff:
```python
import functools
import math

import jax
import jax.numpy as jnp
import numpy as np
from jax import lax
from jax.experimental import pallas as pl
from jax.experimental.pallas import tpu as pltpu
from jax.sharding import PartitionSpec as P

NVER = 4
SCALE = 0.15
EXACT = lax.Precision.HIGHEST
VMEM = pl.BlockSpec(memory_space=pltpu.VMEM)
SMEM = pl.BlockSpec(memory_space=pltpu.SMEM)
ANY = pl.BlockSpec(memory_space=pl.ANY)
GAP, ADV, STALE, DEST, RANK, POS = range(6)


def iota(shape, axis):
    return lax.broadcasted_iota(jnp.int32, shape, axis)


def rows_of(*rows):
    n = rows[0].shape[1]
    row = iota((8, n), 0)
    table = jnp.zeros((8, n), jnp.float32)
    for i, values in enumerate(rows):
        table = jnp.where(row == i, values, table)
    return table


def my_place():
    return lax.axis_index("dp"), lax.axis_index("mp")


def live_tokens(live_rows, seglen, lens):
    respond = lens.shape[1]
    tokens = respond * seglen
    expand = (iota((respond, tokens), 0) == lax.div(iota((respond, tokens), 1), seglen)).astype(jnp.bfloat16)
    lens_wide = jnp.broadcast_to(lens.astype(jnp.float32), (16, respond)).astype(jnp.bfloat16)
    by_token = jnp.dot(lens_wide, expand, preferred_element_type=jnp.float32)
    live = lax.rem(iota((16, tokens), 1), seglen).astype(jnp.float32) < by_token
    before = (iota((tokens, tokens), 0) < iota((tokens, tokens), 1)).astype(jnp.bfloat16)
    order = jnp.dot(live.astype(jnp.float32).astype(jnp.bfloat16), before, preferred_element_type=jnp.float32)
    place = jnp.where(live, order, -1.0)[0:1, :]
    return place == iota((live_rows, tokens), 0).astype(jnp.float32)


def pack_first(live_rows, seglen, lens, read, first, both, held, sems):
    _, mp = my_place()
    wide = held.shape[2]
    copies = []
    for i, e in enumerate((0, 2)):
        columns = pl.ds(pl.multiple_of((mp ^ e) * wide, 128), wide)
        copies.append(pltpu.make_async_copy(read.at[:, columns], held.at[i], sems.at[i]))
        copies[-1].start()
    select = live_tokens(live_rows, seglen, lens[...]).astype(jnp.float32).astype(jnp.bfloat16)
    for i in range(2):
        copies[i].wait()
        part = jnp.dot(select, held[i], preferred_element_type=jnp.float32).astype(jnp.bfloat16)
        both[i * live_rows:(i + 1) * live_rows] = part
        if i == 0:
            first[...] = part


def packed_rows(units, live_rows):
    return units * live_rows // 128


def fold_of(live_rows):
    tail = live_rows - 128
    return tail, 128 // math.gcd(tail, 128)


def pack_rest(live_rows, seglen, lens, routes, gap, adv, version, read, hidden, *rest):
    table, own, outs, held = rest[0], rest[1], rest[2:-1], rest[-1]
    dp, mp = my_place()
    seg, respond = gap.shape
    tokens = respond * seg
    chosen = live_tokens(live_rows, seglen, lens[...])
    chosen_f32 = chosen.astype(jnp.float32)
    select = chosen_f32.astype(jnp.bfloat16)
    units = hidden.shape[1] // len(outs)
    tail, fold = fold_of(live_rows)
    short = units // fold
    pieces = tail * fold // 128
    rows = packed_rows(units, live_rows)
    for block in range(0, len(outs), 2):
        turned = lax.dot_general(
            hidden[:, block * units:(block + 2) * units], select, (((0,), (1,)), ((), ())),
            preferred_element_type=jnp.float32,
        )
        for i in range(2):
            part = turned[i * units:(i + 1) * units]
            at = (block + i) * rows
            held[at:at + units] = part[:, :128].astype(jnp.bfloat16)
            wide = jnp.concatenate([part[j * short:(j + 1) * short, 128:] for j in range(fold)], axis=1)
            for j in range(pieces):
                start = at + units + j * short
                held[start:start + short] = wide[:, j * 128:(j + 1) * 128].astype(jnp.bfloat16)
    for k, out in enumerate(outs):
        out[...] = held[pl.ds(pl.multiple_of((dp ^ k) * rows, 16), rows)]

    wide = read.shape[1] // own.shape[0]
    for quarter in range(own.shape[0]):
        own[mp ^ quarter] = jnp.dot(
            select, read[:, quarter * wide:(quarter + 1) * wide], preferred_element_type=jnp.float32
        ).astype(jnp.bfloat16)

    expand = (iota((respond, tokens), 0) == lax.div(iota((respond, tokens), 1), seg)).astype(jnp.float32)
    eye = iota((respond, respond), 0) == iota((respond, respond), 1)
    dest_row = routes[...].astype(jnp.float32)
    dest_col = jnp.sum(jnp.where(eye, dest_row, 0.0), axis=1, keepdims=True)
    earlier = (dest_col == dest_row) & (iota((respond, respond), 0) < iota((respond, respond), 1))
    rank_row = jnp.sum(jnp.where(earlier, 1.0, 0.0), axis=0, keepdims=True)
    age = NVER - 1 - version[...]
    stale = jnp.ones(age.shape, jnp.float32)
    for years in range(1, NVER):
        stale = jnp.where(age == years, jnp.float32(np.float32(0.7) ** years), stale)
    by_token = jnp.dot(
        jnp.concatenate([rows_of(adv[...], stale, dest_row, rank_row), gap[...]], axis=0),
        expand, precision=EXACT, preferred_element_type=jnp.float32,
    )
    pos = lax.rem(iota((seg, tokens), 1), seg)
    gap_row = jnp.sum(jnp.where(pos == iota((seg, tokens), 0), by_token[8:], 0.0), axis=0, keepdims=True)
    table[...] = lax.dot_general(
        rows_of(gap_row, *(by_token[i:i + 1] for i in range(4)), pos[0:1].astype(jnp.float32)),
        chosen_f32, (((1,), (1,)), ((), ())), precision=EXACT, preferred_element_type=jnp.float32,
    )


def unpack_hidden(packed, units, live_rows):
    tail, fold = fold_of(live_rows)
    short = units // fold
    pieces = tail * fold // 128
    wide = jnp.concatenate(
        [packed[units + j * short:units + (j + 1) * short].astype(jnp.float32) for j in range(pieces)], axis=1
    )
    folded = jnp.concatenate([wide[:, j * tail:(j + 1) * tail] for j in range(fold)], axis=0)
    return packed[:units], folded.astype(jnp.bfloat16)


def fetch(pieces, refs, held, sems, slots):
    copies = {}
    live_rows = held.shape[1] // len(slots)
    for e in range(held.shape[0]):
        for i, k in enumerate(slots):
            ref, at = pieces[k, e]
            source = refs[ref].at[at] if ref == 0 else refs[ref].at[pl.ds(at * live_rows, live_rows)]
            copies[k, e] = pltpu.make_async_copy(source, held.at[e, pl.ds(i * live_rows, live_rows)], sems.at[i, e])
            copies[k, e].start()
    return copies


def shift_kernel(pieces, n_refs, slots, live_rows, weight, *rest):
    n = len(slots)
    hidden, refs, rest = rest[:n], rest[n:n + n_refs], rest[n + n_refs:]
    before, (sums, turned, held, rows_held, packed, sems, more_sems) = rest[:-7], rest[-7:]
    _, mp = my_place()
    quarters, wide = held.shape[0], held.shape[2]
    units = weight.shape[0]
    rows_copies = []
    for e in range(quarters):
        columns = pl.ds(pl.multiple_of((mp ^ e) * wide, 128), wide)
        rows_copies.append(pltpu.make_async_copy(weight.at[:, columns], rows_held.at[e], more_sems.at[e]))
        rows_copies[e].start()
    copies = fetch(pieces, refs, held, sems, slots)
    packed_copies = []
    for i in range(n):
        packed_copies.append(pltpu.make_async_copy(hidden[i], packed.at[i], more_sems.at[quarters + i]))
        packed_copies[i].start()
    product = jnp.zeros((units, n * live_rows), jnp.float32)
    for e in range(quarters):
        rows_copies[e].wait()
        for k in slots:
            copies[k, e].wait()
        product += lax.dot_general(
            rows_held[e], held[e], (((1,), (1,)), ((), ())), preferred_element_type=jnp.float32
        )
        if e == 1:
            for i in range(n):
                packed_copies[i].wait()
                head, tail = unpack_hidden(packed[i], units, live_rows)
                turned[:, i * live_rows:(i + 1) * live_rows] = jnp.concatenate([head, tail], axis=1)
    line = jnp.sum(product * turned[...].astype(jnp.float32), axis=0, keepdims=True)
    total = before[0][...] if before else jnp.zeros(sums.shape, jnp.float32)
    row = iota(total.shape, 0)
    for i, k in enumerate(slots):
        total = jnp.where(row == k, line[:, i * live_rows:(i + 1) * live_rows], total)
    sums[...] = total


def by_slot(notes, which):
    slots = 2 * len(notes)
    out = jnp.zeros((slots, notes[0].shape[1]), jnp.float32)
    row = iota(out.shape, 0)
    for k in range(slots):
        at = slots + 8 * (k % 2) + which
        out = jnp.where(row == k, notes[k // 2][at:at + 1, :], out)
    return out


def swap_rows(values, m):
    row = iota(values.shape, 0)
    out = jnp.zeros_like(values)
    for k in range(values.shape[0]):
        out = jnp.where(row == k, values[k ^ m:(k ^ m) + 1, :], out)
    return out


def grad_kernel(pieces, n_refs, groups, slots_each, seglen, *rest):
    order = sum(groups, ())
    shards = len(order)
    hidden, rest = rest[:len(groups)], rest[len(groups):]
    refs, rest = rest[:n_refs], rest[n_refs:]
    notes, rest = rest[:shards // 2], rest[shards // 2:]
    ratio_out, grad_out, held, turned, scaled, result, sems, out_sems = rest
    dp, mp = my_place()
    quarters, wide = held.shape[0], held.shape[2]
    live_rows = notes[0].shape[1]
    copies = fetch(pieces, refs, held, sems, order)
    scale = SCALE / math.sqrt(quarters * wide)
    at = 0
    for part in hidden:
        turned[:, at:at + part.shape[1]] = part[...]
        at += part.shape[1]

    total = notes[0][:shards]
    for i in range(1, len(notes)):
        total = total + swap_rows(notes[i][:shards], 2 * i)
    logit = by_slot(notes, GAP) + total * scale
    adv, dest = by_slot(notes, ADV), by_slot(notes, DEST)
    counts = jnp.zeros((shards, live_rows), jnp.float32)
    for shard in range(shards):
        here = dest == float(shard)
        tally = jnp.sum(jnp.sum(jnp.where(here, 1.0, 0.0), axis=1, keepdims=True), axis=0, keepdims=True)
        counts = jnp.where(here, tally, counts)
    ratio = jnp.exp(logit)
    squash = jnp.tanh((ratio - 1.0) / 0.2)
    clipped = 1.0 + 0.2 * squash
    slope = jnp.where(ratio * adv <= clipped * adv, 1.0, 1.0 - squash * squash)
    coef = -512.0 * by_slot(notes, STALE) * adv * ratio * slope / counts * scale

    eye = iota((live_rows, live_rows), 0) == iota((live_rows, live_rows), 1)
    columns = [jnp.sum(jnp.where(eye, coef[k:k + 1], 0.0), axis=1, keepdims=True) for k in order]
    writes = []
    for e in range(quarters):
        for i, k in enumerate(order):
            copies[k, e].wait()
            rows = slice(i * live_rows, (i + 1) * live_rows)
            scaled[rows] = (columns[i] * held[e, rows].astype(jnp.float32)).astype(jnp.bfloat16)
        result[e] = jnp.dot(turned[...], scaled[...], preferred_element_type=jnp.float32)
        write = pltpu.make_async_copy(
            result.at[e], grad_out.at[:, pl.ds(pl.multiple_of((mp ^ e) * wide, 128), wide)], out_sems.at[e]
        )
        write.start()
        writes.append(write)

    rank, pos = by_slot(notes, RANK), by_slot(notes, POS)
    spots = shards * slots_each
    spot = iota((spots, live_rows), 0).astype(jnp.float32)
    lane = iota((seglen, live_rows), 0).astype(jnp.float32)
    ratios = jnp.zeros((3 * seglen, spots), jnp.float32)
    for k in range(shards):
        to_me = dest[k:k + 1] == dp.astype(jnp.float32)
        target = ((dp ^ k) * slots_each).astype(jnp.float32) + rank[k:k + 1]
        left, spare = [], logit[k:k + 1]
        for _ in range(3):
            part = spare.astype(jnp.bfloat16).astype(jnp.float32)
            left.append(jnp.where(lane == pos[k:k + 1], part, 0.0))
            spare = spare - part
        ratios += lax.dot_general(
            jnp.concatenate(left, axis=0).astype(jnp.bfloat16),
            jnp.where((spot == target) & to_me, 1.0, 0.0).astype(jnp.bfloat16),
            (((1,), (1,)), ((), ())), preferred_element_type=jnp.float32,
        )
    ratio_out[...] = ratios[:seglen] + (ratios[seglen:2 * seglen] + ratios[2 * seglen:])
    for write in writes:
        write.wait()


MOVES = {
    "near": ("first", "dp", 2), "far": ("first", "dp", 6), "next": ("first", "dp", 4), "beside": ("both", "dp", 1),
    "x_n3": ("n3", "mp", 2), "y_n3": ("n3", "dp", 1), "xy_n3": ("y_n3", "mp", 2),
}
MOVES.update({f"h{k}": (f"pack{k}", "dp", k) for k in range(1, 8)})
HOLDS = {
    "beside": ((1, 0), (1, 2)), "n3": ((2, 0), (6, 0), (4, 0)), "y_n3": ((3, 0), (7, 0), (5, 0)),
    "x_n3": ((2, 2), (6, 2), (4, 2)), "xy_n3": ((3, 2), (7, 2), (5, 2)),
}
MOVES.update({"c_" + name: (name, "mp", 1) for name in HOLDS})
PLAN = (
    ("far", "next", "near", "beside", "rest", "h1",),
    ("x_n3", "y_n3", "h4", "h6", "c_beside", "c_n3",),
    ("xy_n3", "h7", "h5", "h3", "h2", "c_x_n3", "c_y_n3", "early",),
    ("c_xy_n3",),
)
BESIDES = {"early": ("h7",), "c_xy_n3": ("early",)}
EARLY = (0, 1, 2, 6, 4, )
LATE = (3, 7, 5, )


def cube_body(hidden_act, readout, log_gap, advantage, version, lengths, routes, weight):
    shards, quarters = lax.axis_size("dp"), lax.axis_size("mp")
    respond, seglen = log_gap.shape
    live_rows = 7 * respond * seglen // 8
    width = readout.shape[1]
    wide = width // quarters
    units = weight.shape[0]
    rows = packed_rows(units, live_rows)
    slots_each = 2 * respond // shards
    bf16, f32 = jnp.bfloat16, jnp.float32
    big = pltpu.CompilerParams(vmem_limit_bytes=56 * 1024 * 1024)

    def cost(flops, moved):
        return pl.CostEstimate(flops=int(flops), bytes_accessed=int(moved), transcendentals=0)

    def over_dp(x, m):
        return lax.ppermute(x, "dp", [(s, s ^ m) for s in range(shards)])

    def over_mp(x, m):
        return lax.ppermute(x, "mp", [(s, s ^ m) for s in range(quarters)])

    def over_both(x, m, h):
        pairs = [(s * quarters + t, (s ^ m) * quarters + (t ^ h)) for s in range(shards) for t in range(quarters)]
        return lax.ppermute(x, ("dp", "mp"), pairs)

    got = {}

    def after(x, names):
        names = [name for name in names if name in got]
        return lax.optimization_barrier((x, *(got[name] for name in names)))[0] if names else x

    got["first"], got["both"] = pl.pallas_call(
        functools.partial(pack_first, live_rows, seglen),
        out_shape=(jax.ShapeDtypeStruct((live_rows, wide), bf16), jax.ShapeDtypeStruct((2 * live_rows, wide), bf16)),
        in_specs=[VMEM, ANY],
        out_specs=(VMEM, VMEM),
        scratch_shapes=[pltpu.VMEM((2, respond * seglen, wide), bf16), pltpu.SemaphoreType.DMA((2,))],
        compiler_params=big,
        name="pack_first",
    )(lengths, readout)

    def rest(gates):
        table, own, *hidden = pl.pallas_call(
            functools.partial(pack_rest, live_rows, seglen),
            out_shape=(
                jax.ShapeDtypeStruct((8, live_rows), f32),
                jax.ShapeDtypeStruct((quarters, live_rows, wide), bf16),
            ) + (jax.ShapeDtypeStruct((rows, 128), bf16),) * shards,
            in_specs=[VMEM] * 7,
            out_specs=(VMEM,) * (shards + 2),
            scratch_shapes=[pltpu.VMEM((shards * rows, 128), bf16)],
            compiler_params=big,
            cost_estimate=cost(2e9, 8e6),
            name="pack_rest",
        )(after(lengths, gates), routes.reshape(1, respond), log_gap.T, advantage.reshape(1, respond),
          version.reshape(1, respond), readout, hidden_act)
        got.update({"table": table, "own": own, "h0": hidden[0], "rest": table})
        got.update({f"pack{k}": hidden[k] for k in range(1, shards)})

    def used(slots):
        names, places = ["own"], {(0, e): (0, e) for e in range(quarters)}
        for name, blocks in HOLDS.items():
            for core in (0, 1):
                if any(k in slots for k, _ in blocks):
                    for block, (k, e) in enumerate(blocks):
                        places[k, e ^ core] = (len(names), block)
                    names.append("c_" + name if core else name)
        return [got[name] for name in names], places

    groups = (EARLY, LATE) if EARLY else (LATE,)
    turned = []

    def shift_sums(slots, *before, gates=()):
        refs, places = used(slots)
        refs[0] = after(refs[0], gates)
        sums, part = pl.pallas_call(
            functools.partial(shift_kernel, places, len(refs), slots, live_rows),
            out_shape=(
                jax.ShapeDtypeStruct((shards, live_rows), f32),
                jax.ShapeDtypeStruct((units, len(slots) * live_rows), bf16),
            ),
            in_specs=[ANY] * (1 + len(slots) + len(refs)) + [VMEM] * len(before),
            out_specs=(VMEM, VMEM),
            scratch_shapes=[
                pltpu.VMEM((quarters, len(slots) * live_rows, wide), bf16),
                pltpu.VMEM((quarters, units, wide), bf16),
                pltpu.VMEM((len(slots), rows, 128), bf16),
                pltpu.SemaphoreType.DMA((len(slots), quarters)),
                pltpu.SemaphoreType.DMA((quarters + len(slots),)),
            ],
            compiler_params=big,
            cost_estimate=cost(2 * units * len(slots) * live_rows * width, 2 * len(slots) * live_rows * width),
            name="shift_sums",
        )(weight, *(got[f"h{k}"] for k in slots), *refs, *before)
        turned.append(part)
        return sums

    gates = ()
    for steps in PLAN:
        moved = []
        for step in steps:
            if step == "rest":
                rest(gates)
                moved.append(step)
            elif step == "early":
                got[step] = shift_sums(EARLY, gates=BESIDES.get(step, ()))
            else:
                source, axis, m = MOVES[step]
                if source == "n3" and source not in got:
                    got[source] = jnp.concatenate([got["near"], got["far"], got["next"]], axis=0)
                core = [name for name in moved if name[:2] == "c_" and step[:2] == "c_"]
                got[step] = (over_dp if axis == "dp" else over_mp)(
                    after(got[source], (*gates, *core, *BESIDES.get(step, ()))), m
                )
                moved.append(step)
        gates = tuple(moved)
    sums = shift_sums(LATE, *([got["early"]] if EARLY else []))

    sums = sums + over_mp(sums, 1)
    table = got["table"]
    beside = over_dp(jnp.concatenate([sums, table], axis=0), 1)
    across = beside[:shards] + over_both(sums, 1, 2)
    sums = sums + over_mp(sums, 2)
    note = jnp.concatenate(
        [sums + jnp.concatenate([across[k ^ 1:(k ^ 1) + 1] for k in range(shards)], axis=0), table, beside[shards:]], axis=0
    )
    notes = [note] + [over_dp(note, m) for m in (2, 4, 6)]

    order = sum(groups, ())
    refs, places = used(order)
    log_ratio, weight_grad = pl.pallas_call(
        functools.partial(grad_kernel, places, len(refs), groups, slots_each, seglen),
        out_shape=(
            jax.ShapeDtypeStruct((seglen, shards * slots_each), f32),
            jax.ShapeDtypeStruct((units, width), f32),
        ),
        in_specs=[VMEM] * len(groups) + [ANY] * len(refs) + [VMEM] * len(notes),
        out_specs=(VMEM, ANY),
        scratch_shapes=[
            pltpu.VMEM((quarters, shards * live_rows, wide), bf16),
            pltpu.VMEM((units, shards * live_rows), bf16),
            pltpu.VMEM((shards * live_rows, wide), bf16),
            pltpu.VMEM((quarters, units, wide), f32),
            pltpu.SemaphoreType.DMA((shards, quarters)),
            pltpu.SemaphoreType.DMA((quarters,)),
        ],
        compiler_params=big,
        cost_estimate=cost(2 * units * shards * live_rows * width, 2 * shards * live_rows * width + 4 * units * width),
        name="weight_grad",
    )(*turned, *refs, *notes)
    return (log_ratio.T, weight_grad)


def general_body(hidden_act, readout, log_gap, advantage, version, lengths, routes, weight):
    shards = lax.axis_size("dp")
    respond, seglen = log_gap.shape
    tokens = respond * seglen
    live_rows = 7 * tokens // 8
    width = readout.shape[1]
    units = weight.shape[0]
    slots = 2 * respond // shards
    scale = SCALE / math.sqrt(width)
    f32 = jnp.float32
    dest = routes[:, 0]
    onehot = (dest[:, None] == jnp.arange(shards, dtype=jnp.int32)[None, :]).astype(jnp.int32)
    rank = jnp.sum((jnp.cumsum(onehot, axis=0) - onehot) * onehot, axis=1)
    lens = lengths[0]
    live = (jnp.arange(seglen, dtype=jnp.int32)[None, :] < lens[:, None]).reshape(-1)
    order = jnp.cumsum(live.astype(jnp.int32)) - 1
    select = live[None, :] & (order[None, :] == jnp.arange(live_rows, dtype=jnp.int32)[:, None])
    hidden = jnp.dot(select.astype(jnp.bfloat16), hidden_act)
    hidden = lax.all_to_all(
        hidden.reshape(live_rows, shards, units).swapaxes(0, 1), "dp", split_axis=0, concat_axis=0
    )
    read = lax.all_gather(jnp.dot(select.astype(jnp.bfloat16), readout), "dp", axis=0)

    def one_sum(k, sums):
        product = lax.dot_general(read[k], weight, (((1,), (1,)), ((), ())), preferred_element_type=f32)
        return sums.at[k].set(jnp.sum(product * hidden[k].astype(f32), axis=1))

    sums = lax.fori_loop(0, shards, one_sum, jnp.zeros((shards, live_rows), f32))
    sums = lax.psum(lax.psum_scatter(sums, "dp", scatter_dimension=0, tiled=True)[0], "mp")
    shift = jnp.dot(sums[None, :], select.astype(f32), precision=EXACT).reshape(respond, seglen) * scale
    logit = log_gap + shift
    live = live.reshape(respond, seglen)
    onehot_float = onehot.astype(f32)
    shard_count = lax.psum(jnp.sum(onehot_float * lens.astype(f32)[:, None], axis=0), "dp")
    count_each = jnp.sum(onehot_float * shard_count[None, :], axis=1)
    stale = jnp.power(jnp.float32(0.7), (NVER - 1 - version).astype(f32))
    send = jnp.arange(shards * slots, dtype=jnp.int32)[:, None] == (dest * slots + rank)[None, :]
    log_ratio = lax.all_to_all(
        jnp.dot(send.astype(f32), jnp.where(live, logit, 0.0), precision=EXACT),
        "dp", split_axis=0, concat_axis=0, tiled=True,
    )
    ratio = jnp.exp(logit)
    squash = jnp.tanh((ratio - 1.0) / 0.2)
    clipped = 1.0 + 0.2 * squash
    adv = advantage[:, None]
    slope = jnp.where(ratio * adv <= clipped * adv, 1.0, 1.0 - squash * squash)
    coef = jnp.where(live, -512.0 * stale[:, None] * adv * ratio * slope / count_each[:, None], 0.0)
    coef = jnp.dot(select.astype(f32), coef.reshape(-1, 1), precision=EXACT)[:, 0]
    coefs = lax.all_gather(coef, "dp", axis=0)

    def one_term(k, grad):
        out_grad = (coefs[k][:, None] * scale * read[k].astype(f32)).astype(jnp.bfloat16)
        return grad + lax.dot_general(
            hidden[k], out_grad, (((0,), (0,)), ((), ())), preferred_element_type=f32
        )

    return (log_ratio, lax.fori_loop(0, shards, one_term, jnp.zeros((units, width), f32)))


def body(*args):
    if lax.axis_size("dp") == 8 and lax.axis_size("mp") == 4:
        return cube_body(*args)
    return general_body(*args)


def solution(mesh):
    placed = (
        P("dp", "mp"),
        P("dp", None),
        P("dp", None),
        P("dp"),
        P("dp"),
        P("dp", None),
        P("dp", None),
        P(("mp", "dp"), None),
    )
    return jax.shard_map(
        body,
        mesh=mesh,
        in_specs=placed,
        out_specs=(P("dp", None), P(("mp", "dp"), None)),
        check_vma=False,
    )
```

time: 1030 us -> 124 us (0.12)
  waiting for transfers between devices: 886 us -> 44.1 us
  blocking collectives: 62.1 us -> 0 us
  starting transfers between devices: 0.08 us -> 39.1 us
  local copies, waits for them, and re-layouts: 39.4 us -> 2.43 us
  Pallas kernels: 0 us -> 36.5 us
  matrix products: 24.2 us -> 0 us
  between operations: 14.1 us -> 1.1 us
    unnamed x3 -> x0, waiting for transfers between devices: 577 us -> none
    all_gather x1 -> x0, waiting for transfers between devices: 310 us -> none  [token_shift(): lax.all_gather(weight, 'dp', axis=0, tiled=True)]
    psum x2 -> x0, blocking collectives: 50.7 us -> none  [the longest x1 43.8 us: body(): shard_count = lax.psum(histogram, 'dp')]
    ppermute x0 -> x26, waiting for transfers between devices: none -> 44.1 us  [the longest x16 36.5 us: over_dp(): return lax.ppermute(x, 'dp', [(s, s ^ m) for s in range(shards)])]
    ppermute x0 -> x26, starting transfers between devices: none -> 39.1 us  [the longest x16 33.8 us: over_dp(): return lax.ppermute(x, 'dp', [(s, s ^ m) for s in range(shards)])]
    pallas_call x0 -> x5, Pallas kernels: none -> 36.5 us  [the longest x2 15 us: shift_sums(): pl.pallas_call(functools.partial(shift_kernel, places, len(refs), slots,...]
    unnamed x14 -> x44, local copies, waits for them, and re-layouts: 38.4 us -> 2.36 us
    dot_general x3 -> x0, matrix products: 24.2 us -> none  [the longest x1 14.4 us: weight_terms(): lax.dot_general(rows_act, out_grad, (((0,), (0,)), ((), ())), preferred_e...]
  transfers between devices with their start and end apart: 2 -> 26, of which waited for: 2 -> 12; matrix products, arithmetic and copies ran while one was open for 0% -> 0% of each run, Pallas kernels for 0% -> 11%
where the time goes in v2:
time: 124 us
  waiting for transfers between devices  44.1 us (36%)
  starting transfers between devices  39.1 us (32%)
  Pallas kernels  36.5 us (29%)
  local copies, waits for them, and re-layouts  2.43 us (2%)
    ppermute x16, waiting for transfers between devices, over_dp(): return lax.ppermute(x, 'dp', [(s, s ^ m) for s in range(shards)])  36.5 us
    ppermute x16, starting transfers between devices, over_dp(): return lax.ppermute(x, 'dp', [(s, s ^ m) for s in range(shards)])  33.8 us
    pallas_call x2, Pallas kernels, shift_sums(): pl.pallas_call(functools.partial(shift_kernel, places, len(refs), slots,...  15 us
    pallas_call x1, Pallas kernels, cube_body(): pl.pallas_call(functools.partial(grad_kernel, places, len(refs), groups,...  13.5 us
    ppermute x9, waiting for transfers between devices, over_mp(): return lax.ppermute(x, 'mp', [(s, s ^ m) for s in range(quarters)])  5.11 us
    pallas_call x1, Pallas kernels, rest(): pl.pallas_call(functools.partial(pack_rest, live_rows, seglen), out_shape...  4.91 us
    ppermute x9, starting transfers between devices, over_mp(): return lax.ppermute(x, 'mp', [(s, s ^ m) for s in range(quarters)])  3.91 us
    pallas_call x1, Pallas kernels, cube_body(): pl.pallas_call(functools.partial(pack_first, live_rows, seglen), out_shap...  3.02 us
  transfers between devices with their start and end apart: 26, of which 12 were waited for; matrix products, arithmetic and copies ran while one was open for 0% of the time, Pallas kernels for 11%

profile of v2, /device:TPU:0, one launch (start us, length us, event | category | flops | bytes accessed | tf_op | source)
XLA Modules:
  0.0 123.9 jit_solution(11271720621867644127)
XLA Ops:
  0.6 3.0 %pack_first.1 = (bf16[224,640]{1,0:T(8,128)(2,1)}, bf16[448,640]{1,0:T(8,128)(2,1)}) custom-call(s32[1,32]{1,0:T(1,128)} %lens.3, bf16[256,2560]{1,0:T(8,128)(2,1)} %read.3), custom_call_target="tpu_custom_call" | custom-call | tf_op jit(solution)/shard_map/pack_first/pallas_call | solution.py:336
  3.7 3.0 %collective-permute-start.4 = (bf16[448,640]{1,0:T(8,128)(2,1)}, bf16[448,640]{1,0:T(8,128)(2,1)S(1)}, u32[]{:S(2)}, u32[]{:S(2)}) collective-permute-start(bf16[448,640]{1,0:T(8,128)(2,1)} %get-tuple-element.38), channel_id=1, source_target_pairs={{0,4},{4,0},{8,12},{12,8},{16,20},{20,16},{24,28},{28,24},{1,5},{5... | collective-permute-start | bytes 1720328 | tf_op jit(solution)/shard_map/ppermute | solution.py:321
  6.7 2.6 %collective-permute-start.3 = (bf16[224,640]{1,0:T(8,128)(2,1)}, bf16[224,640]{1,0:T(8,128)(2,1)S(1)}, u32[]{:S(2)}, u32[]{:S(2)}) collective-permute-start(bf16[224,640]{1,0:T(8,128)(2,1)} %get-tuple-element.37), channel_id=1, source_target_pairs={{0,16},{4,20},{8,24},{12,28},{16,0},{20,4},{24,8},{28,12},{1,17},{... | collective-permute-start | bytes 860168 | tf_op jit(solution)/shard_map/ppermute | solution.py:321
  9.3 1.3 %collective-permute-start.2 = (bf16[224,640]{1,0:T(8,128)(2,1)}, bf16[224,640]{1,0:T(8,128)(2,1)S(1)}, u32[]{:S(2)}, u32[]{:S(2)}) collective-permute-start(bf16[224,640]{1,0:T(8,128)(2,1)} %get-tuple-element.37), channel_id=1, source_target_pairs={{0,24},{4,28},{8,16},{12,20},{16,8},{20,12},{24,0},{28,4},{1,25},{... | collective-permute-start | bytes 860168 | tf_op jit(solution)/shard_map/ppermute | solution.py:321
  10.6 0.2 collective-permute-start.1
  10.9 4.9 %pack_rest.1 = (f32[8,224]{1,0:T(8,128)}, bf16[4,224,640]{2,1,0:T(8,128)(2,1)}, bf16[784,128]{1,0:T(8,128)(2,1)}, bf16[784,128]{1,0:T(8,128)(2,1)}, bf16[784,128...) custom-call(s32[1,32]{1,0:T(1,128)} %lens.3, ...), custom_call_target="tpu_custom_call" | custom-call | flops 2000000000 | bytes 8000000 | tf_op jit(solution)/shard_map/pack_rest/pallas_call | solution.py:347
  15.8 0.6 collective-permute-start
  16.3 7.8 %collective-permute-done.rest_1_ = bf16[784,128]{1,0:T(8,128)(2,1)S(1)} collective-permute-done((bf16[784,128]{1,0:T(8,128)(2,1)}, bf16[784,128]{1,0:T(8,128)(2,1)S(1)}, u32[]{:S(2)}, u32[]{:S(2)}) %collective-permute-start) | collective-permute-done | bytes 200736 | tf_op jit(solution)/shard_map/ppermute | solution.py:321
  24.2 5.4 %collective-permute-done.3 = bf16[224,640]{1,0:T(8,128)(2,1)S(1)} collective-permute-done((bf16[224,640]{1,0:T(8,128)(2,1)}, bf16[224,640]{1,0:T(8,128)(2,1)S(1)}, u32[]{:S(2)}, u32[]{:S(2)}) %collective-permute-start.3) | collective-permute-done | bytes 286752 | tf_op jit(solution)/shard_map/ppermute | solution.py:321
  29.6 0.0 collective-permute-done.2
  29.6 0.1 collective-permute-done.1
  29.7 0.0 collective-permute-done.4.rest_6_.rest_3_
  29.8 0.0 collective-permute-start.9
  29.9 0.5 collective-permute-start.6
  30.4 1.6 %collective-permute-start.5 = (bf16[672,640]{1,0:T(8,128)(2,1)S(1)}, bf16[672,640]{1,0:T(8,128)(2,1)S(1)}, u32[]{:S(2)}, u32[]{:S(2)}) collective-permute-start(bf16[672,640]{1,0:T(8,128)(2,1)S(1)} %constant_dynamic-update-slice_fusion.rest_8_.rest_5_), channel_id=1, source_target_pairs={{0,2},{1,3},{2,0},{3,1},{4,6},{5,7},{6,4},{7,5},{8,10},{9,11},{10,... | collective-permute-start | bytes 2580488 | tf_op jit(solution)/shard_map/ppermute | solution.py:324
  32.0 0.0 collective-permute-done.9.rest_7_.rest_4_
  32.0 0.0 collective-permute-start.10
  32.0 7.6 %collective-permute-start.7 = (bf16[784,128]{1,0:T(8,128)(2,1)}, bf16[784,128]{1,0:T(8,128)(2,1)S(1)}, u32[]{:S(2)}, u32[]{:S(2)}) collective-permute-start(bf16[784,128]{1,0:T(8,128)(2,1)} %get-tuple-element.42), channel_id=1, source_target_pairs={{0,16},{4,20},{8,24},{12,28},{16,0},{20,4},{24,8},{28,12},{1,17},{... | collective-permute-start | bytes 602120 | tf_op jit(solution)/shard_map/ppermute | solution.py:321
  39.5 0.5 collective-permute-start.8
  40.1 14.1 %collective-permute-done.7.rest_4_ = bf16[784,128]{1,0:T(8,128)(2,1)S(1)} collective-permute-done((bf16[784,128]{1,0:T(8,128)(2,1)}, bf16[784,128]{1,0:T(8,128)(2,1)S(1)}, u32[]{:S(2)}, u32[]{:S(2)}) %collective-permute-start.7) | collective-permute-done | bytes 200736 | tf_op jit(solution)/shard_map/ppermute | solution.py:321
  54.2 0.0 collective-permute-done.8.rest_3_
  54.2 0.0 collective-permute-done.6.rest_4_.rest_7_
  54.2 0.0 copy-start
  54.2 0.0 collective-permute-done.5.rest_10_.rest_9_
  54.2 0.7 copy-done.17
  54.9 0.0 collective-permute-done.10.rest_9_.rest_6_
  54.9 0.0 collective-permute-start.13
  54.9 1.4 %collective-permute-start.17 = (bf16[672,640]{1,0:T(8,128)(2,1)S(1)}, bf16[672,640]{1,0:T(8,128)(2,1)S(1)}, u32[]{:S(2)}, u32[]{:S(2)}) collective-permute-start(bf16[672,640]{1,0:T(8,128)(2,1)S(1)} %collective-permute-done.6.rest_4_.rest_7_), channel_id=1, source_target_pairs={{0,2},{1,3},{2,0},{3,1},{4,6},{5,7},{6,4},{7,5},{8,10},{9,11},{10,... | collective-permute-start | bytes 2580488 | tf_op jit(solution)/shard_map/ppermute | solution.py:324
  56.3 1.0 collective-permute-done.13.rest_11_.rest_10_
  57.3 0.1 collective-permute-start.16
  57.4 1.5 %collective-permute-start.12 = (bf16[784,128]{1,0:T(8,128)(2,1)}, bf16[784,128]{1,0:T(8,128)(2,1)S(1)}, u32[]{:S(2)}, u32[]{:S(2)}) collective-permute-start(bf16[784,128]{1,0:T(8,128)(2,1)} %get-tuple-element.50), channel_id=1, source_target_pairs={{0,28},{4,24},{8,20},{12,16},{16,12},{20,8},{24,4},{28,0},{1,29},{... | collective-permute-start | bytes 602120 | tf_op jit(solution)/shard_map/ppermute | solution.py:321
  59.0 4.4 %collective-permute-start.11 = (bf16[784,128]{1,0:T(8,128)(2,1)}, bf16[784,128]{1,0:T(8,128)(2,1)}, u32[]{:S(2)}, u32[]{:S(2)}) collective-permute-start(bf16[784,128]{1,0:T(8,128)(2,1)} %get-tuple-element.47), channel_id=1, source_target_pairs={{0,8},{4,12},{8,0},{12,4},{16,24},{20,28},{24,16},{28,20},{1,9},{5... | collective-permute-start | bytes 602120 | tf_op jit(solution)/shard_map/ppermute | solution.py:321
  63.3 0.0 collective-permute-start.14
  63.3 4.8 %collective-permute-done.12.rest_1_ = bf16[784,128]{1,0:T(8,128)(2,1)S(1)} collective-permute-done((bf16[784,128]{1,0:T(8,128)(2,1)}, bf16[784,128]{1,0:T(8,128)(2,1)S(1)}, u32[]{:S(2)}, u32[]{:S(2)}) %collective-permute-start.12) | collective-permute-done | bytes 200736 | tf_op jit(solution)/shard_map/ppermute | solution.py:321
  68.2 4.4 %collective-permute-start.15 = (bf16[784,128]{1,0:T(8,128)(2,1)}, bf16[784,128]{1,0:T(8,128)(2,1)S(1)}, u32[]{:S(2)}, u32[]{:S(2)}) collective-permute-start(bf16[784,128]{1,0:T(8,128)(2,1)} %get-tuple-element.57), channel_id=1, source_target_pairs={{0,20},{4,16},{8,28},{12,24},{16,4},{20,0},{24,12},{28,8},{1,21},{... | collective-permute-start | bytes 602120 | tf_op jit(solution)/shard_map/ppermute | solution.py:321
  72.6 0.0 collective-permute-done.11.rest_2_
  72.7 8.2 %shift_sums.2 = (f32[8,224]{1,0:T(8,128)}, bf16[448,1120]{1,0:T(8,128)(2,1)}) custom-call(bf16[448,2560]{1,0:T(8,128)(2,1)} %weight.3, bf16[784,128]{1,0:T(8,128)(2,1)} %get-tuple-element.34.rest_0_, bf16[784,128]{1,0:T(8,128)(2,1)} %copy-done.15, bf16[784,128]{1,0:T(8,128)(2,1)} %collective-permute-done.11.rest_2_, bf16[784,128]{1,0:T(8,128)(2,1)} %copy-done.17, ...), custom_call_target="tpu_custom_call" | custom-call | flops 2569011200 | bytes 5734400 | tf_op jit(solution)/shard_map/shift_sums/pallas_call | solution.py:380
  80.9 0.0 collective-permute-done.14.rest_0_
  80.9 0.0 copy-start.5
  80.9 0.0 collective-permute-done.15.rest_2_
  81.0 0.0 collective-permute-done.17.rest_6_.rest_11_
  81.0 0.0 collective-permute-done.16.rest_5_.rest_8_
  81.0 0.1 collective-permute-start.18
  81.1 2.4 %collective-permute-done.18.rest_7_.rest_12_ = bf16[672,640]{1,0:T(8,128)(2,1)S(1)} collective-permute-done((bf16[672,640]{1,0:T(8,128)(2,1)S(1)}, bf16[672,640]{1,0:T(8,128)(2,1)S(1)}, u32[]{:S(2)}, u32[]{:S(2)}) %collective-permute-start.18) | collective-permute-done | bytes 860192 | tf_op jit(solution)/shard_map/ppermute | solution.py:324
  83.5 0.9 copy-done.3
  84.4 6.8 %shift_sums.3 = (f32[8,224]{1,0:T(8,128)}, bf16[448,672]{1,0:T(8,128)(2,1)}) custom-call(bf16[448,2560]{1,0:T(8,128)(2,1)} %weight.3, bf16[784,128]{1,0:T(8,128)(2,1)} %copy-done.5, bf16[784,128]{1,0:T(8,128)(2,1)} %copy-done.4, bf16[784,128]{1,0:T(8,128)(2,1)} %copy-done.6, bf16[4,224,640]{2,1,0:T(8,128)(2,1)} %get-tuple-element.51.rest_5_.rest_3_.rest_2_, ...), custom_call_target="tpu_custom_call" | custom-call | flops 1541406720 | bytes 3440640 | tf_op jit(solution)/shard_map/shift_sums/pallas_call | solution.py:380
  91.2 0.2 collective-permute-start.19
  91.4 1.3 %collective-permute-done.19 = f32[8,224]{1,0:T(8,128)S(1)} collective-permute-done((f32[8,224]{1,0:T(8,128)}, f32[8,224]{1,0:T(8,128)S(1)}, u32[]{:S(2)}, u32[]{:S(2)}) %collective-permute-start.19) | collective-permute-done | bytes 7200 | tf_op jit(solution)/shard_map/ppermute | solution.py:324
  92.7 0.7 add.12
  93.4 1.6 %collective-permute-start.21 = (f32[16,224]{1,0:T(8,128)S(1)}, f32[16,224]{1,0:T(8,128)S(1)}, u32[]{:S(2)}, u32[]{:S(2)}) collective-permute-start(f32[16,224]{1,0:T(8,128)S(1)} %pad_maximum_fusion.1), channel_id=1, source_target_pairs={{0,4},{4,0},{8,12},{12,8},{16,20},{20,16},{24,28},{28,24},{1,5},{5... | collective-permute-start | bytes 43016 | tf_op jit(solution)/shard_map/ppermute | solution.py:321
  95.0 1.4 %collective-permute-start.22 = (f32[8,224]{1,0:T(8,128)S(1)}, f32[8,224]{1,0:T(8,128)S(1)}, u32[]{:S(2)}, u32[]{:S(2)}) collective-permute-start(f32[8,224]{1,0:T(8,128)S(1)} %add.12), channel_id=1, source_target_pairs={{0,6},{1,7},{2,4},{3,5},{4,2},{5,3},{6,0},{7,1},{8,14},{9,15},{10,... | collective-permute-start | bytes 21512 | tf_op jit(solution)/shard_map/ppermute | solution.py:328
  96.4 0.6 collective-permute-start.20
  97.0 2.6 %collective-permute-done.22 = f32[8,224]{1,0:T(8,128)S(1)} collective-permute-done((f32[8,224]{1,0:T(8,128)S(1)}, f32[8,224]{1,0:T(8,128)S(1)}, u32[]{:S(2)}, u32[]{:S(2)}) %collective-permute-start.22) | collective-permute-done | bytes 7200 | tf_op jit(solution)/shard_map/ppermute | solution.py:328
  99.5 0.0 collective-permute-done.21
  99.6 0.5 collective-permute-done.20
  100.1 4.8 %collective-permute-start.25 = (f32[24,224]{1,0:T(8,128)S(1)}, f32[24,224]{1,0:T(8,128)S(1)}, u32[]{:S(2)}, u32[]{:S(2)}) collective-permute-start(f32[24,224]{1,0:T(8,128)S(1)} %pad_maximum_fusion.rest_13_), channel_id=1, source_target_pairs={{0,24},{4,28},{8,16},{12,20},{16,8},{20,12},{24,0},{28,4},{1,25},{... | collective-permute-start | bytes 64520 | tf_op jit(solution)/shard_map/ppermute | solution.py:321
  104.9 0.0 collective-permute-start.24
  104.9 0.6 collective-permute-start.23
  105.5 1.2 collective-permute-done.25.rest_16_
  106.7 2.9 %collective-permute-done.24.rest_15_ = f32[24,224]{1,0:T(8,128)S(1)} collective-permute-done((f32[24,224]{1,0:T(8,128)S(1)}, f32[24,224]{1,0:T(8,128)S(1)}, u32[]{:S(2)}, u32[]{:S(2)}) %collective-permute-start.24) | collective-permute-done | bytes 21536 | tf_op jit(solution)/shard_map/ppermute | solution.py:321
  109.6 0.0 collective-permute-done.23.rest_14_
  109.7 0.6 copy-done.19
  110.2 0.0 copy-done.20
  110.2 13.5 %weight_grad.1 = (f32[8,64]{1,0:T(8,128)}, f32[448,2560]{1,0:T(8,128)}) custom-call(bf16[448,1120]{1,0:T(8,128)(2,1)} %get-tuple-element.53.rest_0_, bf16[448,672]{1,0:T(8,128)(2,1)} %get-tuple-element.62.rest_1_, bf16[4,224,640]{2,1,0:T(8,128)(2,1)} %get-tuple-element.51.rest_5_.rest_3_.rest_2_, bf16[448,640]{1,0:T(8,128)(2,1)} %copy-done.13, ...), custom_call_target="tpu_custom_call" | custom-call | flops 4110417920 | bytes 13762560 | tf_op jit(solution)/shard_map/weight_grad/pallas_call | solution.py:435
  (45 shorter events, 0.2 us)
Async XLA Ops:
  3.7 26.1 %collective-permute-start.4 = (bf16[448,640]{1,0:T(8,128)(2,1)}, bf16[448,640]{1,0:T(8,128)(2,1)S(1)}, u32[]{:S(2)}, u32[]{:S(2)}) collective-permute-start(bf16[448,640]{1,0:T(8,128)(2,1)} %get-tuple-element.38), channel_id=1, source_target_pairs={{0,4},{4,0},{8,12},{12,8},{16,20},{20,16},{24,28},{28,24},{1,5},{5... | collective-permute-start | bytes 1720328 | tf_op jit(solution)/shard_map/ppermute | solution.py:321
  6.7 22.9 %collective-permute-start.3 = (bf16[224,640]{1,0:T(8,128)(2,1)}, bf16[224,640]{1,0:T(8,128)(2,1)S(1)}, u32[]{:S(2)}, u32[]{:S(2)}) collective-permute-start(bf16[224,640]{1,0:T(8,128)(2,1)} %get-tuple-element.37), channel_id=1, source_target_pairs={{0,16},{4,20},{8,24},{12,28},{16,0},{20,4},{24,8},{28,12},{1,17},{... | collective-permute-start | bytes 860168 | tf_op jit(solution)/shard_map/ppermute | solution.py:321
  9.3 20.3 %collective-permute-start.2 = (bf16[224,640]{1,0:T(8,128)(2,1)}, bf16[224,640]{1,0:T(8,128)(2,1)S(1)}, u32[]{:S(2)}, u32[]{:S(2)}) collective-permute-start(bf16[224,640]{1,0:T(8,128)(2,1)} %get-tuple-element.37), channel_id=1, source_target_pairs={{0,24},{4,28},{8,16},{12,20},{16,8},{20,12},{24,0},{28,4},{1,25},{... | collective-permute-start | bytes 860168 | tf_op jit(solution)/shard_map/ppermute | solution.py:321
  10.6 19.1 %collective-permute-start.1 = (bf16[224,640]{1,0:T(8,128)(2,1)}, bf16[224,640]{1,0:T(8,128)(2,1)S(1)}, u32[]{:S(2)}, u32[]{:S(2)}) collective-permute-start(bf16[224,640]{1,0:T(8,128)(2,1)} %get-tuple-element.37), channel_id=1, source_target_pairs={{0,8},{4,12},{8,0},{12,4},{16,24},{20,28},{24,16},{28,20},{1,9},{5... | collective-permute-start | bytes 860168 | tf_op jit(solution)/shard_map/ppermute | solution.py:321
  15.8 8.4 %collective-permute-start = (bf16[784,128]{1,0:T(8,128)(2,1)}, bf16[784,128]{1,0:T(8,128)(2,1)S(1)}, u32[]{:S(2)}, u32[]{:S(2)}) collective-permute-start(bf16[784,128]{1,0:T(8,128)(2,1)} %get-tuple-element.35), channel_id=1, source_target_pairs={{0,4},{4,0},{8,12},{12,8},{16,20},{20,16},{24,28},{28,24},{1,5},{5... | collective-permute-start | bytes 602120 | tf_op jit(solution)/shard_map/ppermute | solution.py:321
  24.2 48.4 %copy-start.15 = (bf16[784,128]{1,0:T(8,128)(2,1)}, bf16[784,128]{1,0:T(8,128)(2,1)S(1)}, u32[]{:S(2)}) copy-start(bf16[784,128]{1,0:T(8,128)(2,1)S(1)} %collective-permute-done.rest_1_) | copy-start | bytes 602116
  29.7 42.9 %copy-start.13 = (bf16[448,640]{1,0:T(8,128)(2,1)}, bf16[448,640]{1,0:T(8,128)(2,1)S(1)}, u32[]{:S(2)}) copy-start(bf16[448,640]{1,0:T(8,128)(2,1)S(1)} %collective-permute-done.4.rest_6_.rest_3_) | copy-start | bytes 1720324
  29.8 2.2 %collective-permute-start.9 = (bf16[448,640]{1,0:T(8,128)(2,1)S(1)}, bf16[448,640]{1,0:T(8,128)(2,1)S(1)}, u32[]{:S(2)}, u32[]{:S(2)}) collective-permute-start(bf16[448,640]{1,0:T(8,128)(2,1)S(1)} %collective-permute-done.4.rest_6_.rest_3_), channel_id=1, source_target_pairs={{0,1},{1,0},{2,3},{3,2},{4,5},{5,4},{6,7},{7,6},{8,9},{9,8},{10,11... | collective-permute-start | bytes 1720328 | tf_op jit(solution)/shard_map/ppermute | solution.py:324
  29.9 42.7 %copy-start.7 = (bf16[672,640]{1,0:T(8,128)(2,1)}, bf16[672,640]{1,0:T(8,128)(2,1)S(1)}, u32[]{:S(2)}) copy-start(bf16[672,640]{1,0:T(8,128)(2,1)S(1)} %constant_dynamic-update-slice_fusion.rest_8_.rest_5_) | copy-start | bytes 2580484
  29.9 24.3 %collective-permute-start.6 = (bf16[672,640]{1,0:T(8,128)(2,1)S(1)}, bf16[672,640]{1,0:T(8,128)(2,1)S(1)}, u32[]{:S(2)}, u32[]{:S(2)}) collective-permute-start(bf16[672,640]{1,0:T(8,128)(2,1)S(1)} %constant_dynamic-update-slice_fusion.rest_8_.rest_5_), channel_id=1, source_target_pairs={{0,4},{4,0},{8,12},{12,8},{16,20},{20,16},{24,28},{28,24},{1,5},{5... | collective-permute-start | bytes 2580488 | tf_op jit(solution)/shard_map/ppermute | solution.py:321
  30.4 23.8 %collective-permute-start.5 = (bf16[672,640]{1,0:T(8,128)(2,1)S(1)}, bf16[672,640]{1,0:T(8,128)(2,1)S(1)}, u32[]{:S(2)}, u32[]{:S(2)}) collective-permute-start(bf16[672,640]{1,0:T(8,128)(2,1)S(1)} %constant_dynamic-update-slice_fusion.rest_8_.rest_5_), channel_id=1, source_target_pairs={{0,2},{1,3},{2,0},{3,1},{4,6},{5,7},{6,4},{7,5},{8,10},{9,11},{10,... | collective-permute-start | bytes 2580488 | tf_op jit(solution)/shard_map/ppermute | solution.py:324
  32.0 40.7 %copy-start.14 = (bf16[448,640]{1,0:T(8,128)(2,1)}, bf16[448,640]{1,0:T(8,128)(2,1)S(1)}, u32[]{:S(2)}) copy-start(bf16[448,640]{1,0:T(8,128)(2,1)S(1)} %collective-permute-done.9.rest_7_.rest_4_) | copy-start | bytes 1720324
  32.0 22.9 %collective-permute-start.10 = (bf16[672,640]{1,0:T(8,128)(2,1)S(1)}, bf16[672,640]{1,0:T(8,128)(2,1)S(1)}, u32[]{:S(2)}, u32[]{:S(2)}) collective-permute-start(bf16[672,640]{1,0:T(8,128)(2,1)S(1)} %constant_dynamic-update-slice_fusion.rest_8_.rest_5_), channel_id=1, source_target_pairs={{0,1},{1,0},{2,3},{3,2},{4,5},{5,4},{6,7},{7,6},{8,9},{9,8},{10,11... | collective-permute-start | bytes 2580488 | tf_op jit(solution)/shard_map/ppermute | solution.py:324
  32.0 22.2 %collective-permute-start.7 = (bf16[784,128]{1,0:T(8,128)(2,1)}, bf16[784,128]{1,0:T(8,128)(2,1)S(1)}, u32[]{:S(2)}, u32[]{:S(2)}) collective-permute-start(bf16[784,128]{1,0:T(8,128)(2,1)} %get-tuple-element.42), channel_id=1, source_target_pairs={{0,16},{4,20},{8,24},{12,28},{16,0},{20,4},{24,8},{28,12},{1,17},{... | collective-permute-start | bytes 602120 | tf_op jit(solution)/shard_map/ppermute | solution.py:321
  39.5 14.7 %collective-permute-start.8 = (bf16[784,128]{1,0:T(8,128)(2,1)}, bf16[784,128]{1,0:T(8,128)(2,1)S(1)}, u32[]{:S(2)}, u32[]{:S(2)}) collective-permute-start(bf16[784,128]{1,0:T(8,128)(2,1)} %get-tuple-element.44), channel_id=1, source_target_pairs={{0,24},{4,28},{8,16},{12,20},{16,8},{20,12},{24,0},{28,4},{1,25},{... | collective-permute-start | bytes 602120 | tf_op jit(solution)/shard_map/ppermute | solution.py:321
  54.2 18.5 %copy-start.16 = (bf16[784,128]{1,0:T(8,128)(2,1)}, bf16[784,128]{1,0:T(8,128)(2,1)S(1)}, u32[]{:S(2)}) copy-start(bf16[784,128]{1,0:T(8,128)(2,1)S(1)} %collective-permute-done.7.rest_4_) | copy-start | bytes 602116
  54.2 0.7 copy-start.17
  54.2 26.7 %copy-start = (bf16[672,640]{1,0:T(8,128)(2,1)}, bf16[672,640]{1,0:T(8,128)(2,1)S(1)}, u32[]{:S(2)}) copy-start(bf16[672,640]{1,0:T(8,128)(2,1)S(1)} %collective-permute-done.6.rest_4_.rest_7_) | copy-start | bytes 2580484
  54.9 17.8 %copy-start.10 = (bf16[672,640]{1,0:T(8,128)(2,1)}, bf16[672,640]{1,0:T(8,128)(2,1)S(1)}, u32[]{:S(2)}) copy-start(bf16[672,640]{1,0:T(8,128)(2,1)S(1)} %collective-permute-done.5.rest_10_.rest_9_) | copy-start | bytes 2580484
  54.9 17.8 %copy-start.11 = (bf16[672,640]{1,0:T(8,128)(2,1)}, bf16[672,640]{1,0:T(8,128)(2,1)S(1)}, u32[]{:S(2)}) copy-start(bf16[672,640]{1,0:T(8,128)(2,1)S(1)} %collective-permute-done.10.rest_9_.rest_6_) | copy-start | bytes 2580484
  54.9 2.4 %collective-permute-start.13 = (bf16[672,640]{1,0:T(8,128)(2,1)S(1)}, bf16[672,640]{1,0:T(8,128)(2,1)S(1)}, u32[]{:S(2)}, u32[]{:S(2)}) collective-permute-start(bf16[672,640]{1,0:T(8,128)(2,1)S(1)} %collective-permute-done.5.rest_10_.rest_9_), channel_id=1, source_target_pairs={{0,1},{1,0},{2,3},{3,2},{4,5},{5,4},{6,7},{7,6},{8,9},{9,8},{10,11... | collective-permute-start | bytes 2580488 | tf_op jit(solution)/shard_map/ppermute | solution.py:324
  54.9 26.0 %collective-permute-start.17 = (bf16[672,640]{1,0:T(8,128)(2,1)S(1)}, bf16[672,640]{1,0:T(8,128)(2,1)S(1)}, u32[]{:S(2)}, u32[]{:S(2)}) collective-permute-start(bf16[672,640]{1,0:T(8,128)(2,1)S(1)} %collective-permute-done.6.rest_4_.rest_7_), channel_id=1, source_target_pairs={{0,2},{1,3},{2,0},{3,1},{4,6},{5,7},{6,4},{7,5},{8,10},{9,11},{10,... | collective-permute-start | bytes 2580488 | tf_op jit(solution)/shard_map/ppermute | solution.py:324
  57.3 15.4 %copy-start.12 = (bf16[672,640]{1,0:T(8,128)(2,1)}, bf16[672,640]{1,0:T(8,128)(2,1)S(1)}, u32[]{:S(2)}) copy-start(bf16[672,640]{1,0:T(8,128)(2,1)S(1)} %collective-permute-done.13.rest_11_.rest_10_) | copy-start | bytes 2580484
  57.3 23.7 %collective-permute-start.16 = (bf16[672,640]{1,0:T(8,128)(2,1)S(1)}, bf16[672,640]{1,0:T(8,128)(2,1)S(1)}, u32[]{:S(2)}, u32[]{:S(2)}) collective-permute-start(bf16[672,640]{1,0:T(8,128)(2,1)S(1)} %collective-permute-done.6.rest_4_.rest_7_), channel_id=1, source_target_pairs={{0,1},{1,0},{2,3},{3,2},{4,5},{5,4},{6,7},{7,6},{8,9},{9,8},{10,11... | collective-permute-start | bytes 2580488 | tf_op jit(solution)/shard_map/ppermute | solution.py:324
  57.4 10.7 %collective-permute-start.12 = (bf16[784,128]{1,0:T(8,128)(2,1)}, bf16[784,128]{1,0:T(8,128)(2,1)S(1)}, u32[]{:S(2)}, u32[]{:S(2)}) collective-permute-start(bf16[784,128]{1,0:T(8,128)(2,1)} %get-tuple-element.50), channel_id=1, source_target_pairs={{0,28},{4,24},{8,20},{12,16},{16,12},{20,8},{24,4},{28,0},{1,29},{... | collective-permute-start | bytes 602120 | tf_op jit(solution)/shard_map/ppermute | solution.py:321
  59.0 13.7 %collective-permute-start.11 = (bf16[784,128]{1,0:T(8,128)(2,1)}, bf16[784,128]{1,0:T(8,128)(2,1)}, u32[]{:S(2)}, u32[]{:S(2)}) collective-permute-start(bf16[784,128]{1,0:T(8,128)(2,1)} %get-tuple-element.47), channel_id=1, source_target_pairs={{0,8},{4,12},{8,0},{12,4},{16,24},{20,28},{24,16},{28,20},{1,9},{5... | collective-permute-start | bytes 602120 | tf_op jit(solution)/shard_map/ppermute | solution.py:321
  63.3 17.6 %collective-permute-start.14 = (bf16[784,128]{1,0:T(8,128)(2,1)}, bf16[784,128]{1,0:T(8,128)(2,1)S(1)}, u32[]{:S(2)}, u32[]{:S(2)}) collective-permute-start(bf16[784,128]{1,0:T(8,128)(2,1)} %get-tuple-element.55), channel_id=1, source_target_pairs={{0,12},{4,8},{8,4},{12,0},{16,28},{20,24},{24,20},{28,16},{1,13},{... | collective-permute-start | bytes 602120 | tf_op jit(solution)/shard_map/ppermute | solution.py:321
  68.2 12.7 %copy-start.4 = (bf16[784,128]{1,0:T(8,128)(2,1)}, bf16[784,128]{1,0:T(8,128)(2,1)S(1)}, u32[]{:S(2)}) copy-start(bf16[784,128]{1,0:T(8,128)(2,1)S(1)} %collective-permute-done.12.rest_1_) | copy-start | bytes 602116
  68.2 12.8 %collective-permute-start.15 = (bf16[784,128]{1,0:T(8,128)(2,1)}, bf16[784,128]{1,0:T(8,128)(2,1)S(1)}, u32[]{:S(2)}, u32[]{:S(2)}) collective-permute-start(bf16[784,128]{1,0:T(8,128)(2,1)} %get-tuple-element.57), channel_id=1, source_target_pairs={{0,20},{4,16},{8,28},{12,24},{16,4},{20,0},{24,12},{28,8},{1,21},{... | collective-permute-start | bytes 602120 | tf_op jit(solution)/shard_map/ppermute | solution.py:321
  80.9 2.5 %copy-start.5 = (bf16[784,128]{1,0:T(8,128)(2,1)}, bf16[784,128]{1,0:T(8,128)(2,1)S(1)}, u32[]{:S(2)}) copy-start(bf16[784,128]{1,0:T(8,128)(2,1)S(1)} %collective-permute-done.14.rest_0_) | copy-start | bytes 602116
  80.9 2.5 %copy-start.6 = (bf16[784,128]{1,0:T(8,128)(2,1)}, bf16[784,128]{1,0:T(8,128)(2,1)S(1)}, u32[]{:S(2)}) copy-start(bf16[784,128]{1,0:T(8,128)(2,1)S(1)} %collective-permute-done.15.rest_2_) | copy-start | bytes 602116
  81.0 2.5 %copy-start.1 = (bf16[672,640]{1,0:T(8,128)(2,1)}, bf16[672,640]{1,0:T(8,128)(2,1)S(1)}, u32[]{:S(2)}) copy-start(bf16[672,640]{1,0:T(8,128)(2,1)S(1)} %collective-permute-done.17.rest_6_.rest_11_) | copy-start | bytes 2580484
  81.0 2.5 %copy-start.2 = (bf16[672,640]{1,0:T(8,128)(2,1)}, bf16[672,640]{1,0:T(8,128)(2,1)S(1)}, u32[]{:S(2)}) copy-start(bf16[672,640]{1,0:T(8,128)(2,1)S(1)} %collective-permute-done.16.rest_5_.rest_8_) | copy-start | bytes 2580484
  81.0 12.4 %copy-start.8 = (f32[8,224]{1,0:T(8,128)S(1)}, f32[8,224]{1,0:T(8,128)}, u32[]{:S(2)}) copy-start(f32[8,224]{1,0:T(8,128)} %get-tuple-element.39) | copy-start | bytes 21508
  81.0 2.5 %collective-permute-start.18 = (bf16[672,640]{1,0:T(8,128)(2,1)S(1)}, bf16[672,640]{1,0:T(8,128)(2,1)S(1)}, u32[]{:S(2)}, u32[]{:S(2)}) collective-permute-start(bf16[672,640]{1,0:T(8,128)(2,1)S(1)} %collective-permute-done.17.rest_6_.rest_11_), channel_id=1, source_target_pairs={{0,1},{1,0},{2,3},{3,2},{4,5},{5,4},{6,7},{7,6},{8,9},{9,8},{10,11... | collective-permute-start | bytes 2580488 | tf_op jit(solution)/shard_map/ppermute | solution.py:324
  83.5 0.9 copy-start.3
  91.2 1.4 %collective-permute-start.19 = (f32[8,224]{1,0:T(8,128)}, f32[8,224]{1,0:T(8,128)S(1)}, u32[]{:S(2)}, u32[]{:S(2)}) collective-permute-start(f32[8,224]{1,0:T(8,128)} %get-tuple-element.63), channel_id=1, source_target_pairs={{0,1},{1,0},{2,3},{3,2},{4,5},{5,4},{6,7},{7,6},{8,9},{9,8},{10,11... | collective-permute-start | bytes 21512 | tf_op jit(solution)/shard_map/ppermute | solution.py:324
  93.4 6.1 %collective-permute-start.21 = (f32[16,224]{1,0:T(8,128)S(1)}, f32[16,224]{1,0:T(8,128)S(1)}, u32[]{:S(2)}, u32[]{:S(2)}) collective-permute-start(f32[16,224]{1,0:T(8,128)S(1)} %pad_maximum_fusion.1), channel_id=1, source_target_pairs={{0,4},{4,0},{8,12},{12,8},{16,20},{20,16},{24,28},{28,24},{1,5},{5... | collective-permute-start | bytes 43016 | tf_op jit(solution)/shard_map/ppermute | solution.py:321
  95.0 4.5 %collective-permute-start.22 = (f32[8,224]{1,0:T(8,128)S(1)}, f32[8,224]{1,0:T(8,128)S(1)}, u32[]{:S(2)}, u32[]{:S(2)}) collective-permute-start(f32[8,224]{1,0:T(8,128)S(1)} %add.12), channel_id=1, source_target_pairs={{0,6},{1,7},{2,4},{3,5},{4,2},{5,3},{6,0},{7,1},{8,14},{9,15},{10,... | collective-permute-start | bytes 21512 | tf_op jit(solution)/shard_map/ppermute | solution.py:328
  96.4 3.7 %collective-permute-start.20 = (f32[8,224]{1,0:T(8,128)S(1)}, f32[8,224]{1,0:T(8,128)S(1)}, u32[]{:S(2)}, u32[]{:S(2)}) collective-permute-start(f32[8,224]{1,0:T(8,128)S(1)} %add.12), channel_id=1, source_target_pairs={{0,2},{1,3},{2,0},{3,1},{4,6},{5,7},{6,4},{7,5},{8,10},{9,11},{10,... | collective-permute-start | bytes 21512 | tf_op jit(solution)/shard_map/ppermute | solution.py:324
  100.1 9.6 %copy-start.9 = (f32[24,224]{1,0:T(8,128)}, f32[24,224]{1,0:T(8,128)S(1)}, u32[]{:S(2)}) copy-start(f32[24,224]{1,0:T(8,128)S(1)} %pad_maximum_fusion.rest_13_) | copy-start | bytes 64516
  100.1 6.6 %collective-permute-start.25 = (f32[24,224]{1,0:T(8,128)S(1)}, f32[24,224]{1,0:T(8,128)S(1)}, u32[]{:S(2)}, u32[]{:S(2)}) collective-permute-start(f32[24,224]{1,0:T(8,128)S(1)} %pad_maximum_fusion.rest_13_), channel_id=1, source_target_pairs={{0,24},{4,28},{8,16},{12,20},{16,8},{20,12},{24,0},{28,4},{1,25},{... | collective-permute-start | bytes 64520 | tf_op jit(solution)/shard_map/ppermute | solution.py:321
  104.9 4.7 %collective-permute-start.24 = (f32[24,224]{1,0:T(8,128)S(1)}, f32[24,224]{1,0:T(8,128)S(1)}, u32[]{:S(2)}, u32[]{:S(2)}) collective-permute-start(f32[24,224]{1,0:T(8,128)S(1)} %pad_maximum_fusion.rest_13_), channel_id=1, source_target_pairs={{0,16},{4,20},{8,24},{12,28},{16,0},{20,4},{24,8},{28,12},{1,17},{... | collective-permute-start | bytes 64520 | tf_op jit(solution)/shard_map/ppermute | solution.py:321
  104.9 4.7 %collective-permute-start.23 = (f32[24,224]{1,0:T(8,128)S(1)}, f32[24,224]{1,0:T(8,128)S(1)}, u32[]{:S(2)}, u32[]{:S(2)}) collective-permute-start(f32[24,224]{1,0:T(8,128)S(1)} %pad_maximum_fusion.rest_13_), channel_id=1, source_target_pairs={{0,8},{4,12},{8,0},{12,4},{16,24},{20,28},{24,16},{28,20},{1,9},{5... | collective-permute-start | bytes 64520 | tf_op jit(solution)/shard_map/ppermute | solution.py:321
  106.7 2.9 %copy-start.18 = (f32[24,224]{1,0:T(8,128)}, f32[24,224]{1,0:T(8,128)S(1)}, u32[]{:S(2)}) copy-start(f32[24,224]{1,0:T(8,128)S(1)} %collective-permute-done.25.rest_16_) | copy-start | bytes 64516
  109.6 0.6 copy-start.19
  109.6 0.6 copy-start.20

commit v3 on v2

--- a/solution.py
+++ b/solution.py
@@ -144,12 +144,14 @@
 
 def fetch(pieces, refs, held, sems, slots):
     copies = {}
-    live_rows = held.shape[1] // len(slots)
-    for e in range(held.shape[0]):
+    quarters = sems.shape[1]
+    live_rows, wide = held.shape[0] // len(slots), held.shape[1] // quarters
+    for e in range(quarters):
         for i, k in enumerate(slots):
             ref, at = pieces[k, e]
             source = refs[ref].at[at] if ref == 0 else refs[ref].at[pl.ds(at * live_rows, live_rows)]
-            copies[k, e] = pltpu.make_async_copy(source, held.at[e, pl.ds(i * live_rows, live_rows)], sems.at[i, e])
+            target = held.at[pl.ds(i * live_rows, live_rows), pl.ds(e * wide, wide)]
+            copies[k, e] = pltpu.make_async_copy(source, target, sems.at[i, e])
             copies[k, e].start()
     return copies
 
@@ -159,31 +161,31 @@
     hidden, refs, rest = rest[:n], rest[n:n + n_refs], rest[n + n_refs:]
     before, (sums, turned, held, rows_held, packed, sems, more_sems) = rest[:-7], rest[-7:]
     _, mp = my_place()
-    quarters, wide = held.shape[0], held.shape[2]
-    units = weight.shape[0]
-    rows_copies = []
-    for e in range(quarters):
-        columns = pl.ds(pl.multiple_of((mp ^ e) * wide, 128), wide)
-        rows_copies.append(pltpu.make_async_copy(weight.at[:, columns], rows_held.at[e], more_sems.at[e]))
-        rows_copies[e].start()
-    copies = fetch(pieces, refs, held, sems, slots)
-    packed_copies = []
+    quarters = sems.shape[1]
+    units, width = weight.shape
+    wide = width // quarters
+    packed_copies, rows_copies = [], []
     for i in range(n):
         packed_copies.append(pltpu.make_async_copy(hidden[i], packed.at[i], more_sems.at[quarters + i]))
         packed_copies[i].start()
-    product = jnp.zeros((units, n * live_rows), jnp.float32)
+    for e in range(quarters):
+        columns = pl.ds(pl.multiple_of((mp ^ e) * wide, 128), wide)
+        rows_copies.append(
+            pltpu.make_async_copy(weight.at[:, columns], rows_held.at[:, pl.ds(e * wide, wide)], more_sems.at[e])
+        )
+        rows_copies[e].start()
+    copies = fetch(pieces, refs, held, sems, slots)
+    for i in range(n):
+        packed_copies[i].wait()
+        head, tail = unpack_hidden(packed[i], units, live_rows)
+        turned[:, i * live_rows:(i + 1) * live_rows] = jnp.concatenate([head, tail], axis=1)
     for e in range(quarters):
         rows_copies[e].wait()
         for k in slots:
             copies[k, e].wait()
-        product += lax.dot_general(
-            rows_held[e], held[e], (((1,), (1,)), ((), ())), preferred_element_type=jnp.float32
-        )
-        if e == 1:
-            for i in range(n):
-                packed_copies[i].wait()
-                head, tail = unpack_hidden(packed[i], units, live_rows)
-                turned[:, i * live_rows:(i + 1) * live_rows] = jnp.concatenate([head, tail], axis=1)
+    product = lax.dot_general(
+        rows_held[...], held[...], (((1,), (1,)), ((), ())), preferred_element_type=jnp.float32
+    )
     line = jnp.sum(product * turned[...].astype(jnp.float32), axis=0, keepdims=True)
     total = before[0][...] if before else jnp.zeros(sums.shape, jnp.float32)
     row = iota(total.shape, 0)
@@ -218,7 +220,7 @@
     notes, rest = rest[:shards // 2], rest[shards // 2:]
     ratio_out, grad_out, held, turned, scaled, result, sems, out_sems = rest
     dp, mp = my_place()
-    quarters, wide = held.shape[0], held.shape[2]
+    quarters, wide = sems.shape[1], held.shape[1] // sems.shape[1]
     live_rows = notes[0].shape[1]
     copies = fetch(pieces, refs, held, sems, order)
     scale = SCALE / math.sqrt(quarters * wide)
@@ -245,13 +247,21 @@
 
     eye = iota((live_rows, live_rows), 0) == iota((live_rows, live_rows), 1)
     columns = [jnp.sum(jnp.where(eye, coef[k:k + 1], 0.0), axis=1, keepdims=True) for k in order]
+
+    def scale_rows(e):
+        for k in order:
+            copies[k, e].wait()
+        for i in range(shards):
+            rows = slice(i * live_rows, (i + 1) * live_rows)
+            part = held[rows, e * wide:(e + 1) * wide].astype(jnp.float32)
+            scaled[e % 2, rows] = (columns[i] * part).astype(jnp.bfloat16)
+
     writes = []
+    scale_rows(0)
     for e in range(quarters):
-        for i, k in enumerate(order):
-            copies[k, e].wait()
-            rows = slice(i * live_rows, (i + 1) * live_rows)
-            scaled[rows] = (columns[i] * held[e, rows].astype(jnp.float32)).astype(jnp.bfloat16)
-        result[e] = jnp.dot(turned[...], scaled[...], preferred_element_type=jnp.float32)
+        if e + 1 < quarters:
+            scale_rows(e + 1)
+        result[e] = jnp.dot(turned[...], scaled[e % 2], preferred_element_type=jnp.float32)
         write = pltpu.make_async_copy(
             result.at[e], grad_out.at[:, pl.ds(pl.multiple_of((mp ^ e) * wide, 128), wide)], out_sems.at[e]
         )
@@ -312,7 +322,8 @@
     rows = packed_rows(units, live_rows)
     slots_each = 2 * respond // shards
     bf16, f32 = jnp.bfloat16, jnp.float32
-    big = pltpu.CompilerParams(vmem_limit_bytes=56 * 1024 * 1024)
+    def room(mib):
+        return pltpu.CompilerParams(vmem_limit_bytes=mib * 1024 * 1024)
 
     def cost(flops, moved):
         return pl.CostEstimate(flops=int(flops), bytes_accessed=int(moved), transcendentals=0)
@@ -339,7 +350,7 @@
         in_specs=[VMEM, ANY],
         out_specs=(VMEM, VMEM),
         scratch_shapes=[pltpu.VMEM((2, respond * seglen, wide), bf16), pltpu.SemaphoreType.DMA((2,))],
-        compiler_params=big,
+        compiler_params=room(12),
         name="pack_first",
     )(lengths, readout)
 
@@ -353,7 +364,7 @@
             in_specs=[VMEM] * 7,
             out_specs=(VMEM,) * (shards + 2),
             scratch_shapes=[pltpu.VMEM((shards * rows, 128), bf16)],
-            compiler_params=big,
+            compiler_params=room(20),
             cost_estimate=cost(2e9, 8e6),
             name="pack_rest",
         )(after(lengths, gates), routes.reshape(1, respond), log_gap.T, advantage.reshape(1, respond),
@@ -386,13 +397,13 @@
             in_specs=[ANY] * (1 + len(slots) + len(refs)) + [VMEM] * len(before),
             out_specs=(VMEM, VMEM),
             scratch_shapes=[
-                pltpu.VMEM((quarters, len(slots) * live_rows, wide), bf16),
-                pltpu.VMEM((quarters, units, wide), bf16),
+                pltpu.VMEM((len(slots) * live_rows, width), bf16),
+                pltpu.VMEM((units, width), bf16),
                 pltpu.VMEM((len(slots), rows, 128), bf16),
                 pltpu.SemaphoreType.DMA((len(slots), quarters)),
                 pltpu.SemaphoreType.DMA((quarters + len(slots),)),
             ],
-            compiler_params=big,
+            compiler_params=room(20),
             cost_estimate=cost(2 * units * len(slots) * live_rows * width, 2 * len(slots) * live_rows * width),
             name="shift_sums",
         )(weight, *(got[f"h{k}"] for k in slots), *refs, *before)
@@ -441,14 +452,14 @@
         in_specs=[VMEM] * len(groups) + [ANY] * len(refs) + [VMEM] * len(notes),
         out_specs=(VMEM, ANY),
         scratch_shapes=[
-            pltpu.VMEM((quarters, shards * live_rows, wide), bf16),
+            pltpu.VMEM((shards * live_rows, width), bf16),
             pltpu.VMEM((units, shards * live_rows), bf16),
-            pltpu.VMEM((shards * live_rows, wide), bf16),
+            pltpu.VMEM((2, shards * live_rows, wide), bf16),
             pltpu.VMEM((quarters, units, wide), f32),
             pltpu.SemaphoreType.DMA((shards, quarters)),
             pltpu.SemaphoreType.DMA((quarters,)),
         ],
-        compiler_params=big,
+        compiler_params=room(56),
         cost_estimate=cost(2 * units * shards * live_rows * width, 2 * shards * live_rows * width + 4 * units * width),
         name="weight_grad",
     )(*turned, *refs, *notes)

time: 124 us -> 118 us (0.952)
  Pallas kernels: 36.5 us -> 26.3 us
  local copies, waits for them, and re-layouts: 2.43 us -> 10.7 us
  waiting for transfers between devices: 44.1 us -> 40 us
    unnamed x44 -> x56, local copies, waits for them, and re-layouts: 2.36 us -> 10.6 us
    ppermute x16, waiting for transfers between devices: 36.5 us -> 32 us  [over_dp(): return lax.ppermute(x, 'dp', [(s, s ^ m) for s in range(shards)])]
    pallas_call x2, Pallas kernels: 15 us -> 10.7 us  [shift_sums(): pl.pallas_call(functools.partial(shift_kernel, places, len(refs), slots,...]
    pallas_call x1, Pallas kernels: 4.91 us -> 1.99 us  [rest(): pl.pallas_call(functools.partial(pack_rest, live_rows, seglen), out_shape...]
    pallas_call x1, Pallas kernels: 3.02 us -> 0.87 us  [cube_body(): pl.pallas_call(functools.partial(pack_first, live_rows, seglen), out_shap...]
    ppermute x1, starting transfers between devices: 1.41 us -> 3.34 us  [over_both(): return lax.ppermute(x, ('dp', 'mp'), pairs)]
    ppermute x9, waiting for transfers between devices: 5.11 us -> 6.44 us  [over_mp(): return lax.ppermute(x, 'mp', [(s, s ^ m) for s in range(quarters)])]
  transfers between devices with their start and end apart: 26 -> 26, of which waited for: 12 -> 13; matrix products, arithmetic and copies ran while one was open for 0% -> 0% of each run, Pallas kernels for 11% -> 7%
where the time goes in v3:
time: 118 us; the launch traced here: 117 us
  waiting for transfers between devices  40 us (34%)
  starting transfers between devices  39.4 us (33%)
  Pallas kernels  26.3 us (22%)
  local copies, waits for them, and re-layouts  10.7 us (9%)
    ppermute x16, starting transfers between devices, over_dp(): return lax.ppermute(x, 'dp', [(s, s ^ m) for s in range(shards)])  32.6 us
    ppermute x16, waiting for transfers between devices, over_dp(): return lax.ppermute(x, 'dp', [(s, s ^ m) for s in range(shards)])  32 us
    pallas_call x1, Pallas kernels, cube_body(): pl.pallas_call(functools.partial(grad_kernel, places, len(refs), groups,...  12.8 us
    pallas_call x2, Pallas kernels, shift_sums(): pl.pallas_call(functools.partial(shift_kernel, places, len(refs), slots,...  10.7 us
    unnamed x56, local copies, waits for them, and re-layouts  10.6 us
    ppermute x9, waiting for transfers between devices, over_mp(): return lax.ppermute(x, 'mp', [(s, s ^ m) for s in range(quarters)])  6.44 us
    ppermute x9, starting transfers between devices, over_mp(): return lax.ppermute(x, 'mp', [(s, s ^ m) for s in range(quarters)])  3.44 us
    ppermute x1, starting transfers between devices, over_both(): return lax.ppermute(x, ('dp', 'mp'), pairs)  3.34 us
  transfers between devices with their start and end apart: 26, of which 13 were waited for; matrix products, arithmetic and copies ran while one was open for 0% of the time, Pallas kernels for 7%

profile of v3, /device:TPU:0, one launch (start us, length us, event | category | flops | bytes accessed | tf_op | source)
XLA Modules:
  0.0 117.5 jit_solution(3730174040730983578)
XLA Ops:
  0.6 0.0 copy-start.1
  0.6 1.3 %copy-done.1 = bf16[256,2560]{1,0:T(8,128)(2,1)S(1)} copy-done((bf16[256,2560]{1,0:T(8,128)(2,1)S(1)}, bf16[256,2560]{1,0:T(8,128)(2,1)}, u32[]{:S(2)}) %copy-start.1) | copy-done | bytes 1310744
  2.0 0.7 copy-done.9
  2.6 0.9 pack_first.1
  3.5 3.0 %collective-permute-start.4 = (bf16[448,640]{1,0:T(8,128)(2,1)S(1)}, bf16[448,640]{1,0:T(8,128)(2,1)S(1)}, u32[]{:S(2)}, u32[]{:S(2)}) collective-permute-start(bf16[448,640]{1,0:T(8,128)(2,1)S(1)} %get-tuple-element.38), channel_id=1, source_target_pairs={{0,4},{4,0},{8,12},{12,8},{16,20},{20,16},{24,28},{28,24},{1,5},{5... | collective-permute-start | bytes 1720328 | tf_op jit(solution)/shard_map/ppermute | solution.py:332
  6.5 2.6 %collective-permute-start.3 = (bf16[224,640]{1,0:T(8,128)(2,1)S(1)}, bf16[224,640]{1,0:T(8,128)(2,1)S(1)}, u32[]{:S(2)}, u32[]{:S(2)}) collective-permute-start(bf16[224,640]{1,0:T(8,128)(2,1)S(1)} %get-tuple-element.37), channel_id=1, source_target_pairs={{0,16},{4,20},{8,24},{12,28},{16,0},{20,4},{24,8},{28,12},{1,17},{... | collective-permute-start | bytes 860168 | tf_op jit(solution)/shard_map/ppermute | solution.py:332
  9.1 1.3 %collective-permute-start.2 = (bf16[224,640]{1,0:T(8,128)(2,1)S(1)}, bf16[224,640]{1,0:T(8,128)(2,1)S(1)}, u32[]{:S(2)}, u32[]{:S(2)}) collective-permute-start(bf16[224,640]{1,0:T(8,128)(2,1)S(1)} %get-tuple-element.37), channel_id=1, source_target_pairs={{0,24},{4,28},{8,16},{12,20},{16,8},{20,12},{24,0},{28,4},{1,25},{... | collective-permute-start | bytes 860168 | tf_op jit(solution)/shard_map/ppermute | solution.py:332
  10.5 0.2 collective-permute-start.1
  10.7 1.3 %copy-done.2 = bf16[256,2560]{1,0:T(8,128)(2,1)S(1)} copy-done((bf16[256,2560]{1,0:T(8,128)(2,1)S(1)}, bf16[256,2560]{1,0:T(8,128)(2,1)}, u32[]{:S(2)}) %copy-start.2) | copy-done | bytes 1310744
  12.0 0.7 copy-done.10
  12.7 1.5 %copy-done.11 = bf16[256,3584]{1,0:T(8,128)(2,1)S(1)} copy-done((bf16[256,3584]{1,0:T(8,128)(2,1)S(1)}, bf16[256,3584]{1,0:T(8,128)(2,1)}, u32[]{:S(2)}) %copy-start.11) | copy-done | bytes 1835032
  14.2 0.7 copy-done.18
  14.9 0.7 copy-done.19
  15.5 0.7 copy-done.20
  16.2 0.7 copy-done.21
  16.8 2.0 %pack_rest.1 = (f32[8,224]{1,0:T(8,128)S(1)}, bf16[4,224,640]{2,1,0:T(8,128)(2,1)S(1)}, bf16[784,128]{1,0:T(8,128)(2,1)S(1)}, bf16[784,128]{1,0:T(8,128)(2,1)S(1...) custom-call(s32[1,32]{1,0:T(1,128)S(1)} %copy-done.10, ...), custom_call_target="tpu_custom_call" | custom-call | flops 2000000000 | bytes 8000000 | tf_op jit(solution)/shard_map/pack_rest/pallas_call | solution.py:358
  18.8 0.5 collective-permute-start
  19.4 5.4 %collective-permute-done.rest_1_ = bf16[784,128]{1,0:T(8,128)(2,1)S(1)} collective-permute-done((bf16[784,128]{1,0:T(8,128)(2,1)S(1)}, bf16[784,128]{1,0:T(8,128)(2,1)S(1)}, u32[]{:S(2)}, u32[]{:S(2)}) %collective-permute-start) | collective-permute-done | bytes 200736 | tf_op jit(solution)/shard_map/ppermute | solution.py:332
  24.7 4.5 %collective-permute-done.3 = bf16[224,640]{1,0:T(8,128)(2,1)S(1)} collective-permute-done((bf16[224,640]{1,0:T(8,128)(2,1)S(1)}, bf16[224,640]{1,0:T(8,128)(2,1)S(1)}, u32[]{:S(2)}, u32[]{:S(2)}) %collective-permute-start.3) | collective-permute-done | bytes 286752 | tf_op jit(solution)/shard_map/ppermute | solution.py:332
  29.2 0.0 collective-permute-done.2
  29.2 0.2 collective-permute-done.1
  29.4 0.0 collective-permute-done.4.rest_6_.rest_3_
  29.5 0.5 collective-permute-start.6
  30.0 1.5 %collective-permute-start.5 = (bf16[672,640]{1,0:T(8,128)(2,1)S(1)}, bf16[672,640]{1,0:T(8,128)(2,1)S(1)}, u32[]{:S(2)}, u32[]{:S(2)}) collective-permute-start(bf16[672,640]{1,0:T(8,128)(2,1)S(1)} %constant_dynamic-update-slice_fusion.rest_8_.rest_5_), channel_id=1, source_target_pairs={{0,2},{1,3},{2,0},{3,1},{4,6},{5,7},{6,4},{7,5},{8,10},{9,11},{10,... | collective-permute-start | bytes 2580488 | tf_op jit(solution)/shard_map/ppermute | solution.py:335
  31.6 0.0 collective-permute-start.10
  31.6 7.6 %collective-permute-start.7 = (bf16[784,128]{1,0:T(8,128)(2,1)S(1)}, bf16[784,128]{1,0:T(8,128)(2,1)S(1)}, u32[]{:S(2)}, u32[]{:S(2)}) collective-permute-start(bf16[784,128]{1,0:T(8,128)(2,1)S(1)} %get-tuple-element.42), channel_id=1, source_target_pairs={{0,16},{4,20},{8,24},{12,28},{16,0},{20,4},{24,8},{28,12},{1,17},{... | collective-permute-start | bytes 602120 | tf_op jit(solution)/shard_map/ppermute | solution.py:332
  39.1 0.4 collective-permute-start.8
  39.6 14.0 %collective-permute-done.7.rest_4_ = bf16[784,128]{1,0:T(8,128)(2,1)S(1)} collective-permute-done((bf16[784,128]{1,0:T(8,128)(2,1)S(1)}, bf16[784,128]{1,0:T(8,128)(2,1)S(1)}, u32[]{:S(2)}, u32[]{:S(2)}) %collective-permute-start.7) | collective-permute-done | bytes 200736 | tf_op jit(solution)/shard_map/ppermute | solution.py:332
  53.6 0.0 collective-permute-done.8.rest_3_
  53.6 0.0 collective-permute-done.6.rest_4_.rest_7_
  53.6 0.0 collective-permute-done.5.rest_10_.rest_9_
  53.6 0.0 collective-permute-done.10.rest_9_.rest_6_
  53.6 0.1 collective-permute-start.13
  53.7 1.3 %collective-permute-start.17 = (bf16[672,640]{1,0:T(8,128)(2,1)S(1)}, bf16[672,640]{1,0:T(8,128)(2,1)S(1)}, u32[]{:S(2)}, u32[]{:S(2)}) collective-permute-start(bf16[672,640]{1,0:T(8,128)(2,1)S(1)} %collective-permute-done.6.rest_4_.rest_7_), channel_id=1, source_target_pairs={{0,2},{1,3},{2,0},{3,1},{4,6},{5,7},{6,4},{7,5},{8,10},{9,11},{10,... | collective-permute-start | bytes 2580488 | tf_op jit(solution)/shard_map/ppermute | solution.py:335
  55.0 1.0 collective-permute-done.13.rest_11_.rest_10_
  56.1 0.1 collective-permute-start.16
  56.2 2.2 %collective-permute-start.12 = (bf16[784,128]{1,0:T(8,128)(2,1)S(1)}, bf16[784,128]{1,0:T(8,128)(2,1)S(1)}, u32[]{:S(2)}, u32[]{:S(2)}) collective-permute-start(bf16[784,128]{1,0:T(8,128)(2,1)S(1)} %get-tuple-element.50), channel_id=1, source_target_pairs={{0,28},{4,24},{8,20},{12,16},{16,12},{20,8},{24,4},{28,0},{1,29},{... | collective-permute-start | bytes 602120 | tf_op jit(solution)/shard_map/ppermute | solution.py:332
  58.4 4.6 %collective-permute-start.11 = (bf16[784,128]{1,0:T(8,128)(2,1)S(1)}, bf16[784,128]{1,0:T(8,128)(2,1)S(1)}, u32[]{:S(2)}, u32[]{:S(2)}) collective-permute-start(bf16[784,128]{1,0:T(8,128)(2,1)S(1)} %get-tuple-element.47), channel_id=1, source_target_pairs={{0,8},{4,12},{8,0},{12,4},{16,24},{20,28},{24,16},{28,20},{1,9},{5... | collective-permute-start | bytes 602120 | tf_op jit(solution)/shard_map/ppermute | solution.py:332
  62.9 3.8 %collective-permute-done.12.rest_1_ = bf16[784,128]{1,0:T(8,128)(2,1)S(1)} collective-permute-done((bf16[784,128]{1,0:T(8,128)(2,1)S(1)}, bf16[784,128]{1,0:T(8,128)(2,1)S(1)}, u32[]{:S(2)}, u32[]{:S(2)}) %collective-permute-start.12) | collective-permute-done | bytes 200736 | tf_op jit(solution)/shard_map/ppermute | solution.py:332
  66.7 5.1 %collective-permute-start.15 = (bf16[784,128]{1,0:T(8,128)(2,1)S(1)}, bf16[784,128]{1,0:T(8,128)(2,1)S(1)}, u32[]{:S(2)}, u32[]{:S(2)}) collective-permute-start(bf16[784,128]{1,0:T(8,128)(2,1)S(1)} %get-tuple-element.57), channel_id=1, source_target_pairs={{0,20},{4,16},{8,28},{12,24},{16,4},{20,0},{24,12},{28,8},{1,21},{... | collective-permute-start | bytes 602120 | tf_op jit(solution)/shard_map/ppermute | solution.py:332
  71.9 0.0 collective-permute-done.11.rest_2_
  71.9 6.4 %shift_sums.2 = (f32[8,224]{1,0:T(8,128)S(1)}, bf16[448,1120]{1,0:T(8,128)(2,1)S(1)}) custom-call(bf16[448,2560]{1,0:T(8,128)(2,1)S(1)} %copy-done, bf16[784,128]{1,0:T(8,128)(2,1)S(1)} %get-tuple-element.34.rest_0_, bf16[784,128]{1,0:T(8,128)(2,1)S(1)} %collective-permute-done.rest_1_, bf16[784,128]{1,0:T(8,128)(2,1)S(1)} %collective-permute-done.11.rest_2_, ...), custom_call_target="tpu_custom_call" | custom-call | flops 2569011200 | bytes 5734400 | tf_op jit(solution)/shard_map/shift_sums/pallas_call | solution.py:391
  78.3 1.0 copy-done.22
  79.3 2.0 %collective-permute-done.15.rest_2_ = bf16[784,128]{1,0:T(8,128)(2,1)S(1)} collective-permute-done((bf16[784,128]{1,0:T(8,128)(2,1)S(1)}, bf16[784,128]{1,0:T(8,128)(2,1)S(1)}, u32[]{:S(2)}, u32[]{:S(2)}) %collective-permute-start.15) | collective-permute-done | bytes 200736 | tf_op jit(solution)/shard_map/ppermute | solution.py:332
  81.3 0.0 collective-permute-done.16.rest_5_.rest_8_
  81.3 0.1 collective-permute-start.18
  81.4 2.4 %collective-permute-done.18.rest_7_.rest_12_ = bf16[672,640]{1,0:T(8,128)(2,1)S(1)} collective-permute-done((bf16[672,640]{1,0:T(8,128)(2,1)S(1)}, bf16[672,640]{1,0:T(8,128)(2,1)S(1)}, u32[]{:S(2)}, u32[]{:S(2)}) %collective-permute-start.18) | collective-permute-done | bytes 860192 | tf_op jit(solution)/shard_map/ppermute | solution.py:335
  83.8 4.3 %shift_sums.3 = (f32[8,224]{1,0:T(8,128)S(1)}, bf16[448,672]{1,0:T(8,128)(2,1)S(1)}) custom-call(bf16[448,2560]{1,0:T(8,128)(2,1)S(1)} %copy-done, bf16[784,128]{1,0:T(8,128)(2,1)S(1)} %collective-permute-done.14.rest_0_, bf16[784,128]{1,0:T(8,128)(2,1)S(1)} %collective-permute-done.12.rest_1_, bf16[784,128]{1,0:T(8,128)(2,1)S(1)} %collective-permute-done.15.rest_2_, ...), custom_call_target="tpu_custom_call" | custom-call | flops 1541406720 | bytes 3440640 | tf_op jit(solution)/shard_map/shift_sums/pallas_call | solution.py:391
  88.1 0.9 copy-done.15
  89.0 0.1 collective-permute-start.19
  89.1 1.0 collective-permute-done.19
  90.2 0.1 collective-permute-start.21
  90.2 3.3 %collective-permute-start.22 = (f32[8,224]{1,0:T(8,128)S(1)}, f32[8,224]{1,0:T(8,128)S(1)}, u32[]{:S(2)}, u32[]{:S(2)}) collective-permute-start(f32[8,224]{1,0:T(8,128)S(1)} %add.12), channel_id=1, source_target_pairs={{0,6},{1,7},{2,4},{3,5},{4,2},{5,3},{6,0},{7,1},{8,14},{9,15},{10,... | collective-permute-start | bytes 21512 | tf_op jit(solution)/shard_map/ppermute | solution.py:339
  93.6 0.1 collective-permute-start.20
  93.7 1.5 %collective-permute-done.22 = f32[8,224]{1,0:T(8,128)S(1)} collective-permute-done((f32[8,224]{1,0:T(8,128)S(1)}, f32[8,224]{1,0:T(8,128)S(1)}, u32[]{:S(2)}, u32[]{:S(2)}) %collective-permute-start.22) | collective-permute-done | bytes 7200 | tf_op jit(solution)/shard_map/ppermute | solution.py:339
  95.2 0.0 collective-permute-done.21
  95.3 2.0 %collective-permute-done.20 = f32[8,224]{1,0:T(8,128)S(1)} collective-permute-done((f32[8,224]{1,0:T(8,128)S(1)}, f32[8,224]{1,0:T(8,128)S(1)}, u32[]{:S(2)}, u32[]{:S(2)}) %collective-permute-start.20) | collective-permute-done | bytes 7200 | tf_op jit(solution)/shard_map/ppermute | solution.py:335
  97.3 1.9 %collective-permute-start.25 = (f32[24,224]{1,0:T(8,128)S(1)}, f32[24,224]{1,0:T(8,128)S(1)}, u32[]{:S(2)}, u32[]{:S(2)}) collective-permute-start(f32[24,224]{1,0:T(8,128)S(1)} %pad_maximum_fusion.rest_13_), channel_id=1, source_target_pairs={{0,24},{4,28},{8,16},{12,20},{16,8},{20,12},{24,0},{28,4},{1,25},{... | collective-permute-start | bytes 64520 | tf_op jit(solution)/shard_map/ppermute | solution.py:332
  99.2 2.5 %collective-permute-start.23 = (f32[24,224]{1,0:T(8,128)S(1)}, f32[24,224]{1,0:T(8,128)S(1)}, u32[]{:S(2)}, u32[]{:S(2)}) collective-permute-start(f32[24,224]{1,0:T(8,128)S(1)} %pad_maximum_fusion.rest_13_), channel_id=1, source_target_pairs={{0,8},{4,12},{8,0},{12,4},{16,24},{20,28},{24,16},{28,20},{1,9},{5... | collective-permute-start | bytes 64520 | tf_op jit(solution)/shard_map/ppermute | solution.py:332
  101.7 1.2 %collective-permute-done.25.rest_16_ = f32[24,224]{1,0:T(8,128)S(1)} collective-permute-done((f32[24,224]{1,0:T(8,128)S(1)}, f32[24,224]{1,0:T(8,128)S(1)}, u32[]{:S(2)}, u32[]{:S(2)}) %collective-permute-start.25) | collective-permute-done | bytes 21536 | tf_op jit(solution)/shard_map/ppermute | solution.py:332
  103.0 1.0 collective-permute-done.24.rest_15_
  104.0 0.6 copy-done.25
  104.5 0.0 copy-done.26
  104.6 12.8 %weight_grad.1 = (f32[8,64]{1,0:T(8,128)}, f32[448,2560]{1,0:T(8,128)}) custom-call(bf16[448,1120]{1,0:T(8,128)(2,1)} %copy-done.22, bf16[448,672]{1,0:T(8,128)(2,1)} %copy-done.15, bf16[4,224,640]{2,1,0:T(8,128)(2,1)} %copy-done.3, bf16[448,640]{1,0:T(8,128)(2,1)} %copy-done.16, bf16[448,640]{1,0:T(8,128)(2,1)} %copy-done.17, bf16[672,640]{1,0:T(8,128)(2,1)} %copy-done.8, ...), custom_call_target="tpu_custom_call" | custom-call | flops 4110417920 | bytes 13762560 | tf_op jit(solution)/shard_map/weight_grad/pallas_call | solution.py:446
  (57 shorter events, 0.3 us)
Async XLA Ops:
  0.6 1.3 %copy-start.1 = (bf16[256,2560]{1,0:T(8,128)(2,1)S(1)}, bf16[256,2560]{1,0:T(8,128)(2,1)}, u32[]{:S(2)}) copy-start(bf16[256,2560]{1,0:T(8,128)(2,1)} %read.3) | copy-start | bytes 3932164
  1.9 0.7 copy-start.9
  3.5 25.9 %collective-permute-start.4 = (bf16[448,640]{1,0:T(8,128)(2,1)S(1)}, bf16[448,640]{1,0:T(8,128)(2,1)S(1)}, u32[]{:S(2)}, u32[]{:S(2)}) collective-permute-start(bf16[448,640]{1,0:T(8,128)(2,1)S(1)} %get-tuple-element.38), channel_id=1, source_target_pairs={{0,4},{4,0},{8,12},{12,8},{16,20},{20,16},{24,28},{28,24},{1,5},{5... | collective-permute-start | bytes 1720328 | tf_op jit(solution)/shard_map/ppermute | solution.py:332
  6.5 22.7 %collective-permute-start.3 = (bf16[224,640]{1,0:T(8,128)(2,1)S(1)}, bf16[224,640]{1,0:T(8,128)(2,1)S(1)}, u32[]{:S(2)}, u32[]{:S(2)}) collective-permute-start(bf16[224,640]{1,0:T(8,128)(2,1)S(1)} %get-tuple-element.37), channel_id=1, source_target_pairs={{0,16},{4,20},{8,24},{12,28},{16,0},{20,4},{24,8},{28,12},{1,17},{... | collective-permute-start | bytes 860168 | tf_op jit(solution)/shard_map/ppermute | solution.py:332
  9.1 20.1 %collective-permute-start.2 = (bf16[224,640]{1,0:T(8,128)(2,1)S(1)}, bf16[224,640]{1,0:T(8,128)(2,1)S(1)}, u32[]{:S(2)}, u32[]{:S(2)}) collective-permute-start(bf16[224,640]{1,0:T(8,128)(2,1)S(1)} %get-tuple-element.37), channel_id=1, source_target_pairs={{0,24},{4,28},{8,16},{12,20},{16,8},{20,12},{24,0},{28,4},{1,25},{... | collective-permute-start | bytes 860168 | tf_op jit(solution)/shard_map/ppermute | solution.py:332
  10.5 18.9 %collective-permute-start.1 = (bf16[224,640]{1,0:T(8,128)(2,1)S(1)}, bf16[224,640]{1,0:T(8,128)(2,1)S(1)}, u32[]{:S(2)}, u32[]{:S(2)}) collective-permute-start(bf16[224,640]{1,0:T(8,128)(2,1)S(1)} %get-tuple-element.37), channel_id=1, source_target_pairs={{0,8},{4,12},{8,0},{12,4},{16,24},{20,28},{24,16},{28,20},{1,9},{5... | collective-permute-start | bytes 860168 | tf_op jit(solution)/shard_map/ppermute | solution.py:332
  10.7 1.3 %copy-start.2 = (bf16[256,2560]{1,0:T(8,128)(2,1)S(1)}, bf16[256,2560]{1,0:T(8,128)(2,1)}, u32[]{:S(2)}) copy-start(bf16[256,2560]{1,0:T(8,128)(2,1)} %read.3) | copy-start | bytes 3932164
  12.0 0.7 copy-start.10
  12.7 1.5 %copy-start.11 = (bf16[256,3584]{1,0:T(8,128)(2,1)S(1)}, bf16[256,3584]{1,0:T(8,128)(2,1)}, u32[]{:S(2)}) copy-start(bf16[256,3584]{1,0:T(8,128)(2,1)} %hidden.1) | copy-start | bytes 5505028
  14.2 0.7 copy-start.18
  14.9 0.7 copy-start.19
  15.5 0.7 copy-start.20
  16.2 0.7 copy-start.21
  16.8 55.1 %copy-start = (bf16[448,2560]{1,0:T(8,128)(2,1)S(1)}, bf16[448,2560]{1,0:T(8,128)(2,1)}, u32[]{:S(2)}) copy-start(bf16[448,2560]{1,0:T(8,128)(2,1)} %weight.3) | copy-start | bytes 6881284
  18.8 65.0 %copy-start.3 = (bf16[4,224,640]{2,1,0:T(8,128)(2,1)}, bf16[4,224,640]{2,1,0:T(8,128)(2,1)S(1)}, u32[]{:S(2)}) copy-start(bf16[4,224,640]{2,1,0:T(8,128)(2,1)S(1)} %get-tuple-element.51.rest_5_.rest_3_.rest_2_) | copy-start | bytes 3440644
  18.8 5.9 %collective-permute-start = (bf16[784,128]{1,0:T(8,128)(2,1)S(1)}, bf16[784,128]{1,0:T(8,128)(2,1)S(1)}, u32[]{:S(2)}, u32[]{:S(2)}) collective-permute-start(bf16[784,128]{1,0:T(8,128)(2,1)S(1)} %get-tuple-element.35), channel_id=1, source_target_pairs={{0,4},{4,0},{8,12},{12,8},{16,20},{20,16},{24,28},{28,24},{1,5},{5... | collective-permute-start | bytes 602120 | tf_op jit(solution)/shard_map/ppermute | solution.py:332
  29.4 48.9 %copy-start.16 = (bf16[448,640]{1,0:T(8,128)(2,1)}, bf16[448,640]{1,0:T(8,128)(2,1)S(1)}, u32[]{:S(2)}) copy-start(bf16[448,640]{1,0:T(8,128)(2,1)S(1)} %collective-permute-done.4.rest_6_.rest_3_) | copy-start | bytes 1720324
  29.4 2.2 %collective-permute-start.9 = (bf16[448,640]{1,0:T(8,128)(2,1)S(1)}, bf16[448,640]{1,0:T(8,128)(2,1)S(1)}, u32[]{:S(2)}, u32[]{:S(2)}) collective-permute-start(bf16[448,640]{1,0:T(8,128)(2,1)S(1)} %collective-permute-done.4.rest_6_.rest_3_), channel_id=1, source_target_pairs={{0,1},{1,0},{2,3},{3,2},{4,5},{5,4},{6,7},{7,6},{8,9},{9,8},{10,11... | collective-permute-start | bytes 1720328 | tf_op jit(solution)/shard_map/ppermute | solution.py:335
  29.5 48.8 %copy-start.8 = (bf16[672,640]{1,0:T(8,128)(2,1)}, bf16[672,640]{1,0:T(8,128)(2,1)S(1)}, u32[]{:S(2)}) copy-start(bf16[672,640]{1,0:T(8,128)(2,1)S(1)} %constant_dynamic-update-slice_fusion.rest_8_.rest_5_) | copy-start | bytes 2580484
  29.5 24.1 %collective-permute-start.6 = (bf16[672,640]{1,0:T(8,128)(2,1)S(1)}, bf16[672,640]{1,0:T(8,128)(2,1)S(1)}, u32[]{:S(2)}, u32[]{:S(2)}) collective-permute-start(bf16[672,640]{1,0:T(8,128)(2,1)S(1)} %constant_dynamic-update-slice_fusion.rest_8_.rest_5_), channel_id=1, source_target_pairs={{0,4},{4,0},{8,12},{12,8},{16,20},{20,16},{24,28},{28,24},{1,5},{5... | collective-permute-start | bytes 2580488 | tf_op jit(solution)/shard_map/ppermute | solution.py:332
  30.0 23.6 %collective-permute-start.5 = (bf16[672,640]{1,0:T(8,128)(2,1)S(1)}, bf16[672,640]{1,0:T(8,128)(2,1)S(1)}, u32[]{:S(2)}, u32[]{:S(2)}) collective-permute-start(bf16[672,640]{1,0:T(8,128)(2,1)S(1)} %constant_dynamic-update-slice_fusion.rest_8_.rest_5_), channel_id=1, source_target_pairs={{0,2},{1,3},{2,0},{3,1},{4,6},{5,7},{6,4},{7,5},{8,10},{9,11},{10,... | collective-permute-start | bytes 2580488 | tf_op jit(solution)/shard_map/ppermute | solution.py:335
  31.6 46.7 %copy-start.17 = (bf16[448,640]{1,0:T(8,128)(2,1)}, bf16[448,640]{1,0:T(8,128)(2,1)S(1)}, u32[]{:S(2)}) copy-start(bf16[448,640]{1,0:T(8,128)(2,1)S(1)} %collective-permute-done.9.rest_7_.rest_4_) | copy-start | bytes 1720324
  31.6 22.0 %collective-permute-start.10 = (bf16[672,640]{1,0:T(8,128)(2,1)S(1)}, bf16[672,640]{1,0:T(8,128)(2,1)S(1)}, u32[]{:S(2)}, u32[]{:S(2)}) collective-permute-start(bf16[672,640]{1,0:T(8,128)(2,1)S(1)} %constant_dynamic-update-slice_fusion.rest_8_.rest_5_), channel_id=1, source_target_pairs={{0,1},{1,0},{2,3},{3,2},{4,5},{5,4},{6,7},{7,6},{8,9},{9,8},{10,11... | collective-permute-start | bytes 2580488 | tf_op jit(solution)/shard_map/ppermute | solution.py:335
  31.6 22.0 %collective-permute-start.7 = (bf16[784,128]{1,0:T(8,128)(2,1)S(1)}, bf16[784,128]{1,0:T(8,128)(2,1)S(1)}, u32[]{:S(2)}, u32[]{:S(2)}) collective-permute-start(bf16[784,128]{1,0:T(8,128)(2,1)S(1)} %get-tuple-element.42), channel_id=1, source_target_pairs={{0,16},{4,20},{8,24},{12,28},{16,0},{20,4},{24,8},{28,12},{1,17},{... | collective-permute-start | bytes 602120 | tf_op jit(solution)/shard_map/ppermute | solution.py:332
  39.1 14.4 %collective-permute-start.8 = (bf16[784,128]{1,0:T(8,128)(2,1)S(1)}, bf16[784,128]{1,0:T(8,128)(2,1)S(1)}, u32[]{:S(2)}, u32[]{:S(2)}) collective-permute-start(bf16[784,128]{1,0:T(8,128)(2,1)S(1)} %get-tuple-element.44), channel_id=1, source_target_pairs={{0,24},{4,28},{8,16},{12,20},{16,8},{20,12},{24,0},{28,4},{1,25},{... | collective-permute-start | bytes 602120 | tf_op jit(solution)/shard_map/ppermute | solution.py:332
  53.6 30.2 %copy-start.4 = (bf16[672,640]{1,0:T(8,128)(2,1)}, bf16[672,640]{1,0:T(8,128)(2,1)S(1)}, u32[]{:S(2)}) copy-start(bf16[672,640]{1,0:T(8,128)(2,1)S(1)} %collective-permute-done.6.rest_4_.rest_7_) | copy-start | bytes 2580484
  53.6 24.7 %copy-start.12 = (bf16[672,640]{1,0:T(8,128)(2,1)}, bf16[672,640]{1,0:T(8,128)(2,1)S(1)}, u32[]{:S(2)}) copy-start(bf16[672,640]{1,0:T(8,128)(2,1)S(1)} %collective-permute-done.5.rest_10_.rest_9_) | copy-start | bytes 2580484
  53.6 24.7 %copy-start.13 = (bf16[672,640]{1,0:T(8,128)(2,1)}, bf16[672,640]{1,0:T(8,128)(2,1)S(1)}, u32[]{:S(2)}) copy-start(bf16[672,640]{1,0:T(8,128)(2,1)S(1)} %collective-permute-done.10.rest_9_.rest_6_) | copy-start | bytes 2580484
  53.6 2.5 %collective-permute-start.13 = (bf16[672,640]{1,0:T(8,128)(2,1)S(1)}, bf16[672,640]{1,0:T(8,128)(2,1)S(1)}, u32[]{:S(2)}, u32[]{:S(2)}) collective-permute-start(bf16[672,640]{1,0:T(8,128)(2,1)S(1)} %collective-permute-done.5.rest_10_.rest_9_), channel_id=1, source_target_pairs={{0,1},{1,0},{2,3},{3,2},{4,5},{5,4},{6,7},{7,6},{8,9},{9,8},{10,11... | collective-permute-start | bytes 2580488 | tf_op jit(solution)/shard_map/ppermute | solution.py:335
  53.7 27.6 %collective-permute-start.17 = (bf16[672,640]{1,0:T(8,128)(2,1)S(1)}, bf16[672,640]{1,0:T(8,128)(2,1)S(1)}, u32[]{:S(2)}, u32[]{:S(2)}) collective-permute-start(bf16[672,640]{1,0:T(8,128)(2,1)S(1)} %collective-permute-done.6.rest_4_.rest_7_), channel_id=1, source_target_pairs={{0,2},{1,3},{2,0},{3,1},{4,6},{5,7},{6,4},{7,5},{8,10},{9,11},{10,... | collective-permute-start | bytes 2580488 | tf_op jit(solution)/shard_map/ppermute | solution.py:335
  56.1 22.2 %copy-start.14 = (bf16[672,640]{1,0:T(8,128)(2,1)}, bf16[672,640]{1,0:T(8,128)(2,1)S(1)}, u32[]{:S(2)}) copy-start(bf16[672,640]{1,0:T(8,128)(2,1)S(1)} %collective-permute-done.13.rest_11_.rest_10_) | copy-start | bytes 2580484
  56.1 25.2 %collective-permute-start.16 = (bf16[672,640]{1,0:T(8,128)(2,1)S(1)}, bf16[672,640]{1,0:T(8,128)(2,1)S(1)}, u32[]{:S(2)}, u32[]{:S(2)}) collective-permute-start(bf16[672,640]{1,0:T(8,128)(2,1)S(1)} %collective-permute-done.6.rest_4_.rest_7_), channel_id=1, source_target_pairs={{0,1},{1,0},{2,3},{3,2},{4,5},{5,4},{6,7},{7,6},{8,9},{9,8},{10,11... | collective-permute-start | bytes 2580488 | tf_op jit(solution)/shard_map/ppermute | solution.py:335
  56.2 10.5 %collective-permute-start.12 = (bf16[784,128]{1,0:T(8,128)(2,1)S(1)}, bf16[784,128]{1,0:T(8,128)(2,1)S(1)}, u32[]{:S(2)}, u32[]{:S(2)}) collective-permute-start(bf16[784,128]{1,0:T(8,128)(2,1)S(1)} %get-tuple-element.50), channel_id=1, source_target_pairs={{0,28},{4,24},{8,20},{12,16},{16,12},{20,8},{24,4},{28,0},{1,29},{... | collective-permute-start | bytes 602120 | tf_op jit(solution)/shard_map/ppermute | solution.py:332
  58.4 13.5 %collective-permute-start.11 = (bf16[784,128]{1,0:T(8,128)(2,1)S(1)}, bf16[784,128]{1,0:T(8,128)(2,1)S(1)}, u32[]{:S(2)}, u32[]{:S(2)}) collective-permute-start(bf16[784,128]{1,0:T(8,128)(2,1)S(1)} %get-tuple-element.47), channel_id=1, source_target_pairs={{0,8},{4,12},{8,0},{12,4},{16,24},{20,28},{24,16},{28,20},{1,9},{5... | collective-permute-start | bytes 602120 | tf_op jit(solution)/shard_map/ppermute | solution.py:332
  62.9 16.4 %collective-permute-start.14 = (bf16[784,128]{1,0:T(8,128)(2,1)S(1)}, bf16[784,128]{1,0:T(8,128)(2,1)S(1)}, u32[]{:S(2)}, u32[]{:S(2)}) collective-permute-start(bf16[784,128]{1,0:T(8,128)(2,1)S(1)} %get-tuple-element.55), channel_id=1, source_target_pairs={{0,12},{4,8},{8,4},{12,0},{16,28},{20,24},{24,20},{28,16},{1,13},{... | collective-permute-start | bytes 602120 | tf_op jit(solution)/shard_map/ppermute | solution.py:332
  66.7 14.5 %collective-permute-start.15 = (bf16[784,128]{1,0:T(8,128)(2,1)S(1)}, bf16[784,128]{1,0:T(8,128)(2,1)S(1)}, u32[]{:S(2)}, u32[]{:S(2)}) collective-permute-start(bf16[784,128]{1,0:T(8,128)(2,1)S(1)} %get-tuple-element.57), channel_id=1, source_target_pairs={{0,20},{4,16},{8,28},{12,24},{16,4},{20,0},{24,12},{28,8},{1,21},{... | collective-permute-start | bytes 602120 | tf_op jit(solution)/shard_map/ppermute | solution.py:332
  78.3 1.0 copy-start.22
  81.3 6.8 %copy-start.5 = (bf16[672,640]{1,0:T(8,128)(2,1)}, bf16[672,640]{1,0:T(8,128)(2,1)S(1)}, u32[]{:S(2)}) copy-start(bf16[672,640]{1,0:T(8,128)(2,1)S(1)} %collective-permute-done.17.rest_6_.rest_11_) | copy-start | bytes 2580484
  81.3 6.8 %copy-start.6 = (bf16[672,640]{1,0:T(8,128)(2,1)}, bf16[672,640]{1,0:T(8,128)(2,1)S(1)}, u32[]{:S(2)}) copy-start(bf16[672,640]{1,0:T(8,128)(2,1)S(1)} %collective-permute-done.16.rest_5_.rest_8_) | copy-start | bytes 2580484
  81.3 2.5 %collective-permute-start.18 = (bf16[672,640]{1,0:T(8,128)(2,1)S(1)}, bf16[672,640]{1,0:T(8,128)(2,1)S(1)}, u32[]{:S(2)}, u32[]{:S(2)}) collective-permute-start(bf16[672,640]{1,0:T(8,128)(2,1)S(1)} %collective-permute-done.17.rest_6_.rest_11_), channel_id=1, source_target_pairs={{0,1},{1,0},{2,3},{3,2},{4,5},{5,4},{6,7},{7,6},{8,9},{9,8},{10,11... | collective-permute-start | bytes 2580488 | tf_op jit(solution)/shard_map/ppermute | solution.py:335
  83.8 4.3 %copy-start.7 = (bf16[672,640]{1,0:T(8,128)(2,1)}, bf16[672,640]{1,0:T(8,128)(2,1)S(1)}, u32[]{:S(2)}) copy-start(bf16[672,640]{1,0:T(8,128)(2,1)S(1)} %collective-permute-done.18.rest_7_.rest_12_) | copy-start | bytes 2580484
  88.1 0.9 copy-start.15
  89.0 1.2 collective-permute-start.19
  90.2 5.1 %collective-permute-start.21 = (f32[16,224]{1,0:T(8,128)S(1)}, f32[16,224]{1,0:T(8,128)S(1)}, u32[]{:S(2)}, u32[]{:S(2)}) collective-permute-start(f32[16,224]{1,0:T(8,128)S(1)} %pad_maximum_fusion.1), channel_id=1, source_target_pairs={{0,4},{4,0},{8,12},{12,8},{16,20},{20,16},{24,28},{28,24},{1,5},{5... | collective-permute-start | bytes 43016 | tf_op jit(solution)/shard_map/ppermute | solution.py:332
  90.2 5.0 %collective-permute-start.22 = (f32[8,224]{1,0:T(8,128)S(1)}, f32[8,224]{1,0:T(8,128)S(1)}, u32[]{:S(2)}, u32[]{:S(2)}) collective-permute-start(f32[8,224]{1,0:T(8,128)S(1)} %add.12), channel_id=1, source_target_pairs={{0,6},{1,7},{2,4},{3,5},{4,2},{5,3},{6,0},{7,1},{8,14},{9,15},{10,... | collective-permute-start | bytes 21512 | tf_op jit(solution)/shard_map/ppermute | solution.py:339
  93.6 3.7 %collective-permute-start.20 = (f32[8,224]{1,0:T(8,128)S(1)}, f32[8,224]{1,0:T(8,128)S(1)}, u32[]{:S(2)}, u32[]{:S(2)}) collective-permute-start(f32[8,224]{1,0:T(8,128)S(1)} %add.12), channel_id=1, source_target_pairs={{0,2},{1,3},{2,0},{3,1},{4,6},{5,7},{6,4},{7,5},{8,10},{9,11},{10,... | collective-permute-start | bytes 21512 | tf_op jit(solution)/shard_map/ppermute | solution.py:335
  97.3 6.7 %copy-start.23 = (f32[24,224]{1,0:T(8,128)}, f32[24,224]{1,0:T(8,128)S(1)}, u32[]{:S(2)}) copy-start(f32[24,224]{1,0:T(8,128)S(1)} %pad_maximum_fusion.rest_13_) | copy-start | bytes 64516
  97.3 5.7 %collective-permute-start.25 = (f32[24,224]{1,0:T(8,128)S(1)}, f32[24,224]{1,0:T(8,128)S(1)}, u32[]{:S(2)}, u32[]{:S(2)}) collective-permute-start(f32[24,224]{1,0:T(8,128)S(1)} %pad_maximum_fusion.rest_13_), channel_id=1, source_target_pairs={{0,24},{4,28},{8,16},{12,20},{16,8},{20,12},{24,0},{28,4},{1,25},{... | collective-permute-start | bytes 64520 | tf_op jit(solution)/shard_map/ppermute | solution.py:332
  99.2 4.7 %collective-permute-start.24 = (f32[24,224]{1,0:T(8,128)S(1)}, f32[24,224]{1,0:T(8,128)S(1)}, u32[]{:S(2)}, u32[]{:S(2)}) collective-permute-start(f32[24,224]{1,0:T(8,128)S(1)} %pad_maximum_fusion.rest_13_), channel_id=1, source_target_pairs={{0,16},{4,20},{8,24},{12,28},{16,0},{20,4},{24,8},{28,12},{1,17},{... | collective-permute-start | bytes 64520 | tf_op jit(solution)/shard_map/ppermute | solution.py:332
  99.2 4.7 %collective-permute-start.23 = (f32[24,224]{1,0:T(8,128)S(1)}, f32[24,224]{1,0:T(8,128)S(1)}, u32[]{:S(2)}, u32[]{:S(2)}) collective-permute-start(f32[24,224]{1,0:T(8,128)S(1)} %pad_maximum_fusion.rest_13_), channel_id=1, source_target_pairs={{0,8},{4,12},{8,0},{12,4},{16,24},{20,28},{24,16},{28,20},{1,9},{5... | collective-permute-start | bytes 64520 | tf_op jit(solution)/shard_map/ppermute | solution.py:332
  103.0 1.0 copy-start.24
  103.9 0.6 copy-start.25
  103.9 0.6 copy-start.26

commit v4 on v3

--- a/solution.py
+++ b/solution.py
@@ -216,13 +216,13 @@
     order = sum(groups, ())
     shards = len(order)
     hidden, rest = rest[:len(groups)], rest[len(groups):]
-    refs, rest = rest[:n_refs], rest[n_refs:]
+    refs, late_rows, rest = rest[:n_refs], rest[n_refs], rest[n_refs + 1:]
     notes, rest = rest[:shards // 2], rest[shards // 2:]
     ratio_out, grad_out, held, turned, scaled, result, sems, out_sems = rest
     dp, mp = my_place()
     quarters, wide = sems.shape[1], held.shape[1] // sems.shape[1]
     live_rows = notes[0].shape[1]
-    copies = fetch(pieces, refs, held, sems, order)
+    copies = fetch(pieces, refs, held, sems, groups[0])
     scale = SCALE / math.sqrt(quarters * wide)
     at = 0
     for part in hidden:
@@ -249,13 +249,14 @@
     columns = [jnp.sum(jnp.where(eye, coef[k:k + 1], 0.0), axis=1, keepdims=True) for k in order]
 
     def scale_rows(e):
-        for k in order:
-            copies[k, e].wait()
+        early = len(groups[0])
         for i in range(shards):
-            rows = slice(i * live_rows, (i + 1) * live_rows)
-            part = held[rows, e * wide:(e + 1) * wide].astype(jnp.float32)
-            scaled[e % 2, rows] = (columns[i] * part).astype(jnp.bfloat16)
-
+            source, at = (held, i) if i < early else (late_rows, i - early)
+            part = source[at * live_rows:(at + 1) * live_rows, e * wide:(e + 1) * wide].astype(jnp.float32)
+            scaled[e % 2, i * live_rows:(i + 1) * live_rows] = (columns[i] * part).astype(jnp.bfloat16)
+
+    for copy in copies.values():
+        copy.wait()
     writes = []
     scale_rows(0)
     for e in range(quarters):
@@ -307,7 +308,8 @@
     ("xy_n3", "h7", "h5", "h3", "h2", "c_x_n3", "c_y_n3", "early",),
     ("c_xy_n3",),
 )
-BESIDES = {"early": ("h7",), "c_xy_n3": ("early",)}
+BESIDES = {"h3": ("c_y_n3",), "early": ("h7",), "c_xy_n3": ("early",)}
+FREE = ()
 EARLY = (0, 1, 2, 6, 4, )
 LATE = (3, 7, 5, )
 
@@ -382,22 +384,22 @@
                     names.append("c_" + name if core else name)
         return [got[name] for name in names], places
 
-    groups = (EARLY, LATE) if EARLY else (LATE,)
-    turned = []
-
-    def shift_sums(slots, *before, gates=()):
+    groups = (EARLY, LATE)
+    turned, late_rows = [], []
+
+    def shift_sums(slots, *before, gates=(), keep=False):
         refs, places = used(slots)
         refs[0] = after(refs[0], gates)
-        sums, part = pl.pallas_call(
+        rows_shape = (len(slots) * live_rows, width)
+        sums, part, *kept = pl.pallas_call(
             functools.partial(shift_kernel, places, len(refs), slots, live_rows),
             out_shape=(
                 jax.ShapeDtypeStruct((shards, live_rows), f32),
                 jax.ShapeDtypeStruct((units, len(slots) * live_rows), bf16),
-            ),
+            ) + (jax.ShapeDtypeStruct(rows_shape, bf16),) * keep,
             in_specs=[ANY] * (1 + len(slots) + len(refs)) + [VMEM] * len(before),
-            out_specs=(VMEM, VMEM),
-            scratch_shapes=[
-                pltpu.VMEM((len(slots) * live_rows, width), bf16),
+            out_specs=(VMEM,) * (2 + keep),
+            scratch_shapes=[pltpu.VMEM(rows_shape, bf16)] * (not keep) + [
                 pltpu.VMEM((units, width), bf16),
                 pltpu.VMEM((len(slots), rows, 128), bf16),
                 pltpu.SemaphoreType.DMA((len(slots), quarters)),
@@ -408,6 +410,7 @@
             name="shift_sums",
         )(weight, *(got[f"h{k}"] for k in slots), *refs, *before)
         turned.append(part)
+        late_rows.extend(kept)
         return sums
 
     gates = ()
@@ -427,9 +430,10 @@
                 got[step] = (over_dp if axis == "dp" else over_mp)(
                     after(got[source], (*gates, *core, *BESIDES.get(step, ()))), m
                 )
-                moved.append(step)
+                if step not in FREE:
+                    moved.append(step)
         gates = tuple(moved)
-    sums = shift_sums(LATE, *([got["early"]] if EARLY else []))
+    sums = shift_sums(LATE, got["early"], keep=True)
 
     sums = sums + over_mp(sums, 1)
     table = got["table"]
@@ -441,28 +445,27 @@
     )
     notes = [note] + [over_dp(note, m) for m in (2, 4, 6)]
 
-    order = sum(groups, ())
-    refs, places = used(order)
+    refs, places = used(EARLY)
     log_ratio, weight_grad = pl.pallas_call(
         functools.partial(grad_kernel, places, len(refs), groups, slots_each, seglen),
         out_shape=(
             jax.ShapeDtypeStruct((seglen, shards * slots_each), f32),
             jax.ShapeDtypeStruct((units, width), f32),
         ),
-        in_specs=[VMEM] * len(groups) + [ANY] * len(refs) + [VMEM] * len(notes),
+        in_specs=[VMEM] * len(groups) + [ANY] * len(refs) + [VMEM] * (1 + len(notes)),
         out_specs=(VMEM, ANY),
         scratch_shapes=[
-            pltpu.VMEM((shards * live_rows, width), bf16),
+            pltpu.VMEM((len(EARLY) * live_rows, width), bf16),
             pltpu.VMEM((units, shards * live_rows), bf16),
             pltpu.VMEM((2, shards * live_rows, wide), bf16),
             pltpu.VMEM((quarters, units, wide), f32),
-            pltpu.SemaphoreType.DMA((shards, quarters)),
+            pltpu.SemaphoreType.DMA((len(EARLY), quarters)),
             pltpu.SemaphoreType.DMA((quarters,)),
         ],
-        compiler_params=room(56),
+        compiler_params=room(52),
         cost_estimate=cost(2 * units * shards * live_rows * width, 2 * shards * live_rows * width + 4 * units * width),
         name="weight_grad",
-    )(*turned, *refs, *notes)
+    )(*turned, *refs, *late_rows, *notes)
     return (log_ratio.T, weight_grad)
 
 

time: 118 us -> 117 us (level)
    unnamed x56 -> x40, local copies, waits for them, and re-layouts: 10.6 us -> 9.88 us
where the time goes in v4:
time: 117 us
  waiting for transfers between devices  40.8 us (35%)
  starting transfers between devices  39.5 us (34%)
  Pallas kernels  25.3 us (22%)
  local copies, waits for them, and re-layouts  9.96 us (9%)
    ppermute x16, waiting for transfers between devices, over_dp(): return lax.ppermute(x, 'dp', [(s, s ^ m) for s in range(shards)])  32.8 us
    ppermute x16, starting transfers between devices, over_dp(): return lax.ppermute(x, 'dp', [(s, s ^ m) for s in range(shards)])  32.7 us
    pallas_call x1, Pallas kernels, cube_body(): pl.pallas_call(functools.partial(grad_kernel, places, len(refs), groups,...  12 us
    pallas_call x2, Pallas kernels, shift_sums(): pl.pallas_call(functools.partial(shift_kernel, places, len(refs), slots,...  10.4 us
    unnamed x40, local copies, waits for them, and re-layouts  9.88 us
    ppermute x9, waiting for transfers between devices, over_mp(): return lax.ppermute(x, 'mp', [(s, s ^ m) for s in range(quarters)])  6.44 us
    ppermute x1, starting transfers between devices, over_both(): return lax.ppermute(x, ('dp', 'mp'), pairs)  3.45 us
    ppermute x9, starting transfers between devices, over_mp(): return lax.ppermute(x, 'mp', [(s, s ^ m) for s in range(quarters)])  3.33 us
  transfers between devices with their start and end apart: 26, of which 13 were waited for; matrix products, arithmetic and copies ran while one was open for 0% of the time, Pallas kernels for 7%

profile of v4, /device:TPU:0, one launch (start us, length us, event | category | flops | bytes accessed | tf_op | source)
XLA Modules:
  0.0 116.7 jit_solution(11470169175297740915)
XLA Ops:
  0.6 0.0 copy-start.1
  0.6 1.3 %copy-done.1 = bf16[256,2560]{1,0:T(8,128)(2,1)S(1)} copy-done((bf16[256,2560]{1,0:T(8,128)(2,1)S(1)}, bf16[256,2560]{1,0:T(8,128)(2,1)}, u32[]{:S(2)}) %copy-start.1) | copy-done | bytes 1310744
  2.0 0.7 copy-done.5
  2.6 0.9 pack_first.1
  3.5 3.0 %collective-permute-start.4 = (bf16[448,640]{1,0:T(8,128)(2,1)S(1)}, bf16[448,640]{1,0:T(8,128)(2,1)S(1)}, u32[]{:S(2)}, u32[]{:S(2)}) collective-permute-start(bf16[448,640]{1,0:T(8,128)(2,1)S(1)} %get-tuple-element.39), channel_id=1, source_target_pairs={{0,4},{4,0},{8,12},{12,8},{16,20},{20,16},{24,28},{28,24},{1,5},{5... | collective-permute-start | bytes 1720328 | tf_op jit(solution)/shard_map/ppermute | solution.py:334
  6.5 2.6 %collective-permute-start.3 = (bf16[224,640]{1,0:T(8,128)(2,1)S(1)}, bf16[224,640]{1,0:T(8,128)(2,1)S(1)}, u32[]{:S(2)}, u32[]{:S(2)}) collective-permute-start(bf16[224,640]{1,0:T(8,128)(2,1)S(1)} %get-tuple-element.38), channel_id=1, source_target_pairs={{0,16},{4,20},{8,24},{12,28},{16,0},{20,4},{24,8},{28,12},{1,17},{... | collective-permute-start | bytes 860168 | tf_op jit(solution)/shard_map/ppermute | solution.py:334
  9.1 1.3 %collective-permute-start.2 = (bf16[224,640]{1,0:T(8,128)(2,1)S(1)}, bf16[224,640]{1,0:T(8,128)(2,1)S(1)}, u32[]{:S(2)}, u32[]{:S(2)}) collective-permute-start(bf16[224,640]{1,0:T(8,128)(2,1)S(1)} %get-tuple-element.38), channel_id=1, source_target_pairs={{0,24},{4,28},{8,16},{12,20},{16,8},{20,12},{24,0},{28,4},{1,25},{... | collective-permute-start | bytes 860168 | tf_op jit(solution)/shard_map/ppermute | solution.py:334
  10.5 0.2 collective-permute-start.1
  10.7 1.3 %copy-done.2 = bf16[256,2560]{1,0:T(8,128)(2,1)S(1)} copy-done((bf16[256,2560]{1,0:T(8,128)(2,1)S(1)}, bf16[256,2560]{1,0:T(8,128)(2,1)}, u32[]{:S(2)}) %copy-start.2) | copy-done | bytes 1310744
  12.0 0.7 copy-done.6
  12.7 1.5 %copy-done.8 = bf16[256,3584]{1,0:T(8,128)(2,1)S(1)} copy-done((bf16[256,3584]{1,0:T(8,128)(2,1)S(1)}, bf16[256,3584]{1,0:T(8,128)(2,1)}, u32[]{:S(2)}) %copy-start.8) | copy-done | bytes 1835032
  14.2 0.7 copy-done.14
  14.9 0.7 copy-done.15
  15.5 0.7 copy-done.16
  16.2 0.7 copy-done.17
  16.8 2.0 %pack_rest.1 = (f32[8,224]{1,0:T(8,128)S(1)}, bf16[4,224,640]{2,1,0:T(8,128)(2,1)S(1)}, bf16[784,128]{1,0:T(8,128)(2,1)S(1)}, bf16[784,128]{1,0:T(8,128)(2,1)S(1...) custom-call(s32[1,32]{1,0:T(1,128)S(1)} %copy-done.6, ...), custom_call_target="tpu_custom_call" | custom-call | flops 2000000000 | bytes 8000000 | tf_op jit(solution)/shard_map/pack_rest/pallas_call | solution.py:360
  18.8 0.5 collective-permute-start
  19.4 5.4 %collective-permute-done.rest_1_ = bf16[784,128]{1,0:T(8,128)(2,1)S(1)} collective-permute-done((bf16[784,128]{1,0:T(8,128)(2,1)S(1)}, bf16[784,128]{1,0:T(8,128)(2,1)S(1)}, u32[]{:S(2)}, u32[]{:S(2)}) %collective-permute-start) | collective-permute-done | bytes 200736 | tf_op jit(solution)/shard_map/ppermute | solution.py:334
  24.7 4.5 %collective-permute-done.3 = bf16[224,640]{1,0:T(8,128)(2,1)S(1)} collective-permute-done((bf16[224,640]{1,0:T(8,128)(2,1)S(1)}, bf16[224,640]{1,0:T(8,128)(2,1)S(1)}, u32[]{:S(2)}, u32[]{:S(2)}) %collective-permute-start.3) | collective-permute-done | bytes 286752 | tf_op jit(solution)/shard_map/ppermute | solution.py:334
  29.2 0.0 collective-permute-done.2
  29.2 0.2 collective-permute-done.1
  29.4 0.0 collective-permute-done.4.rest_6_.rest_3_
  29.4 0.0 collective-permute-start.9
  29.5 0.5 collective-permute-start.6
  30.0 1.5 %collective-permute-start.5 = (bf16[672,640]{1,0:T(8,128)(2,1)S(1)}, bf16[672,640]{1,0:T(8,128)(2,1)S(1)}, u32[]{:S(2)}, u32[]{:S(2)}) collective-permute-start(bf16[672,640]{1,0:T(8,128)(2,1)S(1)} %constant_dynamic-update-slice_fusion.rest_8_.rest_5_), channel_id=1, source_target_pairs={{0,2},{1,3},{2,0},{3,1},{4,6},{5,7},{6,4},{7,5},{8,10},{9,11},{10,... | collective-permute-start | bytes 2580488 | tf_op jit(solution)/shard_map/ppermute | solution.py:337
  31.6 0.0 collective-permute-done.9.rest_7_.rest_4_
  31.6 0.0 collective-permute-start.10
  31.6 7.5 %collective-permute-start.7 = (bf16[784,128]{1,0:T(8,128)(2,1)S(1)}, bf16[784,128]{1,0:T(8,128)(2,1)S(1)}, u32[]{:S(2)}, u32[]{:S(2)}) collective-permute-start(bf16[784,128]{1,0:T(8,128)(2,1)S(1)} %get-tuple-element.43), channel_id=1, source_target_pairs={{0,16},{4,20},{8,24},{12,28},{16,0},{20,4},{24,8},{28,12},{1,17},{... | collective-permute-start | bytes 602120 | tf_op jit(solution)/shard_map/ppermute | solution.py:334
  39.1 0.4 collective-permute-start.8
  39.5 14.0 %collective-permute-done.7.rest_4_ = bf16[784,128]{1,0:T(8,128)(2,1)S(1)} collective-permute-done((bf16[784,128]{1,0:T(8,128)(2,1)S(1)}, bf16[784,128]{1,0:T(8,128)(2,1)S(1)}, u32[]{:S(2)}, u32[]{:S(2)}) %collective-permute-start.7) | collective-permute-done | bytes 200736 | tf_op jit(solution)/shard_map/ppermute | solution.py:334
  53.5 0.0 collective-permute-done.8.rest_3_
  53.5 0.0 collective-permute-done.6.rest_4_
  53.5 0.0 collective-permute-done.5.rest_10_.rest_7_
  53.5 0.0 collective-permute-done.10.rest_9_.rest_6_
  53.6 0.1 collective-permute-start.13
  53.6 1.3 %collective-permute-start.17 = (bf16[672,640]{1,0:T(8,128)(2,1)S(1)}, bf16[672,640]{1,0:T(8,128)(2,1)S(1)}, u32[]{:S(2)}, u32[]{:S(2)}) collective-permute-start(bf16[672,640]{1,0:T(8,128)(2,1)S(1)} %collective-permute-done.6.rest_4_), channel_id=1, source_target_pairs={{0,2},{1,3},{2,0},{3,1},{4,6},{5,7},{6,4},{7,5},{8,10},{9,11},{10,... | collective-permute-start | bytes 2580488 | tf_op jit(solution)/shard_map/ppermute | solution.py:337
  55.0 1.0 collective-permute-done.13.rest_11_.rest_8_
  56.0 0.1 collective-permute-start.16
  56.1 2.2 %collective-permute-start.12 = (bf16[784,128]{1,0:T(8,128)(2,1)S(1)}, bf16[784,128]{1,0:T(8,128)(2,1)S(1)}, u32[]{:S(2)}, u32[]{:S(2)}) collective-permute-start(bf16[784,128]{1,0:T(8,128)(2,1)S(1)} %get-tuple-element.51), channel_id=1, source_target_pairs={{0,28},{4,24},{8,20},{12,16},{16,12},{20,8},{24,4},{28,0},{1,29},{... | collective-permute-start | bytes 602120 | tf_op jit(solution)/shard_map/ppermute | solution.py:334
  58.4 4.5 %collective-permute-start.11 = (bf16[784,128]{1,0:T(8,128)(2,1)S(1)}, bf16[784,128]{1,0:T(8,128)(2,1)S(1)}, u32[]{:S(2)}, u32[]{:S(2)}) collective-permute-start(bf16[784,128]{1,0:T(8,128)(2,1)S(1)} %get-tuple-element.48), channel_id=1, source_target_pairs={{0,8},{4,12},{8,0},{12,4},{16,24},{20,28},{24,16},{28,20},{1,9},{5... | collective-permute-start | bytes 602120 | tf_op jit(solution)/shard_map/ppermute | solution.py:334
  62.9 0.0 collective-permute-start.14
  62.9 3.8 %collective-permute-done.12.rest_1_ = bf16[784,128]{1,0:T(8,128)(2,1)S(1)} collective-permute-done((bf16[784,128]{1,0:T(8,128)(2,1)S(1)}, bf16[784,128]{1,0:T(8,128)(2,1)S(1)}, u32[]{:S(2)}, u32[]{:S(2)}) %collective-permute-start.12) | collective-permute-done | bytes 200736 | tf_op jit(solution)/shard_map/ppermute | solution.py:334
  66.7 5.3 %collective-permute-start.15 = (bf16[784,128]{1,0:T(8,128)(2,1)S(1)}, bf16[784,128]{1,0:T(8,128)(2,1)S(1)}, u32[]{:S(2)}, u32[]{:S(2)}) collective-permute-start(bf16[784,128]{1,0:T(8,128)(2,1)S(1)} %get-tuple-element.58), channel_id=1, source_target_pairs={{0,20},{4,16},{8,28},{12,24},{16,4},{20,0},{24,12},{28,8},{1,21},{... | collective-permute-start | bytes 602120 | tf_op jit(solution)/shard_map/ppermute | solution.py:334
  71.9 0.0 collective-permute-done.11.rest_2_
  71.9 6.3 %shift_sums.2 = (f32[8,224]{1,0:T(8,128)S(1)}, bf16[448,1120]{1,0:T(8,128)(2,1)S(1)}) custom-call(bf16[448,2560]{1,0:T(8,128)(2,1)S(1)} %copy-done, bf16[784,128]{1,0:T(8,128)(2,1)S(1)} %get-tuple-element.35.rest_0_, bf16[784,128]{1,0:T(8,128)(2,1)S(1)} %collective-permute-done.rest_1_, bf16[784,128]{1,0:T(8,128)(2,1)S(1)} %collective-permute-done.11.rest_2_, ...), custom_call_target="tpu_custom_call" | custom-call | flops 2569011200 | bytes 5734400 | tf_op jit(solution)/shard_map/shift_sums/pallas_call | solution.py:394
  78.3 0.0 collective-permute-done.14.rest_0_
  78.4 2.9 %collective-permute-done.15.rest_2_ = bf16[784,128]{1,0:T(8,128)(2,1)S(1)} collective-permute-done((bf16[784,128]{1,0:T(8,128)(2,1)S(1)}, bf16[784,128]{1,0:T(8,128)(2,1)S(1)}, u32[]{:S(2)}, u32[]{:S(2)}) %collective-permute-start.15) | collective-permute-done | bytes 200736 | tf_op jit(solution)/shard_map/ppermute | solution.py:334
  81.3 0.1 collective-permute-start.18
  81.4 2.4 %collective-permute-done.18.rest_7_ = bf16[672,640]{1,0:T(8,128)(2,1)S(1)} collective-permute-done((bf16[672,640]{1,0:T(8,128)(2,1)S(1)}, bf16[672,640]{1,0:T(8,128)(2,1)S(1)}, u32[]{:S(2)}, u32[]{:S(2)}) %collective-permute-start.18) | collective-permute-done | bytes 860192 | tf_op jit(solution)/shard_map/ppermute | solution.py:337
  83.8 4.1 %shift_sums.3 = (f32[8,224]{1,0:T(8,128)S(1)}, bf16[448,672]{1,0:T(8,128)(2,1)S(1)}, bf16[672,2560]{1,0:T(8,128)(2,1)S(1)}) custom-call(bf16[448,2560]{1,0:T(8,128)(2,1)S(1)} %copy-done, bf16[784,128]{1,0:T(8,128)(2,1)S(1)} %collective-permute-done.14.rest_0_, bf16[784,128]{1,0:T(8,128)(2,1)S(1)} %collective-permute-done.12.rest_1_, ...), custom_call_target="tpu_custom_call" | custom-call | flops 1541406720 | bytes 3440640 | tf_op jit(solution)/shard_map/shift_sums/pallas_call | solution.py:394
  87.9 1.7 %copy-done.7 = bf16[672,2560]{1,0:T(8,128)(2,1)} copy-done((bf16[672,2560]{1,0:T(8,128)(2,1)}, bf16[672,2560]{1,0:T(8,128)(2,1)S(1)}, u32[]{:S(2)}) %copy-start.7) | copy-done | bytes 3440664
  89.6 0.1 collective-permute-start.19
  89.7 1.0 collective-permute-done.19
  90.8 0.1 collective-permute-start.21
  90.9 3.4 %collective-permute-start.22 = (f32[8,224]{1,0:T(8,128)S(1)}, f32[8,224]{1,0:T(8,128)S(1)}, u32[]{:S(2)}, u32[]{:S(2)}) collective-permute-start(f32[8,224]{1,0:T(8,128)S(1)} %add.12), channel_id=1, source_target_pairs={{0,6},{1,7},{2,4},{3,5},{4,2},{5,3},{6,0},{7,1},{8,14},{9,15},{10,... | collective-permute-start | bytes 21512 | tf_op jit(solution)/shard_map/ppermute | solution.py:341
  94.3 0.0 collective-permute-start.20
  94.3 1.6 %collective-permute-done.22 = f32[8,224]{1,0:T(8,128)S(1)} collective-permute-done((f32[8,224]{1,0:T(8,128)S(1)}, f32[8,224]{1,0:T(8,128)S(1)}, u32[]{:S(2)}, u32[]{:S(2)}) %collective-permute-start.22) | collective-permute-done | bytes 7200 | tf_op jit(solution)/shard_map/ppermute | solution.py:341
  95.9 0.0 collective-permute-done.21
  96.0 2.0 %collective-permute-done.20 = f32[8,224]{1,0:T(8,128)S(1)} collective-permute-done((f32[8,224]{1,0:T(8,128)S(1)}, f32[8,224]{1,0:T(8,128)S(1)}, u32[]{:S(2)}, u32[]{:S(2)}) %collective-permute-start.20) | collective-permute-done | bytes 7200 | tf_op jit(solution)/shard_map/ppermute | solution.py:337
  98.0 1.7 %collective-permute-start.25 = (f32[24,224]{1,0:T(8,128)S(1)}, f32[24,224]{1,0:T(8,128)S(1)}, u32[]{:S(2)}, u32[]{:S(2)}) collective-permute-start(f32[24,224]{1,0:T(8,128)S(1)} %pad_maximum_fusion.rest_10_), channel_id=1, source_target_pairs={{0,24},{4,28},{8,16},{12,20},{16,8},{20,12},{24,0},{28,4},{1,25},{... | collective-permute-start | bytes 64520 | tf_op jit(solution)/shard_map/ppermute | solution.py:334
  99.7 2.7 %collective-permute-start.23 = (f32[24,224]{1,0:T(8,128)S(1)}, f32[24,224]{1,0:T(8,128)S(1)}, u32[]{:S(2)}, u32[]{:S(2)}) collective-permute-start(f32[24,224]{1,0:T(8,128)S(1)} %pad_maximum_fusion.rest_10_), channel_id=1, source_target_pairs={{0,8},{4,12},{8,0},{12,4},{16,24},{20,28},{24,16},{28,20},{1,9},{5... | collective-permute-start | bytes 64520 | tf_op jit(solution)/shard_map/ppermute | solution.py:334
  102.4 1.2 %collective-permute-done.25.rest_13_ = f32[24,224]{1,0:T(8,128)S(1)} collective-permute-done((f32[24,224]{1,0:T(8,128)S(1)}, f32[24,224]{1,0:T(8,128)S(1)}, u32[]{:S(2)}, u32[]{:S(2)}) %collective-permute-start.25) | collective-permute-done | bytes 21536 | tf_op jit(solution)/shard_map/ppermute | solution.py:334
  103.7 0.8 collective-permute-done.24.rest_12_
  104.5 12.0 %weight_grad.1 = (f32[8,64]{1,0:T(8,128)}, f32[448,2560]{1,0:T(8,128)}) custom-call(bf16[448,1120]{1,0:T(8,128)(2,1)} %copy-done.18, bf16[448,672]{1,0:T(8,128)(2,1)S(1)} %get-tuple-element.63.rest_1_, bf16[4,224,640]{2,1,0:T(8,128)(2,1)} %copy-done.3, bf16[448,640]{1,0:T(8,128)(2,1)S(1)} %collective-permute-done.4.rest_6_.rest_3_, ...), custom_call_target="tpu_custom_call" | custom-call | flops 4110417920 | bytes 13762560 | tf_op jit(solution)/shard_map/weight_grad/pallas_call | solution.py:449
  (41 shorter events, 0.2 us)
Async XLA Ops:
  0.6 1.3 %copy-start.1 = (bf16[256,2560]{1,0:T(8,128)(2,1)S(1)}, bf16[256,2560]{1,0:T(8,128)(2,1)}, u32[]{:S(2)}) copy-start(bf16[256,2560]{1,0:T(8,128)(2,1)} %read.3) | copy-start | bytes 3932164
  1.9 0.7 copy-start.5
  3.5 25.9 %collective-permute-start.4 = (bf16[448,640]{1,0:T(8,128)(2,1)S(1)}, bf16[448,640]{1,0:T(8,128)(2,1)S(1)}, u32[]{:S(2)}, u32[]{:S(2)}) collective-permute-start(bf16[448,640]{1,0:T(8,128)(2,1)S(1)} %get-tuple-element.39), channel_id=1, source_target_pairs={{0,4},{4,0},{8,12},{12,8},{16,20},{20,16},{24,28},{28,24},{1,5},{5... | collective-permute-start | bytes 1720328 | tf_op jit(solution)/shard_map/ppermute | solution.py:334
  6.5 22.7 %collective-permute-start.3 = (bf16[224,640]{1,0:T(8,128)(2,1)S(1)}, bf16[224,640]{1,0:T(8,128)(2,1)S(1)}, u32[]{:S(2)}, u32[]{:S(2)}) collective-permute-start(bf16[224,640]{1,0:T(8,128)(2,1)S(1)} %get-tuple-element.38), channel_id=1, source_target_pairs={{0,16},{4,20},{8,24},{12,28},{16,0},{20,4},{24,8},{28,12},{1,17},{... | collective-permute-start | bytes 860168 | tf_op jit(solution)/shard_map/ppermute | solution.py:334
  9.1 20.1 %collective-permute-start.2 = (bf16[224,640]{1,0:T(8,128)(2,1)S(1)}, bf16[224,640]{1,0:T(8,128)(2,1)S(1)}, u32[]{:S(2)}, u32[]{:S(2)}) collective-permute-start(bf16[224,640]{1,0:T(8,128)(2,1)S(1)} %get-tuple-element.38), channel_id=1, source_target_pairs={{0,24},{4,28},{8,16},{12,20},{16,8},{20,12},{24,0},{28,4},{1,25},{... | collective-permute-start | bytes 860168 | tf_op jit(solution)/shard_map/ppermute | solution.py:334
  10.5 18.9 %collective-permute-start.1 = (bf16[224,640]{1,0:T(8,128)(2,1)S(1)}, bf16[224,640]{1,0:T(8,128)(2,1)S(1)}, u32[]{:S(2)}, u32[]{:S(2)}) collective-permute-start(bf16[224,640]{1,0:T(8,128)(2,1)S(1)} %get-tuple-element.38), channel_id=1, source_target_pairs={{0,8},{4,12},{8,0},{12,4},{16,24},{20,28},{24,16},{28,20},{1,9},{5... | collective-permute-start | bytes 860168 | tf_op jit(solution)/shard_map/ppermute | solution.py:334
  10.7 1.3 %copy-start.2 = (bf16[256,2560]{1,0:T(8,128)(2,1)S(1)}, bf16[256,2560]{1,0:T(8,128)(2,1)}, u32[]{:S(2)}) copy-start(bf16[256,2560]{1,0:T(8,128)(2,1)} %read.3) | copy-start | bytes 3932164
  12.0 0.7 copy-start.6
  12.7 1.5 %copy-start.8 = (bf16[256,3584]{1,0:T(8,128)(2,1)S(1)}, bf16[256,3584]{1,0:T(8,128)(2,1)}, u32[]{:S(2)}) copy-start(bf16[256,3584]{1,0:T(8,128)(2,1)} %hidden.1) | copy-start | bytes 5505028
  14.2 0.7 copy-start.14
  14.9 0.7 copy-start.15
  15.5 0.7 copy-start.16
  16.2 0.7 copy-start.17
  16.8 55.1 %copy-start = (bf16[448,2560]{1,0:T(8,128)(2,1)S(1)}, bf16[448,2560]{1,0:T(8,128)(2,1)}, u32[]{:S(2)}) copy-start(bf16[448,2560]{1,0:T(8,128)(2,1)} %weight.3) | copy-start | bytes 6881284
  18.8 65.0 %copy-start.3 = (bf16[4,224,640]{2,1,0:T(8,128)(2,1)}, bf16[4,224,640]{2,1,0:T(8,128)(2,1)S(1)}, u32[]{:S(2)}) copy-start(bf16[4,224,640]{2,1,0:T(8,128)(2,1)S(1)} %get-tuple-element.52.rest_5_.rest_3_.rest_2_) | copy-start | bytes 3440644
  18.8 5.9 %collective-permute-start = (bf16[784,128]{1,0:T(8,128)(2,1)S(1)}, bf16[784,128]{1,0:T(8,128)(2,1)S(1)}, u32[]{:S(2)}, u32[]{:S(2)}) collective-permute-start(bf16[784,128]{1,0:T(8,128)(2,1)S(1)} %get-tuple-element.36), channel_id=1, source_target_pairs={{0,4},{4,0},{8,12},{12,8},{16,20},{20,16},{24,28},{28,24},{1,5},{5... | collective-permute-start | bytes 602120 | tf_op jit(solution)/shard_map/ppermute | solution.py:334
  29.4 2.2 %collective-permute-start.9 = (bf16[448,640]{1,0:T(8,128)(2,1)S(1)}, bf16[448,640]{1,0:T(8,128)(2,1)S(1)}, u32[]{:S(2)}, u32[]{:S(2)}) collective-permute-start(bf16[448,640]{1,0:T(8,128)(2,1)S(1)} %collective-permute-done.4.rest_6_.rest_3_), channel_id=1, source_target_pairs={{0,1},{1,0},{2,3},{3,2},{4,5},{5,4},{6,7},{7,6},{8,9},{9,8},{10,11... | collective-permute-start | bytes 1720328 | tf_op jit(solution)/shard_map/ppermute | solution.py:337
  29.5 48.8 %copy-start.4 = (bf16[672,640]{1,0:T(8,128)(2,1)}, bf16[672,640]{1,0:T(8,128)(2,1)S(1)}, u32[]{:S(2)}) copy-start(bf16[672,640]{1,0:T(8,128)(2,1)S(1)} %constant_dynamic-update-slice_fusion.rest_8_.rest_5_) | copy-start | bytes 2580484
  29.5 24.0 %collective-permute-start.6 = (bf16[672,640]{1,0:T(8,128)(2,1)S(1)}, bf16[672,640]{1,0:T(8,128)(2,1)S(1)}, u32[]{:S(2)}, u32[]{:S(2)}) collective-permute-start(bf16[672,640]{1,0:T(8,128)(2,1)S(1)} %constant_dynamic-update-slice_fusion.rest_8_.rest_5_), channel_id=1, source_target_pairs={{0,4},{4,0},{8,12},{12,8},{16,20},{20,16},{24,28},{28,24},{1,5},{5... | collective-permute-start | bytes 2580488 | tf_op jit(solution)/shard_map/ppermute | solution.py:334
  30.0 23.5 %collective-permute-start.5 = (bf16[672,640]{1,0:T(8,128)(2,1)S(1)}, bf16[672,640]{1,0:T(8,128)(2,1)S(1)}, u32[]{:S(2)}, u32[]{:S(2)}) collective-permute-start(bf16[672,640]{1,0:T(8,128)(2,1)S(1)} %constant_dynamic-update-slice_fusion.rest_8_.rest_5_), channel_id=1, source_target_pairs={{0,2},{1,3},{2,0},{3,1},{4,6},{5,7},{6,4},{7,5},{8,10},{9,11},{10,... | collective-permute-start | bytes 2580488 | tf_op jit(solution)/shard_map/ppermute | solution.py:337
  31.6 46.7 %copy-start.12 = (bf16[448,640]{1,0:T(8,128)(2,1)}, bf16[448,640]{1,0:T(8,128)(2,1)S(1)}, u32[]{:S(2)}) copy-start(bf16[448,640]{1,0:T(8,128)(2,1)S(1)} %collective-permute-done.9.rest_7_.rest_4_) | copy-start | bytes 1720324
  31.6 22.0 %collective-permute-start.10 = (bf16[672,640]{1,0:T(8,128)(2,1)S(1)}, bf16[672,640]{1,0:T(8,128)(2,1)S(1)}, u32[]{:S(2)}, u32[]{:S(2)}) collective-permute-start(bf16[672,640]{1,0:T(8,128)(2,1)S(1)} %constant_dynamic-update-slice_fusion.rest_8_.rest_5_), channel_id=1, source_target_pairs={{0,1},{1,0},{2,3},{3,2},{4,5},{5,4},{6,7},{7,6},{8,9},{9,8},{10,11... | collective-permute-start | bytes 2580488 | tf_op jit(solution)/shard_map/ppermute | solution.py:337
  31.6 21.9 %collective-permute-start.7 = (bf16[784,128]{1,0:T(8,128)(2,1)S(1)}, bf16[784,128]{1,0:T(8,128)(2,1)S(1)}, u32[]{:S(2)}, u32[]{:S(2)}) collective-permute-start(bf16[784,128]{1,0:T(8,128)(2,1)S(1)} %get-tuple-element.43), channel_id=1, source_target_pairs={{0,16},{4,20},{8,24},{12,28},{16,0},{20,4},{24,8},{28,12},{1,17},{... | collective-permute-start | bytes 602120 | tf_op jit(solution)/shard_map/ppermute | solution.py:334
  39.1 14.4 %collective-permute-start.8 = (bf16[784,128]{1,0:T(8,128)(2,1)S(1)}, bf16[784,128]{1,0:T(8,128)(2,1)S(1)}, u32[]{:S(2)}, u32[]{:S(2)}) collective-permute-start(bf16[784,128]{1,0:T(8,128)(2,1)S(1)} %get-tuple-element.45), channel_id=1, source_target_pairs={{0,24},{4,28},{8,16},{12,20},{16,8},{20,12},{24,0},{28,4},{1,25},{... | collective-permute-start | bytes 602120 | tf_op jit(solution)/shard_map/ppermute | solution.py:334
  53.5 24.8 %copy-start.9 = (bf16[672,640]{1,0:T(8,128)(2,1)}, bf16[672,640]{1,0:T(8,128)(2,1)S(1)}, u32[]{:S(2)}) copy-start(bf16[672,640]{1,0:T(8,128)(2,1)S(1)} %collective-permute-done.5.rest_10_.rest_7_) | copy-start | bytes 2580484
  53.5 24.8 %copy-start.10 = (bf16[672,640]{1,0:T(8,128)(2,1)}, bf16[672,640]{1,0:T(8,128)(2,1)S(1)}, u32[]{:S(2)}) copy-start(bf16[672,640]{1,0:T(8,128)(2,1)S(1)} %collective-permute-done.10.rest_9_.rest_6_) | copy-start | bytes 2580484
  53.6 2.5 %collective-permute-start.13 = (bf16[672,640]{1,0:T(8,128)(2,1)S(1)}, bf16[672,640]{1,0:T(8,128)(2,1)S(1)}, u32[]{:S(2)}, u32[]{:S(2)}) collective-permute-start(bf16[672,640]{1,0:T(8,128)(2,1)S(1)} %collective-permute-done.5.rest_10_.rest_7_), channel_id=1, source_target_pairs={{0,1},{1,0},{2,3},{3,2},{4,5},{5,4},{6,7},{7,6},{8,9},{9,8},{10,11... | collective-permute-start | bytes 2580488 | tf_op jit(solution)/shard_map/ppermute | solution.py:337
  53.6 27.7 %collective-permute-start.17 = (bf16[672,640]{1,0:T(8,128)(2,1)S(1)}, bf16[672,640]{1,0:T(8,128)(2,1)S(1)}, u32[]{:S(2)}, u32[]{:S(2)}) collective-permute-start(bf16[672,640]{1,0:T(8,128)(2,1)S(1)} %collective-permute-done.6.rest_4_), channel_id=1, source_target_pairs={{0,2},{1,3},{2,0},{3,1},{4,6},{5,7},{6,4},{7,5},{8,10},{9,11},{10,... | collective-permute-start | bytes 2580488 | tf_op jit(solution)/shard_map/ppermute | solution.py:337
  56.0 22.3 %copy-start.11 = (bf16[672,640]{1,0:T(8,128)(2,1)}, bf16[672,640]{1,0:T(8,128)(2,1)S(1)}, u32[]{:S(2)}) copy-start(bf16[672,640]{1,0:T(8,128)(2,1)S(1)} %collective-permute-done.13.rest_11_.rest_8_) | copy-start | bytes 2580484
  56.0 25.3 %collective-permute-start.16 = (bf16[672,640]{1,0:T(8,128)(2,1)S(1)}, bf16[672,640]{1,0:T(8,128)(2,1)S(1)}, u32[]{:S(2)}, u32[]{:S(2)}) collective-permute-start(bf16[672,640]{1,0:T(8,128)(2,1)S(1)} %collective-permute-done.6.rest_4_), channel_id=1, source_target_pairs={{0,1},{1,0},{2,3},{3,2},{4,5},{5,4},{6,7},{7,6},{8,9},{9,8},{10,11... | collective-permute-start | bytes 2580488 | tf_op jit(solution)/shard_map/ppermute | solution.py:337
  56.1 10.5 %collective-permute-start.12 = (bf16[784,128]{1,0:T(8,128)(2,1)S(1)}, bf16[784,128]{1,0:T(8,128)(2,1)S(1)}, u32[]{:S(2)}, u32[]{:S(2)}) collective-permute-start(bf16[784,128]{1,0:T(8,128)(2,1)S(1)} %get-tuple-element.51), channel_id=1, source_target_pairs={{0,28},{4,24},{8,20},{12,16},{16,12},{20,8},{24,4},{28,0},{1,29},{... | collective-permute-start | bytes 602120 | tf_op jit(solution)/shard_map/ppermute | solution.py:334
  58.4 13.5 %collective-permute-start.11 = (bf16[784,128]{1,0:T(8,128)(2,1)S(1)}, bf16[784,128]{1,0:T(8,128)(2,1)S(1)}, u32[]{:S(2)}, u32[]{:S(2)}) collective-permute-start(bf16[784,128]{1,0:T(8,128)(2,1)S(1)} %get-tuple-element.48), channel_id=1, source_target_pairs={{0,8},{4,12},{8,0},{12,4},{16,24},{20,28},{24,16},{28,20},{1,9},{5... | collective-permute-start | bytes 602120 | tf_op jit(solution)/shard_map/ppermute | solution.py:334
  62.9 15.5 %collective-permute-start.14 = (bf16[784,128]{1,0:T(8,128)(2,1)S(1)}, bf16[784,128]{1,0:T(8,128)(2,1)S(1)}, u32[]{:S(2)}, u32[]{:S(2)}) collective-permute-start(bf16[784,128]{1,0:T(8,128)(2,1)S(1)} %get-tuple-element.56), channel_id=1, source_target_pairs={{0,12},{4,8},{8,4},{12,0},{16,28},{20,24},{24,20},{28,16},{1,13},{... | collective-permute-start | bytes 602120 | tf_op jit(solution)/shard_map/ppermute | solution.py:334
  66.7 14.6 %collective-permute-start.15 = (bf16[784,128]{1,0:T(8,128)(2,1)S(1)}, bf16[784,128]{1,0:T(8,128)(2,1)S(1)}, u32[]{:S(2)}, u32[]{:S(2)}) collective-permute-start(bf16[784,128]{1,0:T(8,128)(2,1)S(1)} %get-tuple-element.58), channel_id=1, source_target_pairs={{0,20},{4,16},{8,28},{12,24},{16,4},{20,0},{24,12},{28,8},{1,21},{... | collective-permute-start | bytes 602120 | tf_op jit(solution)/shard_map/ppermute | solution.py:334
  78.3 9.5 %copy-start.18 = (bf16[448,1120]{1,0:T(8,128)(2,1)}, bf16[448,1120]{1,0:T(8,128)(2,1)S(1)}, u32[]{:S(2)}) copy-start(bf16[448,1120]{1,0:T(8,128)(2,1)S(1)} %get-tuple-element.54.rest_0_) | copy-start | bytes 3010564
  81.3 23.2 %copy-start.13 = (bf16[448,640]{1,0:T(8,128)(2,1)S(1)}, bf16[448,640]{1,0:T(8,128)(2,1)}, u32[]{:S(2)}) copy-start(bf16[448,640]{1,0:T(8,128)(2,1)} %copy-done.12) | copy-start | bytes 1720324
  81.3 2.5 %collective-permute-start.18 = (bf16[672,640]{1,0:T(8,128)(2,1)S(1)}, bf16[672,640]{1,0:T(8,128)(2,1)S(1)}, u32[]{:S(2)}, u32[]{:S(2)}) collective-permute-start(bf16[672,640]{1,0:T(8,128)(2,1)S(1)} %collective-permute-done.17.rest_6_), channel_id=1, source_target_pairs={{0,1},{1,0},{2,3},{3,2},{4,5},{5,4},{6,7},{7,6},{8,9},{9,8},{10,11... | collective-permute-start | bytes 2580488 | tf_op jit(solution)/shard_map/ppermute | solution.py:337
  87.9 1.7 %copy-start.7 = (bf16[672,2560]{1,0:T(8,128)(2,1)}, bf16[672,2560]{1,0:T(8,128)(2,1)S(1)}, u32[]{:S(2)}) copy-start(bf16[672,2560]{1,0:T(8,128)(2,1)S(1)} %get-tuple-element.64.rest_9_) | copy-start | bytes 10321924
  89.6 1.2 %collective-permute-start.19 = (f32[8,224]{1,0:T(8,128)S(1)}, f32[8,224]{1,0:T(8,128)S(1)}, u32[]{:S(2)}, u32[]{:S(2)}) collective-permute-start(f32[8,224]{1,0:T(8,128)S(1)} %get-tuple-element.65), channel_id=1, source_target_pairs={{0,1},{1,0},{2,3},{3,2},{4,5},{5,4},{6,7},{7,6},{8,9},{9,8},{10,11... | collective-permute-start | bytes 21512 | tf_op jit(solution)/shard_map/ppermute | solution.py:337
  90.8 5.2 %collective-permute-start.21 = (f32[16,224]{1,0:T(8,128)S(1)}, f32[16,224]{1,0:T(8,128)S(1)}, u32[]{:S(2)}, u32[]{:S(2)}) collective-permute-start(f32[16,224]{1,0:T(8,128)S(1)} %pad_maximum_fusion.1), channel_id=1, source_target_pairs={{0,4},{4,0},{8,12},{12,8},{16,20},{20,16},{24,28},{28,24},{1,5},{5... | collective-permute-start | bytes 43016 | tf_op jit(solution)/shard_map/ppermute | solution.py:334
  90.9 5.1 %collective-permute-start.22 = (f32[8,224]{1,0:T(8,128)S(1)}, f32[8,224]{1,0:T(8,128)S(1)}, u32[]{:S(2)}, u32[]{:S(2)}) collective-permute-start(f32[8,224]{1,0:T(8,128)S(1)} %add.12), channel_id=1, source_target_pairs={{0,6},{1,7},{2,4},{3,5},{4,2},{5,3},{6,0},{7,1},{8,14},{9,15},{10,... | collective-permute-start | bytes 21512 | tf_op jit(solution)/shard_map/ppermute | solution.py:341
  94.3 3.7 %collective-permute-start.20 = (f32[8,224]{1,0:T(8,128)S(1)}, f32[8,224]{1,0:T(8,128)S(1)}, u32[]{:S(2)}, u32[]{:S(2)}) collective-permute-start(f32[8,224]{1,0:T(8,128)S(1)} %add.12), channel_id=1, source_target_pairs={{0,2},{1,3},{2,0},{3,1},{4,6},{5,7},{6,4},{7,5},{8,10},{9,11},{10,... | collective-permute-start | bytes 21512 | tf_op jit(solution)/shard_map/ppermute | solution.py:337
  98.0 5.7 %collective-permute-start.25 = (f32[24,224]{1,0:T(8,128)S(1)}, f32[24,224]{1,0:T(8,128)S(1)}, u32[]{:S(2)}, u32[]{:S(2)}) collective-permute-start(f32[24,224]{1,0:T(8,128)S(1)} %pad_maximum_fusion.rest_10_), channel_id=1, source_target_pairs={{0,24},{4,28},{8,16},{12,20},{16,8},{20,12},{24,0},{28,4},{1,25},{... | collective-permute-start | bytes 64520 | tf_op jit(solution)/shard_map/ppermute | solution.py:334
  99.7 4.8 %collective-permute-start.24 = (f32[24,224]{1,0:T(8,128)S(1)}, f32[24,224]{1,0:T(8,128)S(1)}, u32[]{:S(2)}, u32[]{:S(2)}) collective-permute-start(f32[24,224]{1,0:T(8,128)S(1)} %pad_maximum_fusion.rest_10_), channel_id=1, source_target_pairs={{0,16},{4,20},{8,24},{12,28},{16,0},{20,4},{24,8},{28,12},{1,17},{... | collective-permute-start | bytes 64520 | tf_op jit(solution)/shard_map/ppermute | solution.py:334
  99.7 4.8 %collective-permute-start.23 = (f32[24,224]{1,0:T(8,128)S(1)}, f32[24,224]{1,0:T(8,128)S(1)}, u32[]{:S(2)}, u32[]{:S(2)}) collective-permute-start(f32[24,224]{1,0:T(8,128)S(1)} %pad_maximum_fusion.rest_10_), channel_id=1, source_target_pairs={{0,8},{4,12},{8,0},{12,4},{16,24},{20,28},{24,16},{28,20},{1,9},{5... | collective-permute-start | bytes 64520 | tf_op jit(solution)/shard_map/ppermute | solution.py:334

commit v5 on v4

--- a/solution.py
+++ b/solution.py
@@ -143,16 +143,21 @@
 
 
 def fetch(pieces, refs, held, sems, slots):
-    copies = {}
+    copies = []
     quarters = sems.shape[1]
     live_rows, wide = held.shape[0] // len(slots), held.shape[1] // quarters
     for e in range(quarters):
-        for i, k in enumerate(slots):
-            ref, at = pieces[k, e]
-            source = refs[ref].at[at] if ref == 0 else refs[ref].at[pl.ds(at * live_rows, live_rows)]
-            target = held.at[pl.ds(i * live_rows, live_rows), pl.ds(e * wide, wide)]
-            copies[k, e] = pltpu.make_async_copy(source, target, sems.at[i, e])
-            copies[k, e].start()
+        i = 0
+        while i < len(slots):
+            ref, at = pieces[slots[i], e]
+            n = 1
+            while ref and i + n < len(slots) and pieces[slots[i + n], e] == (ref, at + n):
+                n += 1
+            source = refs[ref].at[pl.ds(at * live_rows, n * live_rows)] if ref else refs[ref].at[at]
+            target = held.at[pl.ds(i * live_rows, n * live_rows), pl.ds(e * wide, wide)]
+            copies.append(pltpu.make_async_copy(source, target, sems.at[i, e]))
+            copies[-1].start()
+            i += n
     return copies
 
 
@@ -181,8 +186,8 @@
         turned[:, i * live_rows:(i + 1) * live_rows] = jnp.concatenate([head, tail], axis=1)
     for e in range(quarters):
         rows_copies[e].wait()
-        for k in slots:
-            copies[k, e].wait()
+    for copy in copies:
+        copy.wait()
     product = lax.dot_general(
         rows_held[...], held[...], (((1,), (1,)), ((), ())), preferred_element_type=jnp.float32
     )
@@ -255,7 +260,7 @@
             part = source[at * live_rows:(at + 1) * live_rows, e * wide:(e + 1) * wide].astype(jnp.float32)
             scaled[e % 2, i * live_rows:(i + 1) * live_rows] = (columns[i] * part).astype(jnp.bfloat16)
 
-    for copy in copies.values():
+    for copy in copies:
         copy.wait()
     writes = []
     scale_rows(0)

time: 117 us -> 117 us (level)
  no operation moved by 1% of the time
where the time goes in v5:
time: 117 us
  waiting for transfers between devices  40.9 us (35%)
  starting transfers between devices  39.5 us (34%)
  Pallas kernels  25.3 us (22%)
  local copies, waits for them, and re-layouts  9.96 us (9%)
    ppermute x16, waiting for transfers between devices, over_dp(): return lax.ppermute(x, 'dp', [(s, s ^ m) for s in range(shards)])  32.8 us
    ppermute x16, starting transfers between devices, over_dp(): return lax.ppermute(x, 'dp', [(s, s ^ m) for s in range(shards)])  32.7 us
    pallas_call x1, Pallas kernels, cube_body(): pl.pallas_call(functools.partial(grad_kernel, places, len(refs), groups,...  12 us
    pallas_call x2, Pallas kernels, shift_sums(): pl.pallas_call(functools.partial(shift_kernel, places, len(refs), slots,...  10.4 us
    unnamed x40, local copies, waits for them, and re-layouts  9.88 us
    ppermute x9, waiting for transfers between devices, over_mp(): return lax.ppermute(x, 'mp', [(s, s ^ m) for s in range(quarters)])  6.44 us
    ppermute x1, starting transfers between devices, over_both(): return lax.ppermute(x, ('dp', 'mp'), pairs)  3.46 us
    ppermute x9, starting transfers between devices, over_mp(): return lax.ppermute(x, 'mp', [(s, s ^ m) for s in range(quarters)])  3.32 us
  transfers between devices with their start and end apart: 26, of which 13 were waited for; matrix products, arithmetic and copies ran while one was open for 0% of the time, Pallas kernels for 7%

profile of v5, /device:TPU:0, one launch (start us, length us, event | category | flops | bytes accessed | tf_op | source)
XLA Modules:
  0.0 116.7 jit_solution(16616983541250080989)
XLA Ops:
  0.6 0.0 copy-start.1
  0.6 1.3 %copy-done.1 = bf16[256,2560]{1,0:T(8,128)(2,1)S(1)} copy-done((bf16[256,2560]{1,0:T(8,128)(2,1)S(1)}, bf16[256,2560]{1,0:T(8,128)(2,1)}, u32[]{:S(2)}) %copy-start.1) | copy-done | bytes 1310744
  2.0 0.7 copy-done.5
  2.6 0.9 pack_first.1
  3.5 3.0 %collective-permute-start.4 = (bf16[448,640]{1,0:T(8,128)(2,1)S(1)}, bf16[448,640]{1,0:T(8,128)(2,1)S(1)}, u32[]{:S(2)}, u32[]{:S(2)}) collective-permute-start(bf16[448,640]{1,0:T(8,128)(2,1)S(1)} %get-tuple-element.39), channel_id=1, source_target_pairs={{0,4},{4,0},{8,12},{12,8},{16,20},{20,16},{24,28},{28,24},{1,5},{5... | collective-permute-start | bytes 1720328 | tf_op jit(solution)/shard_map/ppermute | solution.py:339
  6.5 2.6 %collective-permute-start.3 = (bf16[224,640]{1,0:T(8,128)(2,1)S(1)}, bf16[224,640]{1,0:T(8,128)(2,1)S(1)}, u32[]{:S(2)}, u32[]{:S(2)}) collective-permute-start(bf16[224,640]{1,0:T(8,128)(2,1)S(1)} %get-tuple-element.38), channel_id=1, source_target_pairs={{0,16},{4,20},{8,24},{12,28},{16,0},{20,4},{24,8},{28,12},{1,17},{... | collective-permute-start | bytes 860168 | tf_op jit(solution)/shard_map/ppermute | solution.py:339
  9.1 1.3 %collective-permute-start.2 = (bf16[224,640]{1,0:T(8,128)(2,1)S(1)}, bf16[224,640]{1,0:T(8,128)(2,1)S(1)}, u32[]{:S(2)}, u32[]{:S(2)}) collective-permute-start(bf16[224,640]{1,0:T(8,128)(2,1)S(1)} %get-tuple-element.38), channel_id=1, source_target_pairs={{0,24},{4,28},{8,16},{12,20},{16,8},{20,12},{24,0},{28,4},{1,25},{... | collective-permute-start | bytes 860168 | tf_op jit(solution)/shard_map/ppermute | solution.py:339
  10.5 0.2 collective-permute-start.1
  10.7 1.3 %copy-done.2 = bf16[256,2560]{1,0:T(8,128)(2,1)S(1)} copy-done((bf16[256,2560]{1,0:T(8,128)(2,1)S(1)}, bf16[256,2560]{1,0:T(8,128)(2,1)}, u32[]{:S(2)}) %copy-start.2) | copy-done | bytes 1310744
  12.0 0.7 copy-done.6
  12.7 1.5 %copy-done.8 = bf16[256,3584]{1,0:T(8,128)(2,1)S(1)} copy-done((bf16[256,3584]{1,0:T(8,128)(2,1)S(1)}, bf16[256,3584]{1,0:T(8,128)(2,1)}, u32[]{:S(2)}) %copy-start.8) | copy-done | bytes 1835032
  14.2 0.7 copy-done.14
  14.9 0.7 copy-done.15
  15.5 0.7 copy-done.16
  16.2 0.7 copy-done.17
  16.8 2.0 %pack_rest.1 = (f32[8,224]{1,0:T(8,128)S(1)}, bf16[4,224,640]{2,1,0:T(8,128)(2,1)S(1)}, bf16[784,128]{1,0:T(8,128)(2,1)S(1)}, bf16[784,128]{1,0:T(8,128)(2,1)S(1...) custom-call(s32[1,32]{1,0:T(1,128)S(1)} %copy-done.6, ...), custom_call_target="tpu_custom_call" | custom-call | flops 2000000000 | bytes 8000000 | tf_op jit(solution)/shard_map/pack_rest/pallas_call | solution.py:365
  18.8 0.5 collective-permute-start
  19.4 5.4 %collective-permute-done.rest_1_ = bf16[784,128]{1,0:T(8,128)(2,1)S(1)} collective-permute-done((bf16[784,128]{1,0:T(8,128)(2,1)S(1)}, bf16[784,128]{1,0:T(8,128)(2,1)S(1)}, u32[]{:S(2)}, u32[]{:S(2)}) %collective-permute-start) | collective-permute-done | bytes 200736 | tf_op jit(solution)/shard_map/ppermute | solution.py:339
  24.7 4.5 %collective-permute-done.3 = bf16[224,640]{1,0:T(8,128)(2,1)S(1)} collective-permute-done((bf16[224,640]{1,0:T(8,128)(2,1)S(1)}, bf16[224,640]{1,0:T(8,128)(2,1)S(1)}, u32[]{:S(2)}, u32[]{:S(2)}) %collective-permute-start.3) | collective-permute-done | bytes 286752 | tf_op jit(solution)/shard_map/ppermute | solution.py:339
  29.2 0.0 collective-permute-done.2
  29.2 0.2 collective-permute-done.1
  29.4 0.0 collective-permute-done.4.rest_6_.rest_3_
  29.4 0.0 collective-permute-start.9
  29.5 0.5 collective-permute-start.6
  30.0 1.5 %collective-permute-start.5 = (bf16[672,640]{1,0:T(8,128)(2,1)S(1)}, bf16[672,640]{1,0:T(8,128)(2,1)S(1)}, u32[]{:S(2)}, u32[]{:S(2)}) collective-permute-start(bf16[672,640]{1,0:T(8,128)(2,1)S(1)} %constant_dynamic-update-slice_fusion.rest_8_.rest_5_), channel_id=1, source_target_pairs={{0,2},{1,3},{2,0},{3,1},{4,6},{5,7},{6,4},{7,5},{8,10},{9,11},{10,... | collective-permute-start | bytes 2580488 | tf_op jit(solution)/shard_map/ppermute | solution.py:342
  31.6 0.0 collective-permute-done.9.rest_7_.rest_4_
  31.6 0.0 collective-permute-start.10
  31.6 7.5 %collective-permute-start.7 = (bf16[784,128]{1,0:T(8,128)(2,1)S(1)}, bf16[784,128]{1,0:T(8,128)(2,1)S(1)}, u32[]{:S(2)}, u32[]{:S(2)}) collective-permute-start(bf16[784,128]{1,0:T(8,128)(2,1)S(1)} %get-tuple-element.43), channel_id=1, source_target_pairs={{0,16},{4,20},{8,24},{12,28},{16,0},{20,4},{24,8},{28,12},{1,17},{... | collective-permute-start | bytes 602120 | tf_op jit(solution)/shard_map/ppermute | solution.py:339
  39.1 0.4 collective-permute-start.8
  39.5 14.0 %collective-permute-done.7.rest_4_ = bf16[784,128]{1,0:T(8,128)(2,1)S(1)} collective-permute-done((bf16[784,128]{1,0:T(8,128)(2,1)S(1)}, bf16[784,128]{1,0:T(8,128)(2,1)S(1)}, u32[]{:S(2)}, u32[]{:S(2)}) %collective-permute-start.7) | collective-permute-done | bytes 200736 | tf_op jit(solution)/shard_map/ppermute | solution.py:339
  53.5 0.0 collective-permute-done.8.rest_3_
  53.5 0.0 collective-permute-done.6.rest_4_
  53.5 0.0 collective-permute-done.5.rest_10_.rest_7_
  53.6 0.1 collective-permute-start.13
  53.6 1.3 %collective-permute-start.17 = (bf16[672,640]{1,0:T(8,128)(2,1)S(1)}, bf16[672,640]{1,0:T(8,128)(2,1)S(1)}, u32[]{:S(2)}, u32[]{:S(2)}) collective-permute-start(bf16[672,640]{1,0:T(8,128)(2,1)S(1)} %collective-permute-done.6.rest_4_), channel_id=1, source_target_pairs={{0,2},{1,3},{2,0},{3,1},{4,6},{5,7},{6,4},{7,5},{8,10},{9,11},{10,... | collective-permute-start | bytes 2580488 | tf_op jit(solution)/shard_map/ppermute | solution.py:342
  55.0 1.0 collective-permute-done.13.rest_11_.rest_8_
  56.0 0.1 collective-permute-start.16
  56.1 2.2 %collective-permute-start.12 = (bf16[784,128]{1,0:T(8,128)(2,1)S(1)}, bf16[784,128]{1,0:T(8,128)(2,1)S(1)}, u32[]{:S(2)}, u32[]{:S(2)}) collective-permute-start(bf16[784,128]{1,0:T(8,128)(2,1)S(1)} %get-tuple-element.51), channel_id=1, source_target_pairs={{0,28},{4,24},{8,20},{12,16},{16,12},{20,8},{24,4},{28,0},{1,29},{... | collective-permute-start | bytes 602120 | tf_op jit(solution)/shard_map/ppermute | solution.py:339
  58.4 4.5 %collective-permute-start.11 = (bf16[784,128]{1,0:T(8,128)(2,1)S(1)}, bf16[784,128]{1,0:T(8,128)(2,1)S(1)}, u32[]{:S(2)}, u32[]{:S(2)}) collective-permute-start(bf16[784,128]{1,0:T(8,128)(2,1)S(1)} %get-tuple-element.48), channel_id=1, source_target_pairs={{0,8},{4,12},{8,0},{12,4},{16,24},{20,28},{24,16},{28,20},{1,9},{5... | collective-permute-start | bytes 602120 | tf_op jit(solution)/shard_map/ppermute | solution.py:339
  62.9 3.8 %collective-permute-done.12.rest_1_ = bf16[784,128]{1,0:T(8,128)(2,1)S(1)} collective-permute-done((bf16[784,128]{1,0:T(8,128)(2,1)S(1)}, bf16[784,128]{1,0:T(8,128)(2,1)S(1)}, u32[]{:S(2)}, u32[]{:S(2)}) %collective-permute-start.12) | collective-permute-done | bytes 200736 | tf_op jit(solution)/shard_map/ppermute | solution.py:339
  66.7 5.3 %collective-permute-start.15 = (bf16[784,128]{1,0:T(8,128)(2,1)S(1)}, bf16[784,128]{1,0:T(8,128)(2,1)S(1)}, u32[]{:S(2)}, u32[]{:S(2)}) collective-permute-start(bf16[784,128]{1,0:T(8,128)(2,1)S(1)} %get-tuple-element.58), channel_id=1, source_target_pairs={{0,20},{4,16},{8,28},{12,24},{16,4},{20,0},{24,12},{28,8},{1,21},{... | collective-permute-start | bytes 602120 | tf_op jit(solution)/shard_map/ppermute | solution.py:339
  71.9 6.3 %shift_sums.2 = (f32[8,224]{1,0:T(8,128)S(1)}, bf16[448,1120]{1,0:T(8,128)(2,1)S(1)}) custom-call(bf16[448,2560]{1,0:T(8,128)(2,1)S(1)} %copy-done, bf16[784,128]{1,0:T(8,128)(2,1)S(1)} %get-tuple-element.35.rest_0_, bf16[784,128]{1,0:T(8,128)(2,1)S(1)} %collective-permute-done.rest_1_, bf16[784,128]{1,0:T(8,128)(2,1)S(1)} %collective-permute-done.11.rest_2_, ...), custom_call_target="tpu_custom_call" | custom-call | flops 2569011200 | bytes 5734400 | tf_op jit(solution)/shard_map/shift_sums/pallas_call | solution.py:399
  78.3 0.0 collective-permute-done.14.rest_0_
  78.3 3.0 %collective-permute-done.15.rest_2_ = bf16[784,128]{1,0:T(8,128)(2,1)S(1)} collective-permute-done((bf16[784,128]{1,0:T(8,128)(2,1)S(1)}, bf16[784,128]{1,0:T(8,128)(2,1)S(1)}, u32[]{:S(2)}, u32[]{:S(2)}) %collective-permute-start.15) | collective-permute-done | bytes 200736 | tf_op jit(solution)/shard_map/ppermute | solution.py:339
  81.3 0.0 collective-permute-done.17.rest_6_
  81.3 0.0 collective-permute-done.16.rest_5_
  81.3 0.1 collective-permute-start.18
  81.4 2.4 %collective-permute-done.18.rest_7_ = bf16[672,640]{1,0:T(8,128)(2,1)S(1)} collective-permute-done((bf16[672,640]{1,0:T(8,128)(2,1)S(1)}, bf16[672,640]{1,0:T(8,128)(2,1)S(1)}, u32[]{:S(2)}, u32[]{:S(2)}) %collective-permute-start.18) | collective-permute-done | bytes 860192 | tf_op jit(solution)/shard_map/ppermute | solution.py:342
  83.8 4.1 %shift_sums.3 = (f32[8,224]{1,0:T(8,128)S(1)}, bf16[448,672]{1,0:T(8,128)(2,1)S(1)}, bf16[672,2560]{1,0:T(8,128)(2,1)S(1)}) custom-call(bf16[448,2560]{1,0:T(8,128)(2,1)S(1)} %copy-done, bf16[784,128]{1,0:T(8,128)(2,1)S(1)} %collective-permute-done.14.rest_0_, bf16[784,128]{1,0:T(8,128)(2,1)S(1)} %collective-permute-done.12.rest_1_, ...), custom_call_target="tpu_custom_call" | custom-call | flops 1541406720 | bytes 3440640 | tf_op jit(solution)/shard_map/shift_sums/pallas_call | solution.py:399
  87.9 1.7 %copy-done.7 = bf16[672,2560]{1,0:T(8,128)(2,1)} copy-done((bf16[672,2560]{1,0:T(8,128)(2,1)}, bf16[672,2560]{1,0:T(8,128)(2,1)S(1)}, u32[]{:S(2)}) %copy-start.7) | copy-done | bytes 3440664
  89.6 0.1 collective-permute-start.19
  89.7 1.0 collective-permute-done.19
  90.8 0.1 collective-permute-start.21
  90.9 3.5 %collective-permute-start.22 = (f32[8,224]{1,0:T(8,128)S(1)}, f32[8,224]{1,0:T(8,128)S(1)}, u32[]{:S(2)}, u32[]{:S(2)}) collective-permute-start(f32[8,224]{1,0:T(8,128)S(1)} %add.12), channel_id=1, source_target_pairs={{0,6},{1,7},{2,4},{3,5},{4,2},{5,3},{6,0},{7,1},{8,14},{9,15},{10,... | collective-permute-start | bytes 21512 | tf_op jit(solution)/shard_map/ppermute | solution.py:346
  94.3 0.0 collective-permute-start.20
  94.3 1.6 %collective-permute-done.22 = f32[8,224]{1,0:T(8,128)S(1)} collective-permute-done((f32[8,224]{1,0:T(8,128)S(1)}, f32[8,224]{1,0:T(8,128)S(1)}, u32[]{:S(2)}, u32[]{:S(2)}) %collective-permute-start.22) | collective-permute-done | bytes 7200 | tf_op jit(solution)/shard_map/ppermute | solution.py:346
  95.9 0.0 collective-permute-done.21
  96.0 2.0 %collective-permute-done.20 = f32[8,224]{1,0:T(8,128)S(1)} collective-permute-done((f32[8,224]{1,0:T(8,128)S(1)}, f32[8,224]{1,0:T(8,128)S(1)}, u32[]{:S(2)}, u32[]{:S(2)}) %collective-permute-start.20) | collective-permute-done | bytes 7200 | tf_op jit(solution)/shard_map/ppermute | solution.py:342
  98.0 1.7 %collective-permute-start.25 = (f32[24,224]{1,0:T(8,128)S(1)}, f32[24,224]{1,0:T(8,128)S(1)}, u32[]{:S(2)}, u32[]{:S(2)}) collective-permute-start(f32[24,224]{1,0:T(8,128)S(1)} %pad_maximum_fusion.rest_10_), channel_id=1, source_target_pairs={{0,24},{4,28},{8,16},{12,20},{16,8},{20,12},{24,0},{28,4},{1,25},{... | collective-permute-start | bytes 64520 | tf_op jit(solution)/shard_map/ppermute | solution.py:339
  99.7 2.7 %collective-permute-start.23 = (f32[24,224]{1,0:T(8,128)S(1)}, f32[24,224]{1,0:T(8,128)S(1)}, u32[]{:S(2)}, u32[]{:S(2)}) collective-permute-start(f32[24,224]{1,0:T(8,128)S(1)} %pad_maximum_fusion.rest_10_), channel_id=1, source_target_pairs={{0,8},{4,12},{8,0},{12,4},{16,24},{20,28},{24,16},{28,20},{1,9},{5... | collective-permute-start | bytes 64520 | tf_op jit(solution)/shard_map/ppermute | solution.py:339
  102.4 1.2 %collective-permute-done.25.rest_13_ = f32[24,224]{1,0:T(8,128)S(1)} collective-permute-done((f32[24,224]{1,0:T(8,128)S(1)}, f32[24,224]{1,0:T(8,128)S(1)}, u32[]{:S(2)}, u32[]{:S(2)}) %collective-permute-start.25) | collective-permute-done | bytes 21536 | tf_op jit(solution)/shard_map/ppermute | solution.py:339
  103.7 0.8 collective-permute-done.24.rest_12_
  104.5 0.0 collective-permute-done.23.rest_11_
  104.5 12.0 %weight_grad.1 = (f32[8,64]{1,0:T(8,128)}, f32[448,2560]{1,0:T(8,128)}) custom-call(bf16[448,1120]{1,0:T(8,128)(2,1)} %copy-done.18, bf16[448,672]{1,0:T(8,128)(2,1)S(1)} %get-tuple-element.63.rest_1_, bf16[4,224,640]{2,1,0:T(8,128)(2,1)} %copy-done.3, bf16[448,640]{1,0:T(8,128)(2,1)S(1)} %collective-permute-done.4.rest_6_.rest_3_, ...), custom_call_target="tpu_custom_call" | custom-call | flops 4110417920 | bytes 13762560 | tf_op jit(solution)/shard_map/weight_grad/pallas_call | solution.py:454
  (41 shorter events, 0.2 us)
Async XLA Ops:
  0.6 1.3 %copy-start.1 = (bf16[256,2560]{1,0:T(8,128)(2,1)S(1)}, bf16[256,2560]{1,0:T(8,128)(2,1)}, u32[]{:S(2)}) copy-start(bf16[256,2560]{1,0:T(8,128)(2,1)} %read.3) | copy-start | bytes 3932164
  1.9 0.7 copy-start.5
  3.5 25.9 %collective-permute-start.4 = (bf16[448,640]{1,0:T(8,128)(2,1)S(1)}, bf16[448,640]{1,0:T(8,128)(2,1)S(1)}, u32[]{:S(2)}, u32[]{:S(2)}) collective-permute-start(bf16[448,640]{1,0:T(8,128)(2,1)S(1)} %get-tuple-element.39), channel_id=1, source_target_pairs={{0,4},{4,0},{8,12},{12,8},{16,20},{20,16},{24,28},{28,24},{1,5},{5... | collective-permute-start | bytes 1720328 | tf_op jit(solution)/shard_map/ppermute | solution.py:339
  6.5 22.7 %collective-permute-start.3 = (bf16[224,640]{1,0:T(8,128)(2,1)S(1)}, bf16[224,640]{1,0:T(8,128)(2,1)S(1)}, u32[]{:S(2)}, u32[]{:S(2)}) collective-permute-start(bf16[224,640]{1,0:T(8,128)(2,1)S(1)} %get-tuple-element.38), channel_id=1, source_target_pairs={{0,16},{4,20},{8,24},{12,28},{16,0},{20,4},{24,8},{28,12},{1,17},{... | collective-permute-start | bytes 860168 | tf_op jit(solution)/shard_map/ppermute | solution.py:339
  9.1 20.1 %collective-permute-start.2 = (bf16[224,640]{1,0:T(8,128)(2,1)S(1)}, bf16[224,640]{1,0:T(8,128)(2,1)S(1)}, u32[]{:S(2)}, u32[]{:S(2)}) collective-permute-start(bf16[224,640]{1,0:T(8,128)(2,1)S(1)} %get-tuple-element.38), channel_id=1, source_target_pairs={{0,24},{4,28},{8,16},{12,20},{16,8},{20,12},{24,0},{28,4},{1,25},{... | collective-permute-start | bytes 860168 | tf_op jit(solution)/shard_map/ppermute | solution.py:339
  10.5 18.9 %collective-permute-start.1 = (bf16[224,640]{1,0:T(8,128)(2,1)S(1)}, bf16[224,640]{1,0:T(8,128)(2,1)S(1)}, u32[]{:S(2)}, u32[]{:S(2)}) collective-permute-start(bf16[224,640]{1,0:T(8,128)(2,1)S(1)} %get-tuple-element.38), channel_id=1, source_target_pairs={{0,8},{4,12},{8,0},{12,4},{16,24},{20,28},{24,16},{28,20},{1,9},{5... | collective-permute-start | bytes 860168 | tf_op jit(solution)/shard_map/ppermute | solution.py:339
  10.7 1.3 %copy-start.2 = (bf16[256,2560]{1,0:T(8,128)(2,1)S(1)}, bf16[256,2560]{1,0:T(8,128)(2,1)}, u32[]{:S(2)}) copy-start(bf16[256,2560]{1,0:T(8,128)(2,1)} %read.3) | copy-start | bytes 3932164
  12.0 0.7 copy-start.6
  12.7 1.5 %copy-start.8 = (bf16[256,3584]{1,0:T(8,128)(2,1)S(1)}, bf16[256,3584]{1,0:T(8,128)(2,1)}, u32[]{:S(2)}) copy-start(bf16[256,3584]{1,0:T(8,128)(2,1)} %hidden.1) | copy-start | bytes 5505028
  14.2 0.7 copy-start.14
  14.9 0.7 copy-start.15
  15.5 0.7 copy-start.16
  16.2 0.7 copy-start.17
  16.8 55.1 %copy-start = (bf16[448,2560]{1,0:T(8,128)(2,1)S(1)}, bf16[448,2560]{1,0:T(8,128)(2,1)}, u32[]{:S(2)}) copy-start(bf16[448,2560]{1,0:T(8,128)(2,1)} %weight.3) | copy-start | bytes 6881284
  18.8 65.0 %copy-start.3 = (bf16[4,224,640]{2,1,0:T(8,128)(2,1)}, bf16[4,224,640]{2,1,0:T(8,128)(2,1)S(1)}, u32[]{:S(2)}) copy-start(bf16[4,224,640]{2,1,0:T(8,128)(2,1)S(1)} %get-tuple-element.52.rest_5_.rest_3_.rest_2_) | copy-start | bytes 3440644
  18.8 5.9 %collective-permute-start = (bf16[784,128]{1,0:T(8,128)(2,1)S(1)}, bf16[784,128]{1,0:T(8,128)(2,1)S(1)}, u32[]{:S(2)}, u32[]{:S(2)}) collective-permute-start(bf16[784,128]{1,0:T(8,128)(2,1)S(1)} %get-tuple-element.36), channel_id=1, source_target_pairs={{0,4},{4,0},{8,12},{12,8},{16,20},{20,16},{24,28},{28,24},{1,5},{5... | collective-permute-start | bytes 602120 | tf_op jit(solution)/shard_map/ppermute | solution.py:339
  29.4 2.2 %collective-permute-start.9 = (bf16[448,640]{1,0:T(8,128)(2,1)S(1)}, bf16[448,640]{1,0:T(8,128)(2,1)S(1)}, u32[]{:S(2)}, u32[]{:S(2)}) collective-permute-start(bf16[448,640]{1,0:T(8,128)(2,1)S(1)} %collective-permute-done.4.rest_6_.rest_3_), channel_id=1, source_target_pairs={{0,1},{1,0},{2,3},{3,2},{4,5},{5,4},{6,7},{7,6},{8,9},{9,8},{10,11... | collective-permute-start | bytes 1720328 | tf_op jit(solution)/shard_map/ppermute | solution.py:342
  29.5 48.8 %copy-start.4 = (bf16[672,640]{1,0:T(8,128)(2,1)}, bf16[672,640]{1,0:T(8,128)(2,1)S(1)}, u32[]{:S(2)}) copy-start(bf16[672,640]{1,0:T(8,128)(2,1)S(1)} %constant_dynamic-update-slice_fusion.rest_8_.rest_5_) | copy-start | bytes 2580484
  29.5 24.0 %collective-permute-start.6 = (bf16[672,640]{1,0:T(8,128)(2,1)S(1)}, bf16[672,640]{1,0:T(8,128)(2,1)S(1)}, u32[]{:S(2)}, u32[]{:S(2)}) collective-permute-start(bf16[672,640]{1,0:T(8,128)(2,1)S(1)} %constant_dynamic-update-slice_fusion.rest_8_.rest_5_), channel_id=1, source_target_pairs={{0,4},{4,0},{8,12},{12,8},{16,20},{20,16},{24,28},{28,24},{1,5},{5... | collective-permute-start | bytes 2580488 | tf_op jit(solution)/shard_map/ppermute | solution.py:339
  30.0 23.5 %collective-permute-start.5 = (bf16[672,640]{1,0:T(8,128)(2,1)S(1)}, bf16[672,640]{1,0:T(8,128)(2,1)S(1)}, u32[]{:S(2)}, u32[]{:S(2)}) collective-permute-start(bf16[672,640]{1,0:T(8,128)(2,1)S(1)} %constant_dynamic-update-slice_fusion.rest_8_.rest_5_), channel_id=1, source_target_pairs={{0,2},{1,3},{2,0},{3,1},{4,6},{5,7},{6,4},{7,5},{8,10},{9,11},{10,... | collective-permute-start | bytes 2580488 | tf_op jit(solution)/shard_map/ppermute | solution.py:342
  31.6 46.7 %copy-start.12 = (bf16[448,640]{1,0:T(8,128)(2,1)}, bf16[448,640]{1,0:T(8,128)(2,1)S(1)}, u32[]{:S(2)}) copy-start(bf16[448,640]{1,0:T(8,128)(2,1)S(1)} %collective-permute-done.9.rest_7_.rest_4_) | copy-start | bytes 1720324
  31.6 22.0 %collective-permute-start.10 = (bf16[672,640]{1,0:T(8,128)(2,1)S(1)}, bf16[672,640]{1,0:T(8,128)(2,1)S(1)}, u32[]{:S(2)}, u32[]{:S(2)}) collective-permute-start(bf16[672,640]{1,0:T(8,128)(2,1)S(1)} %constant_dynamic-update-slice_fusion.rest_8_.rest_5_), channel_id=1, source_target_pairs={{0,1},{1,0},{2,3},{3,2},{4,5},{5,4},{6,7},{7,6},{8,9},{9,8},{10,11... | collective-permute-start | bytes 2580488 | tf_op jit(solution)/shard_map/ppermute | solution.py:342
  31.6 21.9 %collective-permute-start.7 = (bf16[784,128]{1,0:T(8,128)(2,1)S(1)}, bf16[784,128]{1,0:T(8,128)(2,1)S(1)}, u32[]{:S(2)}, u32[]{:S(2)}) collective-permute-start(bf16[784,128]{1,0:T(8,128)(2,1)S(1)} %get-tuple-element.43), channel_id=1, source_target_pairs={{0,16},{4,20},{8,24},{12,28},{16,0},{20,4},{24,8},{28,12},{1,17},{... | collective-permute-start | bytes 602120 | tf_op jit(solution)/shard_map/ppermute | solution.py:339
  39.1 14.4 %collective-permute-start.8 = (bf16[784,128]{1,0:T(8,128)(2,1)S(1)}, bf16[784,128]{1,0:T(8,128)(2,1)S(1)}, u32[]{:S(2)}, u32[]{:S(2)}) collective-permute-start(bf16[784,128]{1,0:T(8,128)(2,1)S(1)} %get-tuple-element.45), channel_id=1, source_target_pairs={{0,24},{4,28},{8,16},{12,20},{16,8},{20,12},{24,0},{28,4},{1,25},{... | collective-permute-start | bytes 602120 | tf_op jit(solution)/shard_map/ppermute | solution.py:339
  53.5 24.8 %copy-start.9 = (bf16[672,640]{1,0:T(8,128)(2,1)}, bf16[672,640]{1,0:T(8,128)(2,1)S(1)}, u32[]{:S(2)}) copy-start(bf16[672,640]{1,0:T(8,128)(2,1)S(1)} %collective-permute-done.5.rest_10_.rest_7_) | copy-start | bytes 2580484
  53.5 24.8 %copy-start.10 = (bf16[672,640]{1,0:T(8,128)(2,1)}, bf16[672,640]{1,0:T(8,128)(2,1)S(1)}, u32[]{:S(2)}) copy-start(bf16[672,640]{1,0:T(8,128)(2,1)S(1)} %collective-permute-done.10.rest_9_.rest_6_) | copy-start | bytes 2580484
  53.6 2.5 %collective-permute-start.13 = (bf16[672,640]{1,0:T(8,128)(2,1)S(1)}, bf16[672,640]{1,0:T(8,128)(2,1)S(1)}, u32[]{:S(2)}, u32[]{:S(2)}) collective-permute-start(bf16[672,640]{1,0:T(8,128)(2,1)S(1)} %collective-permute-done.5.rest_10_.rest_7_), channel_id=1, source_target_pairs={{0,1},{1,0},{2,3},{3,2},{4,5},{5,4},{6,7},{7,6},{8,9},{9,8},{10,11... | collective-permute-start | bytes 2580488 | tf_op jit(solution)/shard_map/ppermute | solution.py:342
  53.6 27.7 %collective-permute-start.17 = (bf16[672,640]{1,0:T(8,128)(2,1)S(1)}, bf16[672,640]{1,0:T(8,128)(2,1)S(1)}, u32[]{:S(2)}, u32[]{:S(2)}) collective-permute-start(bf16[672,640]{1,0:T(8,128)(2,1)S(1)} %collective-permute-done.6.rest_4_), channel_id=1, source_target_pairs={{0,2},{1,3},{2,0},{3,1},{4,6},{5,7},{6,4},{7,5},{8,10},{9,11},{10,... | collective-permute-start | bytes 2580488 | tf_op jit(solution)/shard_map/ppermute | solution.py:342
  56.0 22.3 %copy-start.11 = (bf16[672,640]{1,0:T(8,128)(2,1)}, bf16[672,640]{1,0:T(8,128)(2,1)S(1)}, u32[]{:S(2)}) copy-start(bf16[672,640]{1,0:T(8,128)(2,1)S(1)} %collective-permute-done.13.rest_11_.rest_8_) | copy-start | bytes 2580484
  56.0 25.3 %collective-permute-start.16 = (bf16[672,640]{1,0:T(8,128)(2,1)S(1)}, bf16[672,640]{1,0:T(8,128)(2,1)S(1)}, u32[]{:S(2)}, u32[]{:S(2)}) collective-permute-start(bf16[672,640]{1,0:T(8,128)(2,1)S(1)} %collective-permute-done.6.rest_4_), channel_id=1, source_target_pairs={{0,1},{1,0},{2,3},{3,2},{4,5},{5,4},{6,7},{7,6},{8,9},{9,8},{10,11... | collective-permute-start | bytes 2580488 | tf_op jit(solution)/shard_map/ppermute | solution.py:342
  56.1 10.5 %collective-permute-start.12 = (bf16[784,128]{1,0:T(8,128)(2,1)S(1)}, bf16[784,128]{1,0:T(8,128)(2,1)S(1)}, u32[]{:S(2)}, u32[]{:S(2)}) collective-permute-start(bf16[784,128]{1,0:T(8,128)(2,1)S(1)} %get-tuple-element.51), channel_id=1, source_target_pairs={{0,28},{4,24},{8,20},{12,16},{16,12},{20,8},{24,4},{28,0},{1,29},{... | collective-permute-start | bytes 602120 | tf_op jit(solution)/shard_map/ppermute | solution.py:339
  58.4 13.5 %collective-permute-start.11 = (bf16[784,128]{1,0:T(8,128)(2,1)S(1)}, bf16[784,128]{1,0:T(8,128)(2,1)S(1)}, u32[]{:S(2)}, u32[]{:S(2)}) collective-permute-start(bf16[784,128]{1,0:T(8,128)(2,1)S(1)} %get-tuple-element.48), channel_id=1, source_target_pairs={{0,8},{4,12},{8,0},{12,4},{16,24},{20,28},{24,16},{28,20},{1,9},{5... | collective-permute-start | bytes 602120 | tf_op jit(solution)/shard_map/ppermute | solution.py:339
  62.9 15.5 %collective-permute-start.14 = (bf16[784,128]{1,0:T(8,128)(2,1)S(1)}, bf16[784,128]{1,0:T(8,128)(2,1)S(1)}, u32[]{:S(2)}, u32[]{:S(2)}) collective-permute-start(bf16[784,128]{1,0:T(8,128)(2,1)S(1)} %get-tuple-element.56), channel_id=1, source_target_pairs={{0,12},{4,8},{8,4},{12,0},{16,28},{20,24},{24,20},{28,16},{1,13},{... | collective-permute-start | bytes 602120 | tf_op jit(solution)/shard_map/ppermute | solution.py:339
  66.7 14.6 %collective-permute-start.15 = (bf16[784,128]{1,0:T(8,128)(2,1)S(1)}, bf16[784,128]{1,0:T(8,128)(2,1)S(1)}, u32[]{:S(2)}, u32[]{:S(2)}) collective-permute-start(bf16[784,128]{1,0:T(8,128)(2,1)S(1)} %get-tuple-element.58), channel_id=1, source_target_pairs={{0,20},{4,16},{8,28},{12,24},{16,4},{20,0},{24,12},{28,8},{1,21},{... | collective-permute-start | bytes 602120 | tf_op jit(solution)/shard_map/ppermute | solution.py:339
  78.3 9.6 %copy-start.18 = (bf16[448,1120]{1,0:T(8,128)(2,1)}, bf16[448,1120]{1,0:T(8,128)(2,1)S(1)}, u32[]{:S(2)}) copy-start(bf16[448,1120]{1,0:T(8,128)(2,1)S(1)} %get-tuple-element.54.rest_0_) | copy-start | bytes 3010564
  81.3 23.2 %copy-start.13 = (bf16[448,640]{1,0:T(8,128)(2,1)S(1)}, bf16[448,640]{1,0:T(8,128)(2,1)}, u32[]{:S(2)}) copy-start(bf16[448,640]{1,0:T(8,128)(2,1)} %copy-done.12) | copy-start | bytes 1720324
  81.3 2.5 %collective-permute-start.18 = (bf16[672,640]{1,0:T(8,128)(2,1)S(1)}, bf16[672,640]{1,0:T(8,128)(2,1)S(1)}, u32[]{:S(2)}, u32[]{:S(2)}) collective-permute-start(bf16[672,640]{1,0:T(8,128)(2,1)S(1)} %collective-permute-done.17.rest_6_), channel_id=1, source_target_pairs={{0,1},{1,0},{2,3},{3,2},{4,5},{5,4},{6,7},{7,6},{8,9},{9,8},{10,11... | collective-permute-start | bytes 2580488 | tf_op jit(solution)/shard_map/ppermute | solution.py:342
  87.9 1.7 %copy-start.7 = (bf16[672,2560]{1,0:T(8,128)(2,1)}, bf16[672,2560]{1,0:T(8,128)(2,1)S(1)}, u32[]{:S(2)}) copy-start(bf16[672,2560]{1,0:T(8,128)(2,1)S(1)} %get-tuple-element.64.rest_9_) | copy-start | bytes 10321924
  89.6 1.2 %collective-permute-start.19 = (f32[8,224]{1,0:T(8,128)S(1)}, f32[8,224]{1,0:T(8,128)S(1)}, u32[]{:S(2)}, u32[]{:S(2)}) collective-permute-start(f32[8,224]{1,0:T(8,128)S(1)} %get-tuple-element.65), channel_id=1, source_target_pairs={{0,1},{1,0},{2,3},{3,2},{4,5},{5,4},{6,7},{7,6},{8,9},{9,8},{10,11... | collective-permute-start | bytes 21512 | tf_op jit(solution)/shard_map/ppermute | solution.py:342
  90.8 5.2 %collective-permute-start.21 = (f32[16,224]{1,0:T(8,128)S(1)}, f32[16,224]{1,0:T(8,128)S(1)}, u32[]{:S(2)}, u32[]{:S(2)}) collective-permute-start(f32[16,224]{1,0:T(8,128)S(1)} %pad_maximum_fusion.1), channel_id=1, source_target_pairs={{0,4},{4,0},{8,12},{12,8},{16,20},{20,16},{24,28},{28,24},{1,5},{5... | collective-permute-start | bytes 43016 | tf_op jit(solution)/shard_map/ppermute | solution.py:339
  90.9 5.1 %collective-permute-start.22 = (f32[8,224]{1,0:T(8,128)S(1)}, f32[8,224]{1,0:T(8,128)S(1)}, u32[]{:S(2)}, u32[]{:S(2)}) collective-permute-start(f32[8,224]{1,0:T(8,128)S(1)} %add.12), channel_id=1, source_target_pairs={{0,6},{1,7},{2,4},{3,5},{4,2},{5,3},{6,0},{7,1},{8,14},{9,15},{10,... | collective-permute-start | bytes 21512 | tf_op jit(solution)/shard_map/ppermute | solution.py:346
  94.3 3.7 %collective-permute-start.20 = (f32[8,224]{1,0:T(8,128)S(1)}, f32[8,224]{1,0:T(8,128)S(1)}, u32[]{:S(2)}, u32[]{:S(2)}) collective-permute-start(f32[8,224]{1,0:T(8,128)S(1)} %add.12), channel_id=1, source_target_pairs={{0,2},{1,3},{2,0},{3,1},{4,6},{5,7},{6,4},{7,5},{8,10},{9,11},{10,... | collective-permute-start | bytes 21512 | tf_op jit(solution)/shard_map/ppermute | solution.py:342
  98.0 5.7 %collective-permute-start.25 = (f32[24,224]{1,0:T(8,128)S(1)}, f32[24,224]{1,0:T(8,128)S(1)}, u32[]{:S(2)}, u32[]{:S(2)}) collective-permute-start(f32[24,224]{1,0:T(8,128)S(1)} %pad_maximum_fusion.rest_10_), channel_id=1, source_target_pairs={{0,24},{4,28},{8,16},{12,20},{16,8},{20,12},{24,0},{28,4},{1,25},{... | collective-permute-start | bytes 64520 | tf_op jit(solution)/shard_map/ppermute | solution.py:339
  99.7 4.8 %collective-permute-start.24 = (f32[24,224]{1,0:T(8,128)S(1)}, f32[24,224]{1,0:T(8,128)S(1)}, u32[]{:S(2)}, u32[]{:S(2)}) collective-permute-start(f32[24,224]{1,0:T(8,128)S(1)} %pad_maximum_fusion.rest_10_), channel_id=1, source_target_pairs={{0,16},{4,20},{8,24},{12,28},{16,0},{20,4},{24,8},{28,12},{1,17},{... | collective-permute-start | bytes 64520 | tf_op jit(solution)/shard_map/ppermute | solution.py:339
  99.7 4.8 %collective-permute-start.23 = (f32[24,224]{1,0:T(8,128)S(1)}, f32[24,224]{1,0:T(8,128)S(1)}, u32[]{:S(2)}, u32[]{:S(2)}) collective-permute-start(f32[24,224]{1,0:T(8,128)S(1)} %pad_maximum_fusion.rest_10_), channel_id=1, source_target_pairs={{0,8},{4,12},{8,0},{12,4},{16,24},{20,28},{24,16},{28,20},{1,9},{5... | collective-permute-start | bytes 64520 | tf_op jit(solution)/shard_map/ppermute | solution.py:339

commit v6 on v5

--- a/solution.py
+++ b/solution.py
@@ -169,6 +169,7 @@
     quarters = sems.shape[1]
     units, width = weight.shape
     wide = width // quarters
+    copies = fetch(pieces, refs, held, sems, slots)
     packed_copies, rows_copies = [], []
     for i in range(n):
         packed_copies.append(pltpu.make_async_copy(hidden[i], packed.at[i], more_sems.at[quarters + i]))
@@ -179,7 +180,6 @@
             pltpu.make_async_copy(weight.at[:, columns], rows_held.at[:, pl.ds(e * wide, wide)], more_sems.at[e])
         )
         rows_copies[e].start()
-    copies = fetch(pieces, refs, held, sems, slots)
     for i in range(n):
         packed_copies[i].wait()
         head, tail = unpack_hidden(packed[i], units, live_rows)

time: 117 us -> 117 us (level)
  no operation moved by 1% of the time
where the time goes in v6:
time: 117 us
  waiting for transfers between devices  40.9 us (35%)
  starting transfers between devices  39.5 us (34%)
  Pallas kernels  25.4 us (22%)
  local copies, waits for them, and re-layouts  9.96 us (9%)
    ppermute x16, waiting for transfers between devices, over_dp(): return lax.ppermute(x, 'dp', [(s, s ^ m) for s in range(shards)])  32.8 us
    ppermute x16, starting transfers between devices, over_dp(): return lax.ppermute(x, 'dp', [(s, s ^ m) for s in range(shards)])  32.7 us
    pallas_call x1, Pallas kernels, cube_body(): pl.pallas_call(functools.partial(grad_kernel, places, len(refs), groups,...  12 us
    pallas_call x2, Pallas kernels, shift_sums(): pl.pallas_call(functools.partial(shift_kernel, places, len(refs), slots,...  10.5 us
    unnamed x40, local copies, waits for them, and re-layouts  9.88 us
    ppermute x9, waiting for transfers between devices, over_mp(): return lax.ppermute(x, 'mp', [(s, s ^ m) for s in range(quarters)])  6.44 us
    ppermute x1, starting transfers between devices, over_both(): return lax.ppermute(x, ('dp', 'mp'), pairs)  3.46 us
    ppermute x9, starting transfers between devices, over_mp(): return lax.ppermute(x, 'mp', [(s, s ^ m) for s in range(quarters)])  3.32 us
  transfers between devices with their start and end apart: 26, of which 13 were waited for; matrix products, arithmetic and copies ran while one was open for 0% of the time, Pallas kernels for 7%

profile of v6, /device:TPU:0, one launch (start us, length us, event | category | flops | bytes accessed | tf_op | source)
XLA Modules:
  0.0 116.7 jit_solution(3337442971302469037)
XLA Ops:
  0.6 0.0 copy-start.1
  0.6 1.3 %copy-done.1 = bf16[256,2560]{1,0:T(8,128)(2,1)S(1)} copy-done((bf16[256,2560]{1,0:T(8,128)(2,1)S(1)}, bf16[256,2560]{1,0:T(8,128)(2,1)}, u32[]{:S(2)}) %copy-start.1) | copy-done | bytes 1310744
  2.0 0.7 copy-done.5
  2.6 0.9 pack_first.1
  3.5 3.0 %collective-permute-start.4 = (bf16[448,640]{1,0:T(8,128)(2,1)S(1)}, bf16[448,640]{1,0:T(8,128)(2,1)S(1)}, u32[]{:S(2)}, u32[]{:S(2)}) collective-permute-start(bf16[448,640]{1,0:T(8,128)(2,1)S(1)} %get-tuple-element.39), channel_id=1, source_target_pairs={{0,4},{4,0},{8,12},{12,8},{16,20},{20,16},{24,28},{28,24},{1,5},{5... | collective-permute-start | bytes 1720328 | tf_op jit(solution)/shard_map/ppermute | solution.py:339
  6.5 2.6 %collective-permute-start.3 = (bf16[224,640]{1,0:T(8,128)(2,1)S(1)}, bf16[224,640]{1,0:T(8,128)(2,1)S(1)}, u32[]{:S(2)}, u32[]{:S(2)}) collective-permute-start(bf16[224,640]{1,0:T(8,128)(2,1)S(1)} %get-tuple-element.38), channel_id=1, source_target_pairs={{0,16},{4,20},{8,24},{12,28},{16,0},{20,4},{24,8},{28,12},{1,17},{... | collective-permute-start | bytes 860168 | tf_op jit(solution)/shard_map/ppermute | solution.py:339
  9.1 1.3 %collective-permute-start.2 = (bf16[224,640]{1,0:T(8,128)(2,1)S(1)}, bf16[224,640]{1,0:T(8,128)(2,1)S(1)}, u32[]{:S(2)}, u32[]{:S(2)}) collective-permute-start(bf16[224,640]{1,0:T(8,128)(2,1)S(1)} %get-tuple-element.38), channel_id=1, source_target_pairs={{0,24},{4,28},{8,16},{12,20},{16,8},{20,12},{24,0},{28,4},{1,25},{... | collective-permute-start | bytes 860168 | tf_op jit(solution)/shard_map/ppermute | solution.py:339
  10.5 0.2 collective-permute-start.1
  10.7 1.3 %copy-done.2 = bf16[256,2560]{1,0:T(8,128)(2,1)S(1)} copy-done((bf16[256,2560]{1,0:T(8,128)(2,1)S(1)}, bf16[256,2560]{1,0:T(8,128)(2,1)}, u32[]{:S(2)}) %copy-start.2) | copy-done | bytes 1310744
  12.0 0.7 copy-done.6
  12.7 1.5 %copy-done.8 = bf16[256,3584]{1,0:T(8,128)(2,1)S(1)} copy-done((bf16[256,3584]{1,0:T(8,128)(2,1)S(1)}, bf16[256,3584]{1,0:T(8,128)(2,1)}, u32[]{:S(2)}) %copy-start.8) | copy-done | bytes 1835032
  14.2 0.7 copy-done.14
  14.9 0.7 copy-done.15
  15.5 0.7 copy-done.16
  16.2 0.7 copy-done.17
  16.8 2.0 %pack_rest.1 = (f32[8,224]{1,0:T(8,128)S(1)}, bf16[4,224,640]{2,1,0:T(8,128)(2,1)S(1)}, bf16[784,128]{1,0:T(8,128)(2,1)S(1)}, bf16[784,128]{1,0:T(8,128)(2,1)S(1...) custom-call(s32[1,32]{1,0:T(1,128)S(1)} %copy-done.6, ...), custom_call_target="tpu_custom_call" | custom-call | flops 2000000000 | bytes 8000000 | tf_op jit(solution)/shard_map/pack_rest/pallas_call | solution.py:365
  18.8 0.5 collective-permute-start
  19.4 5.4 %collective-permute-done.rest_1_ = bf16[784,128]{1,0:T(8,128)(2,1)S(1)} collective-permute-done((bf16[784,128]{1,0:T(8,128)(2,1)S(1)}, bf16[784,128]{1,0:T(8,128)(2,1)S(1)}, u32[]{:S(2)}, u32[]{:S(2)}) %collective-permute-start) | collective-permute-done | bytes 200736 | tf_op jit(solution)/shard_map/ppermute | solution.py:339
  24.7 4.5 %collective-permute-done.3 = bf16[224,640]{1,0:T(8,128)(2,1)S(1)} collective-permute-done((bf16[224,640]{1,0:T(8,128)(2,1)S(1)}, bf16[224,640]{1,0:T(8,128)(2,1)S(1)}, u32[]{:S(2)}, u32[]{:S(2)}) %collective-permute-start.3) | collective-permute-done | bytes 286752 | tf_op jit(solution)/shard_map/ppermute | solution.py:339
  29.2 0.0 collective-permute-done.2
  29.2 0.2 collective-permute-done.1
  29.4 0.0 collective-permute-done.4.rest_6_.rest_3_
  29.4 0.0 collective-permute-start.9
  29.5 0.5 collective-permute-start.6
  30.0 1.5 %collective-permute-start.5 = (bf16[672,640]{1,0:T(8,128)(2,1)S(1)}, bf16[672,640]{1,0:T(8,128)(2,1)S(1)}, u32[]{:S(2)}, u32[]{:S(2)}) collective-permute-start(bf16[672,640]{1,0:T(8,128)(2,1)S(1)} %constant_dynamic-update-slice_fusion.rest_8_.rest_5_), channel_id=1, source_target_pairs={{0,2},{1,3},{2,0},{3,1},{4,6},{5,7},{6,4},{7,5},{8,10},{9,11},{10,... | collective-permute-start | bytes 2580488 | tf_op jit(solution)/shard_map/ppermute | solution.py:342
  31.6 0.0 collective-permute-done.9.rest_7_.rest_4_
  31.6 0.0 collective-permute-start.10
  31.6 7.5 %collective-permute-start.7 = (bf16[784,128]{1,0:T(8,128)(2,1)S(1)}, bf16[784,128]{1,0:T(8,128)(2,1)S(1)}, u32[]{:S(2)}, u32[]{:S(2)}) collective-permute-start(bf16[784,128]{1,0:T(8,128)(2,1)S(1)} %get-tuple-element.43), channel_id=1, source_target_pairs={{0,16},{4,20},{8,24},{12,28},{16,0},{20,4},{24,8},{28,12},{1,17},{... | collective-permute-start | bytes 602120 | tf_op jit(solution)/shard_map/ppermute | solution.py:339
  39.1 0.4 collective-permute-start.8
  39.5 14.0 %collective-permute-done.7.rest_4_ = bf16[784,128]{1,0:T(8,128)(2,1)S(1)} collective-permute-done((bf16[784,128]{1,0:T(8,128)(2,1)S(1)}, bf16[784,128]{1,0:T(8,128)(2,1)S(1)}, u32[]{:S(2)}, u32[]{:S(2)}) %collective-permute-start.7) | collective-permute-done | bytes 200736 | tf_op jit(solution)/shard_map/ppermute | solution.py:339
  53.5 0.0 collective-permute-done.8.rest_3_
  53.5 0.0 collective-permute-done.6.rest_4_
  53.5 0.0 collective-permute-done.5.rest_10_.rest_7_
  53.6 0.1 collective-permute-start.13
  53.6 1.3 %collective-permute-start.17 = (bf16[672,640]{1,0:T(8,128)(2,1)S(1)}, bf16[672,640]{1,0:T(8,128)(2,1)S(1)}, u32[]{:S(2)}, u32[]{:S(2)}) collective-permute-start(bf16[672,640]{1,0:T(8,128)(2,1)S(1)} %collective-permute-done.6.rest_4_), channel_id=1, source_target_pairs={{0,2},{1,3},{2,0},{3,1},{4,6},{5,7},{6,4},{7,5},{8,10},{9,11},{10,... | collective-permute-start | bytes 2580488 | tf_op jit(solution)/shard_map/ppermute | solution.py:342
  55.0 1.0 collective-permute-done.13.rest_11_.rest_8_
  56.0 0.1 collective-permute-start.16
  56.1 2.2 %collective-permute-start.12 = (bf16[784,128]{1,0:T(8,128)(2,1)S(1)}, bf16[784,128]{1,0:T(8,128)(2,1)S(1)}, u32[]{:S(2)}, u32[]{:S(2)}) collective-permute-start(bf16[784,128]{1,0:T(8,128)(2,1)S(1)} %get-tuple-element.51), channel_id=1, source_target_pairs={{0,28},{4,24},{8,20},{12,16},{16,12},{20,8},{24,4},{28,0},{1,29},{... | collective-permute-start | bytes 602120 | tf_op jit(solution)/shard_map/ppermute | solution.py:339
  58.4 4.5 %collective-permute-start.11 = (bf16[784,128]{1,0:T(8,128)(2,1)S(1)}, bf16[784,128]{1,0:T(8,128)(2,1)S(1)}, u32[]{:S(2)}, u32[]{:S(2)}) collective-permute-start(bf16[784,128]{1,0:T(8,128)(2,1)S(1)} %get-tuple-element.48), channel_id=1, source_target_pairs={{0,8},{4,12},{8,0},{12,4},{16,24},{20,28},{24,16},{28,20},{1,9},{5... | collective-permute-start | bytes 602120 | tf_op jit(solution)/shard_map/ppermute | solution.py:339
  62.9 3.8 %collective-permute-done.12.rest_1_ = bf16[784,128]{1,0:T(8,128)(2,1)S(1)} collective-permute-done((bf16[784,128]{1,0:T(8,128)(2,1)S(1)}, bf16[784,128]{1,0:T(8,128)(2,1)S(1)}, u32[]{:S(2)}, u32[]{:S(2)}) %collective-permute-start.12) | collective-permute-done | bytes 200736 | tf_op jit(solution)/shard_map/ppermute | solution.py:339
  66.7 5.3 %collective-permute-start.15 = (bf16[784,128]{1,0:T(8,128)(2,1)S(1)}, bf16[784,128]{1,0:T(8,128)(2,1)S(1)}, u32[]{:S(2)}, u32[]{:S(2)}) collective-permute-start(bf16[784,128]{1,0:T(8,128)(2,1)S(1)} %get-tuple-element.58), channel_id=1, source_target_pairs={{0,20},{4,16},{8,28},{12,24},{16,4},{20,0},{24,12},{28,8},{1,21},{... | collective-permute-start | bytes 602120 | tf_op jit(solution)/shard_map/ppermute | solution.py:339
  71.9 6.3 %shift_sums.2 = (f32[8,224]{1,0:T(8,128)S(1)}, bf16[448,1120]{1,0:T(8,128)(2,1)S(1)}) custom-call(bf16[448,2560]{1,0:T(8,128)(2,1)S(1)} %copy-done, bf16[784,128]{1,0:T(8,128)(2,1)S(1)} %get-tuple-element.35.rest_0_, bf16[784,128]{1,0:T(8,128)(2,1)S(1)} %collective-permute-done.rest_1_, bf16[784,128]{1,0:T(8,128)(2,1)S(1)} %collective-permute-done.11.rest_2_, ...), custom_call_target="tpu_custom_call" | custom-call | flops 2569011200 | bytes 5734400 | tf_op jit(solution)/shard_map/shift_sums/pallas_call | solution.py:399
  78.3 0.0 collective-permute-done.14.rest_0_
  78.4 2.9 %collective-permute-done.15.rest_2_ = bf16[784,128]{1,0:T(8,128)(2,1)S(1)} collective-permute-done((bf16[784,128]{1,0:T(8,128)(2,1)S(1)}, bf16[784,128]{1,0:T(8,128)(2,1)S(1)}, u32[]{:S(2)}, u32[]{:S(2)}) %collective-permute-start.15) | collective-permute-done | bytes 200736 | tf_op jit(solution)/shard_map/ppermute | solution.py:339
  81.3 0.0 collective-permute-done.17.rest_6_
  81.3 0.0 collective-permute-done.16.rest_5_
  81.3 0.1 collective-permute-start.18
  81.4 2.4 %collective-permute-done.18.rest_7_ = bf16[672,640]{1,0:T(8,128)(2,1)S(1)} collective-permute-done((bf16[672,640]{1,0:T(8,128)(2,1)S(1)}, bf16[672,640]{1,0:T(8,128)(2,1)S(1)}, u32[]{:S(2)}, u32[]{:S(2)}) %collective-permute-start.18) | collective-permute-done | bytes 860192 | tf_op jit(solution)/shard_map/ppermute | solution.py:342
  83.8 4.1 %shift_sums.3 = (f32[8,224]{1,0:T(8,128)S(1)}, bf16[448,672]{1,0:T(8,128)(2,1)S(1)}, bf16[672,2560]{1,0:T(8,128)(2,1)S(1)}) custom-call(bf16[448,2560]{1,0:T(8,128)(2,1)S(1)} %copy-done, bf16[784,128]{1,0:T(8,128)(2,1)S(1)} %collective-permute-done.14.rest_0_, bf16[784,128]{1,0:T(8,128)(2,1)S(1)} %collective-permute-done.12.rest_1_, ...), custom_call_target="tpu_custom_call" | custom-call | flops 1541406720 | bytes 3440640 | tf_op jit(solution)/shard_map/shift_sums/pallas_call | solution.py:399
  87.9 1.7 %copy-done.7 = bf16[672,2560]{1,0:T(8,128)(2,1)} copy-done((bf16[672,2560]{1,0:T(8,128)(2,1)}, bf16[672,2560]{1,0:T(8,128)(2,1)S(1)}, u32[]{:S(2)}) %copy-start.7) | copy-done | bytes 3440664
  89.6 0.1 collective-permute-start.19
  89.7 1.0 collective-permute-done.19
  90.8 0.1 collective-permute-start.21
  90.9 3.5 %collective-permute-start.22 = (f32[8,224]{1,0:T(8,128)S(1)}, f32[8,224]{1,0:T(8,128)S(1)}, u32[]{:S(2)}, u32[]{:S(2)}) collective-permute-start(f32[8,224]{1,0:T(8,128)S(1)} %add.12), channel_id=1, source_target_pairs={{0,6},{1,7},{2,4},{3,5},{4,2},{5,3},{6,0},{7,1},{8,14},{9,15},{10,... | collective-permute-start | bytes 21512 | tf_op jit(solution)/shard_map/ppermute | solution.py:346
  94.3 0.0 collective-permute-start.20
  94.3 1.6 %collective-permute-done.22 = f32[8,224]{1,0:T(8,128)S(1)} collective-permute-done((f32[8,224]{1,0:T(8,128)S(1)}, f32[8,224]{1,0:T(8,128)S(1)}, u32[]{:S(2)}, u32[]{:S(2)}) %collective-permute-start.22) | collective-permute-done | bytes 7200 | tf_op jit(solution)/shard_map/ppermute | solution.py:346
  96.0 2.0 %collective-permute-done.20 = f32[8,224]{1,0:T(8,128)S(1)} collective-permute-done((f32[8,224]{1,0:T(8,128)S(1)}, f32[8,224]{1,0:T(8,128)S(1)}, u32[]{:S(2)}, u32[]{:S(2)}) %collective-permute-start.20) | collective-permute-done | bytes 7200 | tf_op jit(solution)/shard_map/ppermute | solution.py:342
  98.0 1.7 %collective-permute-start.25 = (f32[24,224]{1,0:T(8,128)S(1)}, f32[24,224]{1,0:T(8,128)S(1)}, u32[]{:S(2)}, u32[]{:S(2)}) collective-permute-start(f32[24,224]{1,0:T(8,128)S(1)} %pad_maximum_fusion.rest_10_), channel_id=1, source_target_pairs={{0,24},{4,28},{8,16},{12,20},{16,8},{20,12},{24,0},{28,4},{1,25},{... | collective-permute-start | bytes 64520 | tf_op jit(solution)/shard_map/ppermute | solution.py:339
  99.7 0.0 collective-permute-start.24
  99.7 2.7 %collective-permute-start.23 = (f32[24,224]{1,0:T(8,128)S(1)}, f32[24,224]{1,0:T(8,128)S(1)}, u32[]{:S(2)}, u32[]{:S(2)}) collective-permute-start(f32[24,224]{1,0:T(8,128)S(1)} %pad_maximum_fusion.rest_10_), channel_id=1, source_target_pairs={{0,8},{4,12},{8,0},{12,4},{16,24},{20,28},{24,16},{28,20},{1,9},{5... | collective-permute-start | bytes 64520 | tf_op jit(solution)/shard_map/ppermute | solution.py:339
  102.4 1.2 %collective-permute-done.25.rest_13_ = f32[24,224]{1,0:T(8,128)S(1)} collective-permute-done((f32[24,224]{1,0:T(8,128)S(1)}, f32[24,224]{1,0:T(8,128)S(1)}, u32[]{:S(2)}, u32[]{:S(2)}) %collective-permute-start.25) | collective-permute-done | bytes 21536 | tf_op jit(solution)/shard_map/ppermute | solution.py:339
  103.7 0.8 collective-permute-done.24.rest_12_
  104.5 0.0 collective-permute-done.23.rest_11_
  104.5 12.0 %weight_grad.1 = (f32[8,64]{1,0:T(8,128)}, f32[448,2560]{1,0:T(8,128)}) custom-call(bf16[448,1120]{1,0:T(8,128)(2,1)} %copy-done.18, bf16[448,672]{1,0:T(8,128)(2,1)S(1)} %get-tuple-element.63.rest_1_, bf16[4,224,640]{2,1,0:T(8,128)(2,1)} %copy-done.3, bf16[448,640]{1,0:T(8,128)(2,1)S(1)} %collective-permute-done.4.rest_6_.rest_3_, ...), custom_call_target="tpu_custom_call" | custom-call | flops 4110417920 | bytes 13762560 | tf_op jit(solution)/shard_map/weight_grad/pallas_call | solution.py:454
  (41 shorter events, 0.2 us)
Async XLA Ops:
  0.6 1.3 %copy-start.1 = (bf16[256,2560]{1,0:T(8,128)(2,1)S(1)}, bf16[256,2560]{1,0:T(8,128)(2,1)}, u32[]{:S(2)}) copy-start(bf16[256,2560]{1,0:T(8,128)(2,1)} %read.3) | copy-start | bytes 3932164
  1.9 0.7 copy-start.5
  3.5 25.9 %collective-permute-start.4 = (bf16[448,640]{1,0:T(8,128)(2,1)S(1)}, bf16[448,640]{1,0:T(8,128)(2,1)S(1)}, u32[]{:S(2)}, u32[]{:S(2)}) collective-permute-start(bf16[448,640]{1,0:T(8,128)(2,1)S(1)} %get-tuple-element.39), channel_id=1, source_target_pairs={{0,4},{4,0},{8,12},{12,8},{16,20},{20,16},{24,28},{28,24},{1,5},{5... | collective-permute-start | bytes 1720328 | tf_op jit(solution)/shard_map/ppermute | solution.py:339
  6.5 22.7 %collective-permute-start.3 = (bf16[224,640]{1,0:T(8,128)(2,1)S(1)}, bf16[224,640]{1,0:T(8,128)(2,1)S(1)}, u32[]{:S(2)}, u32[]{:S(2)}) collective-permute-start(bf16[224,640]{1,0:T(8,128)(2,1)S(1)} %get-tuple-element.38), channel_id=1, source_target_pairs={{0,16},{4,20},{8,24},{12,28},{16,0},{20,4},{24,8},{28,12},{1,17},{... | collective-permute-start | bytes 860168 | tf_op jit(solution)/shard_map/ppermute | solution.py:339
  9.1 20.1 %collective-permute-start.2 = (bf16[224,640]{1,0:T(8,128)(2,1)S(1)}, bf16[224,640]{1,0:T(8,128)(2,1)S(1)}, u32[]{:S(2)}, u32[]{:S(2)}) collective-permute-start(bf16[224,640]{1,0:T(8,128)(2,1)S(1)} %get-tuple-element.38), channel_id=1, source_target_pairs={{0,24},{4,28},{8,16},{12,20},{16,8},{20,12},{24,0},{28,4},{1,25},{... | collective-permute-start | bytes 860168 | tf_op jit(solution)/shard_map/ppermute | solution.py:339
  10.5 18.9 %collective-permute-start.1 = (bf16[224,640]{1,0:T(8,128)(2,1)S(1)}, bf16[224,640]{1,0:T(8,128)(2,1)S(1)}, u32[]{:S(2)}, u32[]{:S(2)}) collective-permute-start(bf16[224,640]{1,0:T(8,128)(2,1)S(1)} %get-tuple-element.38), channel_id=1, source_target_pairs={{0,8},{4,12},{8,0},{12,4},{16,24},{20,28},{24,16},{28,20},{1,9},{5... | collective-permute-start | bytes 860168 | tf_op jit(solution)/shard_map/ppermute | solution.py:339
  10.7 1.3 %copy-start.2 = (bf16[256,2560]{1,0:T(8,128)(2,1)S(1)}, bf16[256,2560]{1,0:T(8,128)(2,1)}, u32[]{:S(2)}) copy-start(bf16[256,2560]{1,0:T(8,128)(2,1)} %read.3) | copy-start | bytes 3932164
  12.0 0.7 copy-start.6
  12.7 1.5 %copy-start.8 = (bf16[256,3584]{1,0:T(8,128)(2,1)S(1)}, bf16[256,3584]{1,0:T(8,128)(2,1)}, u32[]{:S(2)}) copy-start(bf16[256,3584]{1,0:T(8,128)(2,1)} %hidden.1) | copy-start | bytes 5505028
  14.2 0.7 copy-start.14
  14.9 0.7 copy-start.15
  15.5 0.7 copy-start.16
  16.2 0.7 copy-start.17
  16.8 55.1 %copy-start = (bf16[448,2560]{1,0:T(8,128)(2,1)S(1)}, bf16[448,2560]{1,0:T(8,128)(2,1)}, u32[]{:S(2)}) copy-start(bf16[448,2560]{1,0:T(8,128)(2,1)} %weight.3) | copy-start | bytes 6881284
  18.8 65.0 %copy-start.3 = (bf16[4,224,640]{2,1,0:T(8,128)(2,1)}, bf16[4,224,640]{2,1,0:T(8,128)(2,1)S(1)}, u32[]{:S(2)}) copy-start(bf16[4,224,640]{2,1,0:T(8,128)(2,1)S(1)} %get-tuple-element.52.rest_5_.rest_3_.rest_2_) | copy-start | bytes 3440644
  18.8 5.9 %collective-permute-start = (bf16[784,128]{1,0:T(8,128)(2,1)S(1)}, bf16[784,128]{1,0:T(8,128)(2,1)S(1)}, u32[]{:S(2)}, u32[]{:S(2)}) collective-permute-start(bf16[784,128]{1,0:T(8,128)(2,1)S(1)} %get-tuple-element.36), channel_id=1, source_target_pairs={{0,4},{4,0},{8,12},{12,8},{16,20},{20,16},{24,28},{28,24},{1,5},{5... | collective-permute-start | bytes 602120 | tf_op jit(solution)/shard_map/ppermute | solution.py:339
  29.4 2.2 %collective-permute-start.9 = (bf16[448,640]{1,0:T(8,128)(2,1)S(1)}, bf16[448,640]{1,0:T(8,128)(2,1)S(1)}, u32[]{:S(2)}, u32[]{:S(2)}) collective-permute-start(bf16[448,640]{1,0:T(8,128)(2,1)S(1)} %collective-permute-done.4.rest_6_.rest_3_), channel_id=1, source_target_pairs={{0,1},{1,0},{2,3},{3,2},{4,5},{5,4},{6,7},{7,6},{8,9},{9,8},{10,11... | collective-permute-start | bytes 1720328 | tf_op jit(solution)/shard_map/ppermute | solution.py:342
  29.5 48.8 %copy-start.4 = (bf16[672,640]{1,0:T(8,128)(2,1)}, bf16[672,640]{1,0:T(8,128)(2,1)S(1)}, u32[]{:S(2)}) copy-start(bf16[672,640]{1,0:T(8,128)(2,1)S(1)} %constant_dynamic-update-slice_fusion.rest_8_.rest_5_) | copy-start | bytes 2580484
  29.5 24.0 %collective-permute-start.6 = (bf16[672,640]{1,0:T(8,128)(2,1)S(1)}, bf16[672,640]{1,0:T(8,128)(2,1)S(1)}, u32[]{:S(2)}, u32[]{:S(2)}) collective-permute-start(bf16[672,640]{1,0:T(8,128)(2,1)S(1)} %constant_dynamic-update-slice_fusion.rest_8_.rest_5_), channel_id=1, source_target_pairs={{0,4},{4,0},{8,12},{12,8},{16,20},{20,16},{24,28},{28,24},{1,5},{5... | collective-permute-start | bytes 2580488 | tf_op jit(solution)/shard_map/ppermute | solution.py:339
  30.0 23.5 %collective-permute-start.5 = (bf16[672,640]{1,0:T(8,128)(2,1)S(1)}, bf16[672,640]{1,0:T(8,128)(2,1)S(1)}, u32[]{:S(2)}, u32[]{:S(2)}) collective-permute-start(bf16[672,640]{1,0:T(8,128)(2,1)S(1)} %constant_dynamic-update-slice_fusion.rest_8_.rest_5_), channel_id=1, source_target_pairs={{0,2},{1,3},{2,0},{3,1},{4,6},{5,7},{6,4},{7,5},{8,10},{9,11},{10,... | collective-permute-start | bytes 2580488 | tf_op jit(solution)/shard_map/ppermute | solution.py:342
  31.6 46.7 %copy-start.12 = (bf16[448,640]{1,0:T(8,128)(2,1)}, bf16[448,640]{1,0:T(8,128)(2,1)S(1)}, u32[]{:S(2)}) copy-start(bf16[448,640]{1,0:T(8,128)(2,1)S(1)} %collective-permute-done.9.rest_7_.rest_4_) | copy-start | bytes 1720324
  31.6 22.0 %collective-permute-start.10 = (bf16[672,640]{1,0:T(8,128)(2,1)S(1)}, bf16[672,640]{1,0:T(8,128)(2,1)S(1)}, u32[]{:S(2)}, u32[]{:S(2)}) collective-permute-start(bf16[672,640]{1,0:T(8,128)(2,1)S(1)} %constant_dynamic-update-slice_fusion.rest_8_.rest_5_), channel_id=1, source_target_pairs={{0,1},{1,0},{2,3},{3,2},{4,5},{5,4},{6,7},{7,6},{8,9},{9,8},{10,11... | collective-permute-start | bytes 2580488 | tf_op jit(solution)/shard_map/ppermute | solution.py:342
  31.6 21.9 %collective-permute-start.7 = (bf16[784,128]{1,0:T(8,128)(2,1)S(1)}, bf16[784,128]{1,0:T(8,128)(2,1)S(1)}, u32[]{:S(2)}, u32[]{:S(2)}) collective-permute-start(bf16[784,128]{1,0:T(8,128)(2,1)S(1)} %get-tuple-element.43), channel_id=1, source_target_pairs={{0,16},{4,20},{8,24},{12,28},{16,0},{20,4},{24,8},{28,12},{1,17},{... | collective-permute-start | bytes 602120 | tf_op jit(solution)/shard_map/ppermute | solution.py:339
  39.1 14.4 %collective-permute-start.8 = (bf16[784,128]{1,0:T(8,128)(2,1)S(1)}, bf16[784,128]{1,0:T(8,128)(2,1)S(1)}, u32[]{:S(2)}, u32[]{:S(2)}) collective-permute-start(bf16[784,128]{1,0:T(8,128)(2,1)S(1)} %get-tuple-element.45), channel_id=1, source_target_pairs={{0,24},{4,28},{8,16},{12,20},{16,8},{20,12},{24,0},{28,4},{1,25},{... | collective-permute-start | bytes 602120 | tf_op jit(solution)/shard_map/ppermute | solution.py:339
  53.5 24.8 %copy-start.9 = (bf16[672,640]{1,0:T(8,128)(2,1)}, bf16[672,640]{1,0:T(8,128)(2,1)S(1)}, u32[]{:S(2)}) copy-start(bf16[672,640]{1,0:T(8,128)(2,1)S(1)} %collective-permute-done.5.rest_10_.rest_7_) | copy-start | bytes 2580484
  53.5 24.8 %copy-start.10 = (bf16[672,640]{1,0:T(8,128)(2,1)}, bf16[672,640]{1,0:T(8,128)(2,1)S(1)}, u32[]{:S(2)}) copy-start(bf16[672,640]{1,0:T(8,128)(2,1)S(1)} %collective-permute-done.10.rest_9_.rest_6_) | copy-start | bytes 2580484
  53.6 2.5 %collective-permute-start.13 = (bf16[672,640]{1,0:T(8,128)(2,1)S(1)}, bf16[672,640]{1,0:T(8,128)(2,1)S(1)}, u32[]{:S(2)}, u32[]{:S(2)}) collective-permute-start(bf16[672,640]{1,0:T(8,128)(2,1)S(1)} %collective-permute-done.5.rest_10_.rest_7_), channel_id=1, source_target_pairs={{0,1},{1,0},{2,3},{3,2},{4,5},{5,4},{6,7},{7,6},{8,9},{9,8},{10,11... | collective-permute-start | bytes 2580488 | tf_op jit(solution)/shard_map/ppermute | solution.py:342
  53.6 27.7 %collective-permute-start.17 = (bf16[672,640]{1,0:T(8,128)(2,1)S(1)}, bf16[672,640]{1,0:T(8,128)(2,1)S(1)}, u32[]{:S(2)}, u32[]{:S(2)}) collective-permute-start(bf16[672,640]{1,0:T(8,128)(2,1)S(1)} %collective-permute-done.6.rest_4_), channel_id=1, source_target_pairs={{0,2},{1,3},{2,0},{3,1},{4,6},{5,7},{6,4},{7,5},{8,10},{9,11},{10,... | collective-permute-start | bytes 2580488 | tf_op jit(solution)/shard_map/ppermute | solution.py:342
  56.0 22.3 %copy-start.11 = (bf16[672,640]{1,0:T(8,128)(2,1)}, bf16[672,640]{1,0:T(8,128)(2,1)S(1)}, u32[]{:S(2)}) copy-start(bf16[672,640]{1,0:T(8,128)(2,1)S(1)} %collective-permute-done.13.rest_11_.rest_8_) | copy-start | bytes 2580484
  56.0 25.3 %collective-permute-start.16 = (bf16[672,640]{1,0:T(8,128)(2,1)S(1)}, bf16[672,640]{1,0:T(8,128)(2,1)S(1)}, u32[]{:S(2)}, u32[]{:S(2)}) collective-permute-start(bf16[672,640]{1,0:T(8,128)(2,1)S(1)} %collective-permute-done.6.rest_4_), channel_id=1, source_target_pairs={{0,1},{1,0},{2,3},{3,2},{4,5},{5,4},{6,7},{7,6},{8,9},{9,8},{10,11... | collective-permute-start | bytes 2580488 | tf_op jit(solution)/shard_map/ppermute | solution.py:342
  56.1 10.5 %collective-permute-start.12 = (bf16[784,128]{1,0:T(8,128)(2,1)S(1)}, bf16[784,128]{1,0:T(8,128)(2,1)S(1)}, u32[]{:S(2)}, u32[]{:S(2)}) collective-permute-start(bf16[784,128]{1,0:T(8,128)(2,1)S(1)} %get-tuple-element.51), channel_id=1, source_target_pairs={{0,28},{4,24},{8,20},{12,16},{16,12},{20,8},{24,4},{28,0},{1,29},{... | collective-permute-start | bytes 602120 | tf_op jit(solution)/shard_map/ppermute | solution.py:339
  58.4 13.5 %collective-permute-start.11 = (bf16[784,128]{1,0:T(8,128)(2,1)S(1)}, bf16[784,128]{1,0:T(8,128)(2,1)S(1)}, u32[]{:S(2)}, u32[]{:S(2)}) collective-permute-start(bf16[784,128]{1,0:T(8,128)(2,1)S(1)} %get-tuple-element.48), channel_id=1, source_target_pairs={{0,8},{4,12},{8,0},{12,4},{16,24},{20,28},{24,16},{28,20},{1,9},{5... | collective-permute-start | bytes 602120 | tf_op jit(solution)/shard_map/ppermute | solution.py:339
  62.9 15.5 %collective-permute-start.14 = (bf16[784,128]{1,0:T(8,128)(2,1)S(1)}, bf16[784,128]{1,0:T(8,128)(2,1)S(1)}, u32[]{:S(2)}, u32[]{:S(2)}) collective-permute-start(bf16[784,128]{1,0:T(8,128)(2,1)S(1)} %get-tuple-element.56), channel_id=1, source_target_pairs={{0,12},{4,8},{8,4},{12,0},{16,28},{20,24},{24,20},{28,16},{1,13},{... | collective-permute-start | bytes 602120 | tf_op jit(solution)/shard_map/ppermute | solution.py:339
  66.7 14.6 %collective-permute-start.15 = (bf16[784,128]{1,0:T(8,128)(2,1)S(1)}, bf16[784,128]{1,0:T(8,128)(2,1)S(1)}, u32[]{:S(2)}, u32[]{:S(2)}) collective-permute-start(bf16[784,128]{1,0:T(8,128)(2,1)S(1)} %get-tuple-element.58), channel_id=1, source_target_pairs={{0,20},{4,16},{8,28},{12,24},{16,4},{20,0},{24,12},{28,8},{1,21},{... | collective-permute-start | bytes 602120 | tf_op jit(solution)/shard_map/ppermute | solution.py:339
  78.3 9.6 %copy-start.18 = (bf16[448,1120]{1,0:T(8,128)(2,1)}, bf16[448,1120]{1,0:T(8,128)(2,1)S(1)}, u32[]{:S(2)}) copy-start(bf16[448,1120]{1,0:T(8,128)(2,1)S(1)} %get-tuple-element.54.rest_0_) | copy-start | bytes 3010564
  81.3 23.2 %copy-start.13 = (bf16[448,640]{1,0:T(8,128)(2,1)S(1)}, bf16[448,640]{1,0:T(8,128)(2,1)}, u32[]{:S(2)}) copy-start(bf16[448,640]{1,0:T(8,128)(2,1)} %copy-done.12) | copy-start | bytes 1720324
  81.3 2.5 %collective-permute-start.18 = (bf16[672,640]{1,0:T(8,128)(2,1)S(1)}, bf16[672,640]{1,0:T(8,128)(2,1)S(1)}, u32[]{:S(2)}, u32[]{:S(2)}) collective-permute-start(bf16[672,640]{1,0:T(8,128)(2,1)S(1)} %collective-permute-done.17.rest_6_), channel_id=1, source_target_pairs={{0,1},{1,0},{2,3},{3,2},{4,5},{5,4},{6,7},{7,6},{8,9},{9,8},{10,11... | collective-permute-start | bytes 2580488 | tf_op jit(solution)/shard_map/ppermute | solution.py:342
  87.9 1.7 %copy-start.7 = (bf16[672,2560]{1,0:T(8,128)(2,1)}, bf16[672,2560]{1,0:T(8,128)(2,1)S(1)}, u32[]{:S(2)}) copy-start(bf16[672,2560]{1,0:T(8,128)(2,1)S(1)} %get-tuple-element.64.rest_9_) | copy-start | bytes 10321924
  89.6 1.2 %collective-permute-start.19 = (f32[8,224]{1,0:T(8,128)S(1)}, f32[8,224]{1,0:T(8,128)S(1)}, u32[]{:S(2)}, u32[]{:S(2)}) collective-permute-start(f32[8,224]{1,0:T(8,128)S(1)} %get-tuple-element.65), channel_id=1, source_target_pairs={{0,1},{1,0},{2,3},{3,2},{4,5},{5,4},{6,7},{7,6},{8,9},{9,8},{10,11... | collective-permute-start | bytes 21512 | tf_op jit(solution)/shard_map/ppermute | solution.py:342
  90.8 5.2 %collective-permute-start.21 = (f32[16,224]{1,0:T(8,128)S(1)}, f32[16,224]{1,0:T(8,128)S(1)}, u32[]{:S(2)}, u32[]{:S(2)}) collective-permute-start(f32[16,224]{1,0:T(8,128)S(1)} %pad_maximum_fusion.1), channel_id=1, source_target_pairs={{0,4},{4,0},{8,12},{12,8},{16,20},{20,16},{24,28},{28,24},{1,5},{5... | collective-permute-start | bytes 43016 | tf_op jit(solution)/shard_map/ppermute | solution.py:339
  90.9 5.1 %collective-permute-start.22 = (f32[8,224]{1,0:T(8,128)S(1)}, f32[8,224]{1,0:T(8,128)S(1)}, u32[]{:S(2)}, u32[]{:S(2)}) collective-permute-start(f32[8,224]{1,0:T(8,128)S(1)} %add.12), channel_id=1, source_target_pairs={{0,6},{1,7},{2,4},{3,5},{4,2},{5,3},{6,0},{7,1},{8,14},{9,15},{10,... | collective-permute-start | bytes 21512 | tf_op jit(solution)/shard_map/ppermute | solution.py:346
  94.3 3.7 %collective-permute-start.20 = (f32[8,224]{1,0:T(8,128)S(1)}, f32[8,224]{1,0:T(8,128)S(1)}, u32[]{:S(2)}, u32[]{:S(2)}) collective-permute-start(f32[8,224]{1,0:T(8,128)S(1)} %add.12), channel_id=1, source_target_pairs={{0,2},{1,3},{2,0},{3,1},{4,6},{5,7},{6,4},{7,5},{8,10},{9,11},{10,... | collective-permute-start | bytes 21512 | tf_op jit(solution)/shard_map/ppermute | solution.py:342
  98.0 5.7 %collective-permute-start.25 = (f32[24,224]{1,0:T(8,128)S(1)}, f32[24,224]{1,0:T(8,128)S(1)}, u32[]{:S(2)}, u32[]{:S(2)}) collective-permute-start(f32[24,224]{1,0:T(8,128)S(1)} %pad_maximum_fusion.rest_10_), channel_id=1, source_target_pairs={{0,24},{4,28},{8,16},{12,20},{16,8},{20,12},{24,0},{28,4},{1,25},{... | collective-permute-start | bytes 64520 | tf_op jit(solution)/shard_map/ppermute | solution.py:339
  99.7 4.8 %collective-permute-start.24 = (f32[24,224]{1,0:T(8,128)S(1)}, f32[24,224]{1,0:T(8,128)S(1)}, u32[]{:S(2)}, u32[]{:S(2)}) collective-permute-start(f32[24,224]{1,0:T(8,128)S(1)} %pad_maximum_fusion.rest_10_), channel_id=1, source_target_pairs={{0,16},{4,20},{8,24},{12,28},{16,0},{20,4},{24,8},{28,12},{1,17},{... | collective-permute-start | bytes 64520 | tf_op jit(solution)/shard_map/ppermute | solution.py:339
  99.7 4.8 %collective-permute-start.23 = (f32[24,224]{1,0:T(8,128)S(1)}, f32[24,224]{1,0:T(8,128)S(1)}, u32[]{:S(2)}, u32[]{:S(2)}) collective-permute-start(f32[24,224]{1,0:T(8,128)S(1)} %pad_maximum_fusion.rest_10_), channel_id=1, source_target_pairs={{0,8},{4,12},{8,0},{12,4},{16,24},{20,28},{24,16},{28,20},{1,9},{5... | collective-permute-start | bytes 64520 | tf_op jit(solution)/shard_map/ppermute | solution.py:339
